TPU v7x, 32 devices: a whole 2x2x4 slice. The times are simulated.
32 devices in a mesh: groups: 2 (over y), rows: 4 (over x, core), cols: 4 (over z).
Axes of the slice: x: 2, y: 2, z: 4, core: 2. Of those that a mesh axis runs over, the one named last changes fastest.
Arguments:
- block_values: bfloat16 [192, 8, 128, 128], P(('groups', 'rows'), 'cols'), parts along dimension 0, may hold values from -3 to 3
- block_columns: int32 [192, 8], P(('groups', 'rows'), 'cols'), parts along dimension 0, may hold values from -1 to 95, as said below
- product_columns: int32 [192, 16], P(('groups', 'rows'), 'cols'), parts along dimension 0, may hold values from -1 to 95, as said below
Outputs:
- square: float32 [192, 16, 128, 128], P(('groups', 'rows'), 'cols'), parts along dimension 0
There are 2 independent parts, one for each index of `groups`. A program takes and returns all parts, laid end to end along the dimension named above; each array names one. Nothing has to cross between parts.
Inputs may be any that keep to these rules, and one draw needn't show every extreme that they name: `block_columns`: within a block row the stored columns are distinct and lie in i to i + 9 for block row i; slot 0 is the diagonal; a slot is -1 exactly where its column would pass the last block row. `product_columns`: within a block row the columns are distinct and lie in i to i + 2 * 10 - 2 for block row i; slot 0 is the diagonal; a slot is -1 exactly where its column would pass the last block row.
All inputs are finite; a program needn't handle non-finite values.
Results may differ from a plain program's by a relative error of at most 0.0003.
Values may be sent and summed in bfloat16 or wider, within the bound.
No kernel may reach another device: no remote copies, remote signals or barrier semaphores. Data moves between devices by JAX's collectives and lax.ppermute only.
A program may use at most 320 MiB of HBM per device.

v0:
```python
import jax
import jax.numpy as jnp
from jax import lax
from jax.sharding import PartitionSpec as P

W = 10


def from_behind(array, axis, by):
    size = lax.axis_size(axis)
    pairs = [(i, i + by) for i in range(size) if 0 <= i + by < size]
    return lax.ppermute(array, axis, pairs)


def make_band(values, columns, row_ids):
    offsets = columns - row_ids[:, None]
    reach = jnp.arange(W, dtype=jnp.int32)
    slot_ids = jnp.arange(values.shape[1], dtype=jnp.int32)
    picked = (offsets[:, None, :] == reach[None, :, None]) & (columns[:, None, :] >= 0)
    source = jnp.sum(jnp.where(picked, slot_ids[None, None, :], 0), axis=2)
    present = jnp.any(picked, axis=2)
    taken = jnp.take_along_axis(values, source[:, :, None, None], axis=1)
    band_tiles = jnp.where(present[:, :, None, None], taken, jnp.zeros((), values.dtype))
    diagonal = band_tiles[:, 0]
    diagonal = jnp.triu(diagonal) + jnp.swapaxes(jnp.triu(diagonal, 1), 1, 2)
    return band_tiles.at[:, 0].set(diagonal)


def extend_rows(tiles):
    count = tiles.shape[0]
    before = from_behind(tiles[count - (W - 1) :], "rows", 1)
    after = from_behind(tiles[: 2 * W - 2], "rows", -1)
    return jnp.concatenate([before, tiles, after], axis=0)


def block_product(band_tiles, wanted, first_row, row_count):
    lead_rows = W - 1
    ext_count = band_tiles.shape[0]
    global_rows = first_row + jnp.arange(row_count, dtype=jnp.int32)
    distance = jnp.where(wanted >= 0, wanted - global_rows[:, None], -4 * W)
    steps_k = jnp.arange(-(W - 1), W, dtype=jnp.int32)
    local_rows = jnp.arange(row_count, dtype=jnp.int32)
    holder = lead_rows + steps_k[:, None] + local_rows[None, :]
    left_raw = band_tiles[holder, jnp.abs(steps_k)[:, None]]
    left_stack = jnp.where(
        (steps_k < 0)[:, None, None, None], jnp.swapaxes(left_raw, 2, 3), left_raw
    )
    outputs = []
    for slot_q in range(wanted.shape[1]):
        reach = distance[None, :, slot_q] - steps_k[:, None]
        upper_ok = (reach >= 0) & (reach < W)
        lower_ok = (reach < 0) & (reach > -W)
        source_rows = jnp.clip(jnp.where(upper_ok, holder, holder + reach), 0, ext_count - 1)
        source_cols = jnp.clip(jnp.abs(reach), 0, W - 1)
        picked = band_tiles[source_rows, source_cols]
        picked = jnp.where(lower_ok[:, :, None, None], jnp.swapaxes(picked, 2, 3), picked)
        right_stack = jnp.where(
            (upper_ok | lower_ok)[:, :, None, None], picked, jnp.zeros((), band_tiles.dtype)
        )
        outputs.append(
            jnp.einsum(
                "krab,krbc->rac", left_stack, right_stack, preferred_element_type=jnp.float32
            )
        )
    return jnp.stack(outputs, axis=1)


def body(block_values, block_columns, product_columns):
    row_count = block_values.shape[0]
    first_row = lax.axis_index("rows") * row_count
    own_values, own_columns = (
        lax.all_gather(block_values, "cols", axis=1, tiled=True),
        lax.all_gather(block_columns, "cols", axis=1, tiled=True),
    )
    own_band = make_band(
        own_values, own_columns, first_row + jnp.arange(row_count, dtype=jnp.int32)
    )
    band_tiles = extend_rows(own_band)
    return block_product(band_tiles, product_columns, first_row, row_count)


def solution(mesh):
    placed = (
        P(("groups", "rows"), "cols", None, None),
        P(("groups", "rows"), "cols"),
        P(("groups", "rows"), "cols"),
    )
    return jax.shard_map(
        body,
        mesh=mesh,
        in_specs=placed,
        out_specs=P(("groups", "rows"), "cols", None, None),
        check_vma=False,
    )
```

profile of v0, /device:TPU:1, one launch (start us, length us, event | category | flops | bytes accessed | tf_op | source)
XLA Modules:
  0.0 522.4 jit_solution(2149165436565602980)
XLA Ops:
  6.5 0.7 all-gather.3.cloned.1.call-update
  7.3 10.2 %all-gather = s32[4,2,24]{2,1,0:T(2,128)S(1)} all-gather(s32[1,2,24]{2,1,0:T(2,128)} %bitcast.86), channel_id=1, replica_groups=mesh['groups'=2,'rows'=4,'cols'=4] {'cols'}, dimensions={0}, use_global_device_ids=true | all-gather | bytes 960 | tf_op jit(solution)/shard_map/all_gather | solution.py:73
  17.5 0.1 copy.52
  17.6 0.1 reshape.973
  17.7 0.1 copy.51
  17.9 0.1 copy.50
  18.0 108.6 %all-gather.3.cloned.1.call-done = bf16[24,8,128,128]{3,2,1,0:T(8,128)(2,1)} async-done(((bf16[24,2,128,128]{3,2,1,0:T(8,128)(2,1)}), bf16[24,8,128,128]{3,2,1,0:T(8,128)(2,1)}) %all-gather.3.cloned.1.call-update) | async-done | bytes 6291472 | tf_op jit(solution)/shard_map/all_gather | solution.py:72
  126.6 15.0 %gather_fusion.5 = bf16[240,128,128]{2,1,0:T(8,128)(2,1)} fusion(bf16[24,8,128,128]{3,2,1,0:T(8,128)(2,1)} %all-gather.3.cloned.1.call-done, s32[240]{0:T(256)S(1)} %reshape.973), kind=kCustom, calls=%fused_computation.5 | custom fusion | bytes 15730560 | tf_op jit(solution)/shard_map/jit(take_along_axis)/gather | solution.py:22
  141.6 4.5 select_select_fusion
  146.0 3.1 copy-done
  149.1 0.1 slice.65
  149.2 0.4 copy.77
  149.6 0.1 bitcast_select_fusion.1
  149.6 0.4 copy.54
  150.0 1.2 bitcast_dynamic-update-slice_fusion
  151.2 7.7 %slice.67 = bf16[18,10,128,128]{3,2,1,0:T(8,128)(2,1)} slice(bf16[24,10,128,128]{3,2,1,0:T(8,128)(2,1)} %bitcast_dynamic-update-slice_fusion), slice={[0:18], [0:10], [0:128], [0:128]} | slice | bytes 11796480 | tf_op jit(solution)/shard_map/slice | solution.py:32
  158.9 2.4 collective-permute-start.1
  161.3 3.8 slice.66
  165.1 3.4 collective-permute-start
  168.5 0.1 fusion.52
  168.6 0.1 reshape.943
  168.7 0.0 copy-done.3
  168.7 0.1 fusion.55
  168.8 0.1 reshape.949
  168.9 0.1 reshape.955
  169.0 0.1 reshape.961
  169.1 0.1 reshape.967
  169.2 0.7 fusion.74
  169.9 30.8 %collective-permute-done = bf16[9,10,128,128]{3,2,1,0:T(8,128)(2,1)S(1)} collective-permute-done((bf16[9,10,128,128]{3,2,1,0:T(8,128)(2,1)}, bf16[9,10,128,128]{3,2,1,0:T(8,128)(2,1)S(1)}, u32[]{:S(2)}, u32[]{:S(2)}) %collective-permute-start) | collective-permute-done | bytes 2949152 | tf_op jit(solution)/shard_map/ppermute | solution.py:12
  200.7 26.6 %collective-permute-done.1 = bf16[18,10,128,128]{3,2,1,0:T(8,128)(2,1)} collective-permute-done((bf16[18,10,128,128]{3,2,1,0:T(8,128)(2,1)}, bf16[18,10,128,128]{3,2,1,0:T(8,128)(2,1)}, u32[]{:S(2)}, u32[]{:S(2)}) %collective-permute-start.1) | collective-permute-done | bytes 5898272 | tf_op jit(solution)/shard_map/ppermute | solution.py:12
  227.3 13.0 %pad_maximum_fusion = bf16[51,10,128,128]{3,2,1,0:T(8,128)(2,1)} fusion(bf16[18,10,128,128]{3,2,1,0:T(8,128)(2,1)} %collective-permute-done.1, bf16[24,10,128,128]{3,2,1,0:T(8,128)(2,1)} %bitcast_dynamic-update-slice_fusion, bf16[9,10,128,128]{3,2,1,0:T(8,128)(2,1)S(1)} %collective-permute-done), kind=kLoop, calls=%fused_computation.6 | loop fusion | flops 16711680 | bytes 33423360 | tf_op jit(solution)/shard_map/concatenate | solution.py:33
  240.4 17.2 %gather_fusion = bf16[456,128,128]{2,1,0:T(8,128)(2,1)} fusion(bf16[51,10,128,128]{3,2,1,0:T(8,128)(2,1)} %pad_maximum_fusion, s32[456]{0:T(512)S(1)} %reshape.943), kind=kCustom, calls=%fused_computation | custom fusion | bytes 29888064 | tf_op jit(solution)/shard_map/gather | solution.py:44
  257.6 20.2 %copy.55 = bf16[19,24,128,128]{2,3,1,0:T(8,128)(2,1)} copy(bf16[19,24,128,128]{3,2,1,0:T(8,128)(2,1)} %bitcast.73) | data formatting | bytes 29884416 | tf_op jit(solution)/shard_map/gather | solution.py:44
  277.8 17.2 %gather_fusion.1 = bf16[456,128,128]{2,1,0:T(8,128)(2,1)} fusion(bf16[51,10,128,128]{3,2,1,0:T(8,128)(2,1)} %pad_maximum_fusion, s32[456]{0:T(512)S(1)} %reshape.949), kind=kCustom, calls=%fused_computation.1 | custom fusion | bytes 29888064 | tf_op jit(solution)/shard_map/gather | solution.py:55
  295.1 20.3 %copy.56 = bf16[19,24,128,128]{2,3,1,0:T(8,128)(2,1)} copy(bf16[19,24,128,128]{3,2,1,0:T(8,128)(2,1)} %bitcast.81) | data formatting | bytes 29884416 | tf_op jit(solution)/shard_map/gather | solution.py:55
  315.4 17.4 %gather_fusion.2 = bf16[456,128,128]{2,1,0:T(8,128)(2,1)} fusion(bf16[51,10,128,128]{3,2,1,0:T(8,128)(2,1)} %pad_maximum_fusion, s32[456]{0:T(512)S(1)} %reshape.955), kind=kCustom, calls=%fused_computation.2 | custom fusion | bytes 29888064 | tf_op jit(solution)/shard_map/gather | solution.py:55
  332.8 20.3 %copy.59 = bf16[19,24,128,128]{2,3,1,0:T(8,128)(2,1)} copy(bf16[19,24,128,128]{3,2,1,0:T(8,128)(2,1)} %bitcast.79) | data formatting | bytes 29884416 | tf_op jit(solution)/shard_map/gather | solution.py:55
  353.1 17.3 %gather_fusion.3 = bf16[456,128,128]{2,1,0:T(8,128)(2,1)} fusion(bf16[51,10,128,128]{3,2,1,0:T(8,128)(2,1)} %pad_maximum_fusion, s32[456]{0:T(512)S(1)} %reshape.961), kind=kCustom, calls=%fused_computation.3 | custom fusion | bytes 29888064 | tf_op jit(solution)/shard_map/gather | solution.py:55
  370.4 20.4 %copy.62 = bf16[19,24,128,128]{2,3,1,0:T(8,128)(2,1)} copy(bf16[19,24,128,128]{3,2,1,0:T(8,128)(2,1)} %bitcast.77) | data formatting | bytes 29884416 | tf_op jit(solution)/shard_map/gather | solution.py:55
  390.7 17.2 %gather_fusion.4 = bf16[456,128,128]{2,1,0:T(8,128)(2,1)} fusion(bf16[51,10,128,128]{3,2,1,0:T(8,128)(2,1)} %pad_maximum_fusion, s32[456]{0:T(512)S(1)} %reshape.967), kind=kCustom, calls=%fused_computation.4 | custom fusion | bytes 29888064 | tf_op jit(solution)/shard_map/gather | solution.py:55
  407.9 20.2 %copy.65 = bf16[19,24,128,128]{2,3,1,0:T(8,128)(2,1)} copy(bf16[19,24,128,128]{3,2,1,0:T(8,128)(2,1)} %bitcast.75) | data formatting | bytes 29884416 | tf_op jit(solution)/shard_map/gather | solution.py:55
  428.1 16.2 %broadcast_select_fusion = bf16[19,24,128,128]{2,3,1,0:T(8,128)(2,1)} fusion(bf16[19,24,128,128]{2,3,1,0:T(8,128)(2,1)} %bitcast.74, bf16[19,24,128,128]{2,3,1,0:T(8,128)(2,1)} %copy.55, pred[19]{0:T(512)(128)(4,1)S(1)} %broadcast_compare_fusion), kind=kLoop, calls=%fused_computation.19 | loop fusion | flops 7471104 | bytes 44826644 | tf_op jit(solution)/shard_map/jit(_where)/select_n | solution.py:45
  444.3 16.3 %fusion.24 = f32[24,1,128,128]{3,2,0,1:T(8,128)S(1)} fusion(bf16[19,24,128,128]{2,3,1,0:T(8,128)(2,1)} %broadcast_select_fusion, bf16[19,24,128,128]{2,3,1,0:T(8,128)(2,1)} %bitcast.82, bf16[19,24,128,128]{2,3,1,0:T(8,128)(2,1)} %copy.56, pred[19,24]{1,0:T(8,128)(4,1)S(1)} %get-tuple-element.22, pred[19,24]{1,0:T(8,128)(4,1)S(1)} %get-tuple-element.21), kind=kOutput, calls=%fused_computation.34 | convolution fusion | flops 1927544832 | bytes 46400400 | tf_op jit(solution)/shard_map/krab,krbc->rac/dot_general | solution.py:61
  460.5 16.3 %fusion.27 = f32[24,1,128,128]{3,2,0,1:T(8,128)S(1)} fusion(bf16[19,24,128,128]{2,3,1,0:T(8,128)(2,1)} %broadcast_select_fusion, bf16[19,24,128,128]{2,3,1,0:T(8,128)(2,1)} %bitcast.80, bf16[19,24,128,128]{2,3,1,0:T(8,128)(2,1)} %copy.59, pred[19,24]{1,0:T(8,128)(4,1)S(1)} %get-tuple-element.31, pred[19,24]{1,0:T(8,128)(4,1)S(1)} %get-tuple-element.32), kind=kOutput, calls=%fused_computation.35 | convolution fusion | flops 1927544832 | bytes 46400400 | tf_op jit(solution)/shard_map/krab,krbc->rac/dot_general | solution.py:61
  476.8 16.5 %fusion.30 = f32[24,1,128,128]{3,2,0,1:T(8,128)S(1)} fusion(bf16[19,24,128,128]{2,3,1,0:T(8,128)(2,1)} %broadcast_select_fusion, bf16[19,24,128,128]{2,3,1,0:T(8,128)(2,1)} %bitcast.78, bf16[19,24,128,128]{2,3,1,0:T(8,128)(2,1)} %copy.62, pred[19,24]{1,0:T(8,128)(4,1)S(1)} %get-tuple-element.33, pred[19,24]{1,0:T(8,128)(4,1)S(1)} %get-tuple-element.34), kind=kOutput, calls=%fused_computation.36 | convolution fusion | flops 1927544832 | bytes 46400400 | tf_op jit(solution)/shard_map/krab,krbc->rac/dot_general | solution.py:61
  493.3 17.4 %fusion.33 = f32[24,1,128,128]{3,2,0,1:T(8,128)} fusion(bf16[19,24,128,128]{2,3,1,0:T(8,128)(2,1)} %broadcast_select_fusion, bf16[19,24,128,128]{2,3,1,0:T(8,128)(2,1)} %bitcast.76, bf16[19,24,128,128]{2,3,1,0:T(8,128)(2,1)} %copy.65, pred[19,24]{1,0:T(8,128)(4,1)S(1)} %copy-done.1, pred[19,24]{1,0:T(8,128)(4,1)S(1)} %copy-done.2), kind=kOutput, calls=%fused_computation.37 | convolution fusion | flops 1927544832 | bytes 46400400 | tf_op jit(solution)/shard_map/krab,krbc->rac/dot_general | solution.py:61
  510.7 1.7 pad_maximum_fusion.1
  512.4 3.1 copy.68
  (22 shorter events, 0.2 us)
Async XLA Ops:
  6.5 120.1 %all-gather.3.cloned.1.call-start = ((), (), s32[]{:S(2)}) async-start(), calls=%async_computation | async-start | bytes 7864320 | tf_op jit(solution)/shard_map/all_gather | solution.py:72
  146.0 3.1 copy-start
  149.1 19.6 %copy-start.3 = (s32[24,4]{0,1:T(4,128)S(1)}, s32[24,4]{0,1:T(4,128)}, u32[]{:S(2)}) copy-start(s32[24,4]{0,1:T(4,128)} %param.7) | copy-start | bytes 1156
  158.9 68.4 %collective-permute-start.1 = (bf16[18,10,128,128]{3,2,1,0:T(8,128)(2,1)}, bf16[18,10,128,128]{3,2,1,0:T(8,128)(2,1)}, u32[]{:S(2)}, u32[]{:S(2)}) collective-permute-start(bf16[18,10,128,128]{3,2,1,0:T(8,128)(2,1)} %slice.67), channel_id=1, source_target_pairs={{4,0},{8,4},{12,8},{5,1},{9,5},{13,9},{6,2},{10,6},{14,10},{7,3},{... | collective-permute-start | bytes 17694728 | tf_op jit(solution)/shard_map/ppermute | solution.py:12
  165.1 35.6 %collective-permute-start = (bf16[9,10,128,128]{3,2,1,0:T(8,128)(2,1)}, bf16[9,10,128,128]{3,2,1,0:T(8,128)(2,1)S(1)}, u32[]{:S(2)}, u32[]{:S(2)}) collective-permute-start(bf16[9,10,128,128]{3,2,1,0:T(8,128)(2,1)} %slice.66), channel_id=1, source_target_pairs={{0,4},{4,8},{8,12},{1,5},{5,9},{9,13},{2,6},{6,10},{10,14},{3,7},{... | collective-permute-start | bytes 8847368 | tf_op jit(solution)/shard_map/ppermute | solution.py:12
  476.8 16.5 %copy-start.1 = (pred[19,24]{1,0:T(8,128)(4,1)S(1)}, pred[19,24]{1,0:T(8,128)(4,1)}, u32[]{:S(2)}) copy-start(pred[19,24]{1,0:T(8,128)(4,1)} %get-tuple-element.29) | copy-start | bytes 1372
  476.8 16.5 %copy-start.2 = (pred[19,24]{1,0:T(8,128)(4,1)S(1)}, pred[19,24]{1,0:T(8,128)(4,1)}, u32[]{:S(2)}) copy-start(pred[19,24]{1,0:T(8,128)(4,1)} %get-tuple-element.30) | copy-start | bytes 1372
Sparse Core Ops, SparseCore 0:
  8.9 117.6 all-gather.2
where the time goes:
time: 526 us; the launch traced here: 522 us
  local copies, waits for them, and re-layouts  222 us (42%)
  waiting for transfers between devices  167 us (32%)
  matrix products  66.4 us (13%)
  other arithmetic  37.7 us (7%)
  between operations  13.6 us (3%)
  blocking collectives  10.2 us (2%)
  starting transfers between devices  5.72 us (1%)
    gather x8, local copies, waits for them, and re-layouts, block_product(): picked = band_tiles[source_rows, source_cols]  150 us
    all_gather x1, waiting for transfers between devices, body(): lax.all_gather(block_values, 'cols', axis=1, tiled=True)  109 us
    dot_general x4, matrix products, block_product(): jnp.einsum('krab,krbc->rac', left_stack, right_stack, preferred_element_t...  66.4 us
    ppermute x2, waiting for transfers between devices, from_behind(): return lax.ppermute(array, axis, pairs)  57.4 us
    gather x2, local copies, waits for them, and re-layouts, block_product(): left_raw = band_tiles[holder, jnp.abs(steps_k)[:, None]]  37.5 us
    select_n x1, other arithmetic, block_product(): jnp.where((steps_k < 0)[:, None, None, None], jnp.swapaxes(left_raw, 2, 3...  16.2 us
    gather x3, local copies, waits for them, and re-layouts, make_band(): taken = jnp.take_along_axis(values, source[:, :, None, None], axis=1)  15.1 us
    concatenate x1, other arithmetic, extend_rows(): return jnp.concatenate([before, tiles, after], axis=0)  13 us
  transfers between devices with their start and end apart: 3, of which 3 were waited for; matrix products, arithmetic and copies ran while one was open for 1% of the time, Pallas kernels for 0%

commit v1 on v0

v1 whole, which is shorter than its diff:
```python
import functools

import jax
import jax.numpy as jnp
from jax import lax
from jax.experimental import pallas as pl
from jax.experimental.pallas import tpu as pltpu
from jax.sharding import PartitionSpec as P

W = 10
LEAD = W - 1
SPAN = 2 * W - 1
UNROLL = 4
BITS = 10
MASK = (1 << BITS) - 1


def up_pairs(size, step):
    return [(i, i + 1) for i in range(step - 1, size - 1)]


def down_pairs(size, step):
    return [(i + 1, i) for i in range(size - step)]


def row_shift(array, by):
    size = lax.axis_size("rows")
    return lax.ppermute(array, "rows", [(i, i + by) for i in range(size) if 0 <= i + by < size])


def factor_table(columns, first_row, row_count):
    total, slots = columns.shape
    ext = row_count + 2 * LEAD
    padded = jnp.pad(columns, ((LEAD, LEAD), (0, 0)), constant_values=-1)
    here = lax.dynamic_slice_in_dim(padded, first_row, ext, 0)
    row_ids = first_row - LEAD + jnp.arange(ext, dtype=jnp.int32)
    offsets = jnp.where(here >= 0, here - row_ids[:, None], -1)
    reach = jnp.arange(W, dtype=jnp.int32)
    slot_ids = jnp.arange(slots, dtype=jnp.int32)
    index = jnp.arange(ext, dtype=jnp.int32)[:, None] * slots + slot_ids[None, :]
    picked = offsets[:, :, None] == reach[None, None, :]
    upper = jnp.max(jnp.where(picked, index[:, :, None], -1), axis=1)
    lower = jnp.where(upper >= 0, upper + ext * slots, -1)
    parts = []
    for m in range(LEAD, 0, -1):
        parts.append(jnp.pad(lower[: ext - m, m], (m, 0), constant_values=-1)[:, None])
    return jnp.concatenate(parts + [upper], axis=1)


def list_kernel(row_count, slot_count, zero_id, first_ref, table_ref, wanted_ref, left_ref, right_ref, count_ref):
    first = first_ref[0]

    def per_output(out_id, base):
        row = out_id // slot_count
        slot = out_id - row * slot_count
        want = wanted_ref[row, slot]
        distance = want - first - row
        start = jnp.where(want >= 0, distance - LEAD, W)

        def per_step(step, count):
            left = table_ref[row + LEAD + jnp.maximum(step, 0), step + LEAD]
            right = table_ref[row + LEAD + step, distance - step + LEAD]
            valid = (left >= 0) & (right >= 0)
            at = base + count // 2

            @pl.when(valid & (count % 2 == 0))
            def _():
                left_ref[at] = left | (zero_id << BITS)
                right_ref[at] = right | (zero_id << BITS) | (out_id << (2 * BITS))

            @pl.when(valid & (count % 2 == 1))
            def _():
                left_ref[at] = (left_ref[at] & MASK) | (left << BITS)
                right_ref[at] = (right_ref[at] & ~(MASK << BITS)) | (right << BITS)

            return count + valid.astype(jnp.int32)

        count = lax.fori_loop(start, W, per_step, jnp.int32(0))
        return base + (count + 1) // 2

    total = lax.fori_loop(0, row_count * slot_count, per_output, jnp.int32(0))
    for extra in range(UNROLL):
        left_ref[total + extra] = zero_id | (zero_id << BITS)
        right_ref[total + extra] = zero_id | (zero_id << BITS)
    count_ref[0] = (total + UNROLL - 1) // UNROLL


def product_kernel(plan, out_count, ext, slots, here_ref, left_ref, right_ref, count_ref, *refs):
    count = len(plan)
    pieces, out_ref, blocks, sem = refs[:count], refs[count], refs[count + 1], refs[count + 2]
    cols = here_ref[1]
    me = here_ref[0]
    stored = ext * slots

    def copies(go):
        for n, (piece, (rows, shift)) in enumerate(zip(pieces, plan)):
            own = piece.shape[1]
            owner = me + shift

            @pl.when((owner >= 0) & (owner < cols))
            def _(piece=piece, rows=rows, owner=owner, own=own):
                for r in range(piece.shape[0]):
                    go(pltpu.make_async_copy(piece.at[r], blocks.at[pl.ds((rows + r) * slots + owner * own, own)], sem))

    copies(lambda c: c.start())
    out_ref[...] = jnp.zeros_like(out_ref)
    blocks[2 * stored] = jnp.zeros(blocks.shape[1:], blocks.dtype)
    copies(lambda c: c.wait())

    def turn(row, _):
        at = row * slots
        tile = blocks[at]
        a = lax.broadcasted_iota(jnp.int32, tile.shape, 0)
        b = lax.broadcasted_iota(jnp.int32, tile.shape, 1)
        wide = tile.astype(jnp.float32)
        whole = jnp.where(a <= b, wide, wide.T).astype(tile.dtype)
        blocks[at] = whole
        blocks[stored + at] = whole
        for s in range(1, slots):
            blocks[stored + at + s] = blocks[at + s].T
        return 0

    lax.fori_loop(0, ext, turn, 0)

    def multiply(group, _):
        sums = []
        for u in range(UNROLL):
            left = left_ref[group * UNROLL + u]
            right = right_ref[group * UNROLL + u]
            lhs = jnp.concatenate([blocks[left & MASK], blocks[left >> BITS]], axis=1)
            rhs = jnp.concatenate([blocks[right & MASK], blocks[(right >> BITS) & MASK]], axis=0)
            sums.append((right >> (2 * BITS), jnp.dot(lhs, rhs, preferred_element_type=jnp.float32)))
        for at, value in sums:
            out_ref[at] += value
        return 0

    lax.fori_loop(0, count_ref[0], multiply, 0)


def body(block_values, block_columns, product_columns):
    row_count, own, tile, _ = block_values.shape
    size = lax.axis_size("cols")
    slots = size * own
    wanted_slots = product_columns.shape[1]
    ext = row_count + 2 * LEAD
    first_row = lax.axis_index("rows") * row_count
    me = lax.axis_index("cols")

    spans = [(0, LEAD), (row_count - LEAD, row_count), (LEAD, row_count - LEAD)]
    plan, pieces = [], []

    def keep(array, rows, shift):
        plan.append((rows, shift))
        pieces.append(array)

    def halo(part, array, shift):
        if part == 0:
            keep(row_shift(array, -1), LEAD + row_count, shift)
        if part == 1:
            keep(row_shift(array, 1), 0, shift)

    going_up = [block_values[a:b] for a, b in spans]
    going_down = list(going_up)
    keep(block_values, LEAD, 0)
    halo(0, going_up[0], 0)
    halo(1, going_up[1], 0)
    for step in range(1, size):
        for part, (start, _) in enumerate(spans):
            going_up[part] = lax.ppermute(going_up[part], "cols", up_pairs(size, step))
            going_down[part] = lax.ppermute(going_down[part], "cols", down_pairs(size, step))
            keep(going_up[part], LEAD + start, -step)
            keep(going_down[part], LEAD + start, step)
            halo(part, going_up[part], -step)
            halo(part, going_down[part], step)

    columns = lax.all_gather(block_columns, ("rows", "cols"), axis=0)
    columns = columns.reshape(-1, size, row_count, own).swapaxes(1, 2).reshape(-1, slots)
    table = factor_table(columns, first_row, row_count)

    smem = pl.BlockSpec(memory_space=pltpu.SMEM)
    out_count = row_count * wanted_slots
    cap = out_count * W + UNROLL
    zero_id = 2 * ext * slots
    left, right, count = pl.pallas_call(
        functools.partial(list_kernel, row_count, wanted_slots, zero_id),
        out_shape=[jax.ShapeDtypeStruct((cap,), jnp.int32)] * 2 + [jax.ShapeDtypeStruct((1,), jnp.int32)],
        in_specs=[smem] * 3,
        out_specs=[smem] * 3,
    )(first_row.reshape(1), table, product_columns)

    out = pl.pallas_call(
        functools.partial(product_kernel, tuple(plan), out_count, ext, slots),
        out_shape=jax.ShapeDtypeStruct((out_count, tile, tile), jnp.float32),
        in_specs=[smem] * 4 + [pl.BlockSpec(memory_space=pl.ANY)] * len(pieces),
        out_specs=pl.BlockSpec(memory_space=pltpu.VMEM),
        scratch_shapes=[
            pltpu.VMEM((2 * ext * slots + 1, tile, tile), block_values.dtype),
            pltpu.SemaphoreType.DMA,
        ],
        compiler_params=pltpu.CompilerParams(vmem_limit_bytes=48 << 20),
    )(jnp.stack([me, jnp.int32(size)]), left, right, count, *pieces)
    return out.reshape(row_count, wanted_slots, tile, tile)


def solution(mesh):
    placed = (
        P(("groups", "rows"), "cols", None, None),
        P(("groups", "rows"), "cols"),
        P(("groups", "rows"), "cols"),
    )
    return jax.shard_map(
        body,
        mesh=mesh,
        in_specs=placed,
        out_specs=P(("groups", "rows"), "cols", None, None),
        check_vma=False,
    )
```

time: 526 us -> 240 us (0.46)
  local copies, waits for them, and re-layouts: 222 us -> 36.3 us
  waiting for transfers between devices: 167 us -> 10.9 us
  starting transfers between devices: 5.72 us -> 87.7 us
  Pallas kernels: 0 us -> 68.6 us
  matrix products: 66.4 us -> 0 us
  other arithmetic: 37.7 us -> 0.2 us
  blocking collectives: 10.2 us -> 32.8 us
  between operations: 13.6 us -> 0.6 us
    gather x13 -> x0, local copies, waits for them, and re-layouts: 203 us -> none  [the longest x8 150 us: block_product(): picked = band_tiles[source_rows, source_cols]]
    all_gather x1 -> x0, waiting for transfers between devices: 109 us -> none  [body(): lax.all_gather(block_values, 'cols', axis=1, tiled=True)]
    ppermute x2 -> x32, starting transfers between devices: 5.72 us -> 87.7 us  [the longest x14 54.7 us: row_shift(): lax.ppermute(array, 'rows', [(i, i + by) for i in range(size) if 0 <= i +...]
    pallas_call x0 -> x2, Pallas kernels: none -> 68.6 us  [the longest x1 38.9 us: body(): pl.pallas_call(functools.partial(product_kernel, tuple(plan), out_count,...]
    dot_general x4 -> x0, matrix products: 66.4 us -> none  [block_product(): jnp.einsum('krab,krbc->rac', left_stack, right_stack, preferred_element_t...]
    ppermute x2 -> x32, waiting for transfers between devices: 57.4 us -> 10.9 us  [the longest x9 10.8 us: body(): lax.ppermute(going_down[part], 'cols', down_pairs(size, step))]
    all_gather x1, blocking collectives: 10.2 us -> 32.8 us  [body(): columns = lax.all_gather(block_columns, ('rows', 'cols'), axis=0)]
    select_n x4 -> x1, other arithmetic: 20.7 us -> 0.01 us  [factor_table(): lower = jnp.where(upper >= 0, upper + ext * slots, -1)]
  transfers between devices with their start and end apart: 3 -> 32, of which waited for: 3 -> 5; matrix products, arithmetic and copies ran while one was open for 1% -> 10% of each run, Pallas kernels for 0% -> 13%
where the time goes in v1:
time: 240 us; the launch traced here: 237 us
  starting transfers between devices  87.7 us (37%)
  Pallas kernels  68.6 us (29%)
  local copies, waits for them, and re-layouts  36.3 us (15%)
  blocking collectives  32.8 us (14%)
  waiting for transfers between devices  10.9 us (5%)
    ppermute x14, starting transfers between devices, row_shift(): lax.ppermute(array, 'rows', [(i, i + by) for i in range(size) if 0 <= i +...  54.7 us
    pallas_call x1, Pallas kernels, body(): pl.pallas_call(functools.partial(product_kernel, tuple(plan), out_count,...  38.9 us
    all_gather x1, blocking collectives, body(): columns = lax.all_gather(block_columns, ('rows', 'cols'), axis=0)  32.8 us
    pallas_call x1, Pallas kernels, body(): pl.pallas_call(functools.partial(list_kernel, row_count, wanted_slots, ze...  29.7 us
    ppermute x9, starting transfers between devices, body(): going_up[part] = lax.ppermute(going_up[part], 'cols', up_pairs(size, step))  21.4 us
    broadcast_in_dim x18, local copies, waits for them, and re-layouts, factor_table(): jnp.pad(lower[:ext - m, m], (m, 0), constant_values=-1)[:, None]  16.1 us
    unnamed x49, local copies, waits for them, and re-layouts  14 us
    ppermute x9, starting transfers between devices, body(): lax.ppermute(going_down[part], 'cols', down_pairs(size, step))  11.6 us
  transfers between devices with their start and end apart: 32, of which 5 were waited for; matrix products, arithmetic and copies ran while one was open for 10% of the time, Pallas kernels for 13%

profile of v1, /device:TPU:1, one launch (start us, length us, event | category | flops | bytes accessed | tf_op | source)
XLA Modules:
  0.0 237.1 jit_solution(7084587256159757428)
XLA Ops:
  0.0 1.0 slice.47
  1.0 1.3 collective-permute-start.11
  2.3 4.7 %collective-permute-start.10 = (bf16[6,2,128,128]{3,2,1,0:T(8,128)(2,1)S(1)}, bf16[6,2,128,128]{3,2,1,0:T(8,128)(2,1)S(1)}, u32[]{:S(2)}, u32[]{:S(2)}) collective-permute-start(bf16[6,2,128,128]{3,2,1,0:T(8,128)(2,1)S(1)} %slice.47), channel_id=1, source_target_pairs={{0,1},{1,2},{2,3},{4,5},{5,6},{6,7},{8,9},{9,10},{10,11},{12,13},{... | collective-permute-start | bytes 1179656 | tf_op jit(solution)/shard_map/ppermute | solution.py:169
  7.0 2.2 fusion
  9.2 1.3 collective-permute-start.7
  10.5 4.8 %collective-permute-start.6 = (bf16[9,2,128,128]{3,2,1,0:T(8,128)(2,1)S(1)}, bf16[9,2,128,128]{3,2,1,0:T(8,128)(2,1)}, u32[]{:S(2)}, u32[]{:S(2)}) collective-permute-start(bf16[9,2,128,128]{3,2,1,0:T(8,128)(2,1)S(1)} %get-tuple-element.11), channel_id=1, source_target_pairs={{0,1},{1,2},{2,3},{4,5},{5,6},{6,7},{8,9},{9,10},{10,11},{12,13},{... | collective-permute-start | bytes 1769480 | tf_op jit(solution)/shard_map/ppermute | solution.py:169
  15.3 4.9 %collective-permute-start.1 = (bf16[9,2,128,128]{3,2,1,0:T(8,128)(2,1)S(1)}, bf16[9,2,128,128]{3,2,1,0:T(8,128)(2,1)S(1)}, u32[]{:S(2)}, u32[]{:S(2)}) collective-permute-start(bf16[9,2,128,128]{3,2,1,0:T(8,128)(2,1)S(1)} %get-tuple-element.11), channel_id=1, source_target_pairs={{0,4},{4,8},{8,12},{1,5},{5,9},{9,13},{2,6},{6,10},{10,14},{3,7},{... | collective-permute-start | bytes 1769480 | tf_op jit(solution)/shard_map/ppermute | solution.py:28
  20.3 32.8 %all-gather.1 = s32[16,24,2]{1,2,0:T(2,128)S(1)} all-gather(s32[1,24,2]{1,2,0:T(2,128)S(1)} %bitcast.48), channel_id=2, replica_groups=mesh['groups'=2,'rows'=4,'cols'=4] {'rows','cols'}, dimensions={0}, use_global_device_ids=true | all-gather | bytes 3264 | tf_op jit(solution)/shard_map/all_gather | solution.py:176
  53.2 1.3 collective-permute-start.21
  57.7 1.3 collective-permute-start.3
  59.0 5.3 %collective-permute-start.2 = (bf16[9,2,128,128]{3,2,1,0:T(8,128)(2,1)}, bf16[9,2,128,128]{3,2,1,0:T(8,128)(2,1)S(1)}, u32[]{:S(2)}, u32[]{:S(2)}) collective-permute-start(bf16[9,2,128,128]{3,2,1,0:T(8,128)(2,1)} %get-tuple-element.12), channel_id=1, source_target_pairs={{0,1},{1,2},{2,3},{4,5},{5,6},{6,7},{8,9},{9,10},{10,11},{12,13},{... | collective-permute-start | bytes 1769480 | tf_op jit(solution)/shard_map/ppermute | solution.py:169
  64.3 5.1 %collective-permute-start = (bf16[9,2,128,128]{3,2,1,0:T(8,128)(2,1)}, bf16[9,2,128,128]{3,2,1,0:T(8,128)(2,1)S(1)}, u32[]{:S(2)}, u32[]{:S(2)}) collective-permute-start(bf16[9,2,128,128]{3,2,1,0:T(8,128)(2,1)} %get-tuple-element.12), channel_id=1, source_target_pairs={{4,0},{8,4},{12,8},{5,1},{9,5},{13,9},{6,2},{10,6},{14,10},{7,3},{... | collective-permute-start | bytes 1769480 | tf_op jit(solution)/shard_map/ppermute | solution.py:28
  69.4 1.3 collective-permute-start.31
  72.9 3.5 %collective-permute-done.3.refs_4_ = bf16[9,2,128,128]{3,2,1,0:T(8,128)(2,1)S(1)} collective-permute-done((bf16[9,2,128,128]{3,2,1,0:T(8,128)(2,1)}, bf16[9,2,128,128]{3,2,1,0:T(8,128)(2,1)S(1)}, u32[]{:S(2)}, u32[]{:S(2)}) %collective-permute-start.3) | collective-permute-done | bytes 589856 | tf_op jit(solution)/shard_map/ppermute | solution.py:170
  76.4 1.3 collective-permute-start.17
  77.7 7.9 %collective-permute-start.9 = (bf16[9,2,128,128]{3,2,1,0:T(8,128)(2,1)}, bf16[9,2,128,128]{3,2,1,0:T(8,128)(2,1)S(1)}, u32[]{:S(2)}, u32[]{:S(2)}) collective-permute-start(bf16[9,2,128,128]{3,2,1,0:T(8,128)(2,1)} %copy-done.14), channel_id=1, source_target_pairs={{0,4},{4,8},{8,12},{1,5},{5,9},{9,13},{2,6},{6,10},{10,14},{3,7},{... | collective-permute-start | bytes 1769480 | tf_op jit(solution)/shard_map/ppermute | solution.py:28
  87.2 6.4 %collective-permute-start.8 = (bf16[9,2,128,128]{3,2,1,0:T(8,128)(2,1)}, bf16[9,2,128,128]{3,2,1,0:T(8,128)(2,1)S(1)}, u32[]{:S(2)}, u32[]{:S(2)}) collective-permute-start(bf16[9,2,128,128]{3,2,1,0:T(8,128)(2,1)} %collective-permute-done.6.refs_7_), channel_id=1, source_target_pairs={{0,4},{4,8},{8,12},{1,5},{5,9},{9,13},{2,6},{6,10},{10,14},{3,7},{... | collective-permute-start | bytes 1769480 | tf_op jit(solution)/shard_map/ppermute | solution.py:28
  94.3 1.3 collective-permute-start.13
  97.5 5.7 %collective-permute-start.5 = (bf16[9,2,128,128]{3,2,1,0:T(8,128)(2,1)S(1)}, bf16[9,2,128,128]{3,2,1,0:T(8,128)(2,1)S(1)}, u32[]{:S(2)}, u32[]{:S(2)}) collective-permute-start(bf16[9,2,128,128]{3,2,1,0:T(8,128)(2,1)S(1)} %collective-permute-done.3.refs_4_), channel_id=1, source_target_pairs={{4,0},{8,4},{12,8},{5,1},{9,5},{13,9},{6,2},{10,6},{14,10},{7,3},{... | collective-permute-start | bytes 1769480 | tf_op jit(solution)/shard_map/ppermute | solution.py:28
  103.2 1.5 collective-permute-start.12
  104.7 1.9 collective-permute-start.4
  106.6 1.3 collective-permute-start.27
  107.9 3.7 %collective-permute-done.13.refs_14_ = bf16[9,2,128,128]{3,2,1,0:T(8,128)(2,1)S(1)} collective-permute-done((bf16[9,2,128,128]{3,2,1,0:T(8,128)(2,1)S(1)}, bf16[9,2,128,128]{3,2,1,0:T(8,128)(2,1)S(1)}, u32[]{:S(2)}, u32[]{:S(2)}) %collective-permute-start.13) | collective-permute-done | bytes 589856 | tf_op jit(solution)/shard_map/ppermute | solution.py:170
  111.6 4.1 %collective-permute-start.19 = (bf16[9,2,128,128]{3,2,1,0:T(8,128)(2,1)S(1)}, bf16[9,2,128,128]{3,2,1,0:T(8,128)(2,1)S(1)}, u32[]{:S(2)}, u32[]{:S(2)}) collective-permute-start(bf16[9,2,128,128]{3,2,1,0:T(8,128)(2,1)S(1)} %collective-permute-done.17.refs_18_), channel_id=1, source_target_pairs={{0,4},{4,8},{8,12},{1,5},{5,9},{9,13},{2,6},{6,10},{10,14},{3,7},{... | collective-permute-start | bytes 1769480 | tf_op jit(solution)/shard_map/ppermute | solution.py:28
  117.0 1.5 collective-permute-start.26
  118.5 1.9 collective-permute-start.18
  120.5 1.3 collective-permute-start.23
  121.8 2.6 %collective-permute-done.27.refs_28_ = bf16[9,2,128,128]{3,2,1,0:T(8,128)(2,1)} collective-permute-done((bf16[9,2,128,128]{3,2,1,0:T(8,128)(2,1)S(1)}, bf16[9,2,128,128]{3,2,1,0:T(8,128)(2,1)}, u32[]{:S(2)}, u32[]{:S(2)}) %collective-permute-start.27) | collective-permute-done | bytes 589856 | tf_op jit(solution)/shard_map/ppermute | solution.py:170
  124.3 3.3 %collective-permute-start.15 = (bf16[9,2,128,128]{3,2,1,0:T(8,128)(2,1)S(1)}, bf16[9,2,128,128]{3,2,1,0:T(8,128)(2,1)S(1)}, u32[]{:S(2)}, u32[]{:S(2)}) collective-permute-start(bf16[9,2,128,128]{3,2,1,0:T(8,128)(2,1)S(1)} %collective-permute-done.13.refs_14_), channel_id=1, source_target_pairs={{4,0},{8,4},{12,8},{5,1},{9,5},{13,9},{6,2},{10,6},{14,10},{7,3},{... | collective-permute-start | bytes 1769480 | tf_op jit(solution)/shard_map/ppermute | solution.py:28
  127.7 1.5 collective-permute-start.22
  131.1 1.9 collective-permute-start.14
  133.0 3.6 %collective-permute-start.29 = (bf16[9,2,128,128]{3,2,1,0:T(8,128)(2,1)}, bf16[9,2,128,128]{3,2,1,0:T(8,128)(2,1)}, u32[]{:S(2)}, u32[]{:S(2)}) collective-permute-start(bf16[9,2,128,128]{3,2,1,0:T(8,128)(2,1)} %collective-permute-done.27.refs_28_), channel_id=1, source_target_pairs={{0,4},{4,8},{8,12},{1,5},{5,9},{9,13},{2,6},{6,10},{10,14},{3,7},{... | collective-permute-start | bytes 1769480 | tf_op jit(solution)/shard_map/ppermute | solution.py:28
  137.1 4.1 %collective-permute-start.28 = (bf16[9,2,128,128]{3,2,1,0:T(8,128)(2,1)}, bf16[9,2,128,128]{3,2,1,0:T(8,128)(2,1)}, u32[]{:S(2)}, u32[]{:S(2)}) collective-permute-start(bf16[9,2,128,128]{3,2,1,0:T(8,128)(2,1)} %collective-permute-done.26.refs_27_), channel_id=1, source_target_pairs={{0,4},{4,8},{8,12},{1,5},{5,9},{9,13},{2,6},{6,10},{10,14},{3,7},{... | collective-permute-start | bytes 1769480 | tf_op jit(solution)/shard_map/ppermute | solution.py:28
  141.3 1.9 collective-permute-start.25
  143.2 1.9 collective-permute-start.24
  146.4 1.4 copy.49.wanted_ref
  147.8 1.3 copy.40
  149.1 1.4 copy.39
  150.4 1.4 copy.41
  151.8 1.4 copy.42
  153.2 1.4 copy.43
  154.5 1.4 copy.44
  155.9 1.3 copy.45
  159.4 1.6 concatenate.3.table_ref
  161.0 29.7 %shard_map.37 = (s32[964]{0:T(1024)}, s32[964]{0:T(1024)}, s32[1]{0:T(128)}) custom-call(s32[1]{0:T(128)} %bitcast.1.first_ref, s32[42,19]{1,0:T(8,128)} %concatenate.3.table_ref, s32[24,4]{1,0:T(8,128)} %copy.49.wanted_ref), custom_call_target="tpu_custom_call" | custom-call | tf_op jit(solution)/shard_map/pallas_call | solution.py:184
  191.9 1.0 copy-done.3
  194.9 1.0 copy-done.9
  198.2 38.9 %shard_map.38 = f32[96,128,128]{2,1,0:T(8,128)} custom-call(s32[2]{0:T(128)S(1)} %pad_add_fusion.here_ref, s32[964]{0:T(1024)S(1)} %copy-done.12, s32[964]{0:T(1024)S(1)} %copy-done.13, s32[1]{0:T(128)} %get-tuple-element.10.count_ref, bf16[24,2,128,128]{3,2,1,0:T(8,128)(2,1)} %refs_0_.1, bf16[9,2,128,128]{3,2,1,0:T(8,128)(2,1)S(1)} %collective-permute-done.refs_1_, ...), custom_call_target="tpu_custom_call" | custom-call | tf_op jit(solution)/shard_map/pallas_call | solution.py:191
  (107 shorter events, 22.1 us)
Async XLA Ops:
  0.0 20.3 %copy-start.23 = (s32[24,2]{0,1:T(2,128)S(1)}, s32[24,2]{0,1:T(2,128)}, u32[]{:S(2)}) copy-start(s32[24,2]{0,1:T(2,128)} %param.4) | copy-start | bytes 580
  1.0 52.1 %collective-permute-start.11 = (bf16[6,2,128,128]{3,2,1,0:T(8,128)(2,1)S(1)}, bf16[6,2,128,128]{3,2,1,0:T(8,128)(2,1)S(1)}, u32[]{:S(2)}, u32[]{:S(2)}) collective-permute-start(bf16[6,2,128,128]{3,2,1,0:T(8,128)(2,1)S(1)} %slice.47), channel_id=1, source_target_pairs={{1,0},{2,1},{3,2},{5,4},{6,5},{7,6},{9,8},{10,9},{11,10},{13,12},{... | collective-permute-start | bytes 1179656 | tf_op jit(solution)/shard_map/ppermute | solution.py:170
  2.3 52.9 %collective-permute-start.10 = (bf16[6,2,128,128]{3,2,1,0:T(8,128)(2,1)S(1)}, bf16[6,2,128,128]{3,2,1,0:T(8,128)(2,1)S(1)}, u32[]{:S(2)}, u32[]{:S(2)}) collective-permute-start(bf16[6,2,128,128]{3,2,1,0:T(8,128)(2,1)S(1)} %slice.47), channel_id=1, source_target_pairs={{0,1},{1,2},{2,3},{4,5},{5,6},{6,7},{8,9},{9,10},{10,11},{12,13},{... | collective-permute-start | bytes 1179656 | tf_op jit(solution)/shard_map/ppermute | solution.py:169
  9.2 47.6 %collective-permute-start.7 = (bf16[9,2,128,128]{3,2,1,0:T(8,128)(2,1)S(1)}, bf16[9,2,128,128]{3,2,1,0:T(8,128)(2,1)S(1)}, u32[]{:S(2)}, u32[]{:S(2)}) collective-permute-start(bf16[9,2,128,128]{3,2,1,0:T(8,128)(2,1)S(1)} %get-tuple-element.11), channel_id=1, source_target_pairs={{1,0},{2,1},{3,2},{5,4},{6,5},{7,6},{9,8},{10,9},{11,10},{13,12},{... | collective-permute-start | bytes 1769480 | tf_op jit(solution)/shard_map/ppermute | solution.py:170
  10.5 48.5 %collective-permute-start.6 = (bf16[9,2,128,128]{3,2,1,0:T(8,128)(2,1)S(1)}, bf16[9,2,128,128]{3,2,1,0:T(8,128)(2,1)}, u32[]{:S(2)}, u32[]{:S(2)}) collective-permute-start(bf16[9,2,128,128]{3,2,1,0:T(8,128)(2,1)S(1)} %get-tuple-element.11), channel_id=1, source_target_pairs={{0,1},{1,2},{2,3},{4,5},{5,6},{6,7},{8,9},{9,10},{10,11},{12,13},{... | collective-permute-start | bytes 1769480 | tf_op jit(solution)/shard_map/ppermute | solution.py:169
  15.3 48.9 %collective-permute-start.1 = (bf16[9,2,128,128]{3,2,1,0:T(8,128)(2,1)S(1)}, bf16[9,2,128,128]{3,2,1,0:T(8,128)(2,1)S(1)}, u32[]{:S(2)}, u32[]{:S(2)}) collective-permute-start(bf16[9,2,128,128]{3,2,1,0:T(8,128)(2,1)S(1)} %get-tuple-element.11), channel_id=1, source_target_pairs={{0,4},{4,8},{8,12},{1,5},{5,9},{9,13},{2,6},{6,10},{10,14},{3,7},{... | collective-permute-start | bytes 1769480 | tf_op jit(solution)/shard_map/ppermute | solution.py:28
  53.2 16.2 %collective-permute-start.21 = (bf16[6,2,128,128]{3,2,1,0:T(8,128)(2,1)S(1)}, bf16[6,2,128,128]{3,2,1,0:T(8,128)(2,1)S(1)}, u32[]{:S(2)}, u32[]{:S(2)}) collective-permute-start(bf16[6,2,128,128]{3,2,1,0:T(8,128)(2,1)S(1)} %collective-permute-done.11.refs_12_), channel_id=1, source_target_pairs={{1,0},{2,1},{5,4},{6,5},{9,8},{10,9},{13,12},{14,13},{17,16},{18,1... | collective-permute-start | bytes 1179656 | tf_op jit(solution)/shard_map/ppermute | solution.py:170
  55.3 16.2 %collective-permute-start.20 = (bf16[6,2,128,128]{3,2,1,0:T(8,128)(2,1)S(1)}, bf16[6,2,128,128]{3,2,1,0:T(8,128)(2,1)S(1)}, u32[]{:S(2)}, u32[]{:S(2)}) collective-permute-start(bf16[6,2,128,128]{3,2,1,0:T(8,128)(2,1)S(1)} %collective-permute-done.10.refs_11_), channel_id=1, source_target_pairs={{1,2},{2,3},{5,6},{6,7},{9,10},{10,11},{13,14},{14,15},{17,18},{18... | collective-permute-start | bytes 1179656 | tf_op jit(solution)/shard_map/ppermute | solution.py:169
  56.8 0.8 copy-start.14
  57.7 18.8 %collective-permute-start.3 = (bf16[9,2,128,128]{3,2,1,0:T(8,128)(2,1)}, bf16[9,2,128,128]{3,2,1,0:T(8,128)(2,1)S(1)}, u32[]{:S(2)}, u32[]{:S(2)}) collective-permute-start(bf16[9,2,128,128]{3,2,1,0:T(8,128)(2,1)} %get-tuple-element.12), channel_id=1, source_target_pairs={{1,0},{2,1},{3,2},{5,4},{6,5},{7,6},{9,8},{10,9},{11,10},{13,12},{... | collective-permute-start | bytes 1769480 | tf_op jit(solution)/shard_map/ppermute | solution.py:170
  59.0 18.8 %collective-permute-start.2 = (bf16[9,2,128,128]{3,2,1,0:T(8,128)(2,1)}, bf16[9,2,128,128]{3,2,1,0:T(8,128)(2,1)S(1)}, u32[]{:S(2)}, u32[]{:S(2)}) collective-permute-start(bf16[9,2,128,128]{3,2,1,0:T(8,128)(2,1)} %get-tuple-element.12), channel_id=1, source_target_pairs={{0,1},{1,2},{2,3},{4,5},{5,6},{6,7},{8,9},{9,10},{10,11},{12,13},{... | collective-permute-start | bytes 1769480 | tf_op jit(solution)/shard_map/ppermute | solution.py:169
  64.3 21.4 %collective-permute-start = (bf16[9,2,128,128]{3,2,1,0:T(8,128)(2,1)}, bf16[9,2,128,128]{3,2,1,0:T(8,128)(2,1)S(1)}, u32[]{:S(2)}, u32[]{:S(2)}) collective-permute-start(bf16[9,2,128,128]{3,2,1,0:T(8,128)(2,1)} %get-tuple-element.12), channel_id=1, source_target_pairs={{4,0},{8,4},{12,8},{5,1},{9,5},{13,9},{6,2},{10,6},{14,10},{7,3},{... | collective-permute-start | bytes 1769480 | tf_op jit(solution)/shard_map/ppermute | solution.py:28
  69.4 17.0 %collective-permute-start.31 = (bf16[6,2,128,128]{3,2,1,0:T(8,128)(2,1)S(1)}, bf16[6,2,128,128]{3,2,1,0:T(8,128)(2,1)S(1)}, u32[]{:S(2)}, u32[]{:S(2)}) collective-permute-start(bf16[6,2,128,128]{3,2,1,0:T(8,128)(2,1)S(1)} %collective-permute-done.21.refs_22_), channel_id=1, source_target_pairs={{1,0},{5,4},{9,8},{13,12},{17,16},{21,20},{25,24},{29,28}} | collective-permute-start | bytes 1179656 | tf_op jit(solution)/shard_map/ppermute | solution.py:170
  71.5 22.1 %collective-permute-start.30 = (bf16[6,2,128,128]{3,2,1,0:T(8,128)(2,1)S(1)}, bf16[6,2,128,128]{3,2,1,0:T(8,128)(2,1)S(1)}, u32[]{:S(2)}, u32[]{:S(2)}) collective-permute-start(bf16[6,2,128,128]{3,2,1,0:T(8,128)(2,1)S(1)} %collective-permute-done.20.refs_21_), channel_id=1, source_target_pairs={{2,3},{6,7},{10,11},{14,15},{18,19},{22,23},{26,27},{30,31}} | collective-permute-start | bytes 1179656 | tf_op jit(solution)/shard_map/ppermute | solution.py:169
  76.4 21.1 %collective-permute-start.17 = (bf16[9,2,128,128]{3,2,1,0:T(8,128)(2,1)}, bf16[9,2,128,128]{3,2,1,0:T(8,128)(2,1)S(1)}, u32[]{:S(2)}, u32[]{:S(2)}) collective-permute-start(bf16[9,2,128,128]{3,2,1,0:T(8,128)(2,1)} %copy-done.14), channel_id=1, source_target_pairs={{1,0},{2,1},{5,4},{6,5},{9,8},{10,9},{13,12},{14,13},{17,16},{18,1... | collective-permute-start | bytes 1769480 | tf_op jit(solution)/shard_map/ppermute | solution.py:170
  77.7 25.4 %collective-permute-start.9 = (bf16[9,2,128,128]{3,2,1,0:T(8,128)(2,1)}, bf16[9,2,128,128]{3,2,1,0:T(8,128)(2,1)S(1)}, u32[]{:S(2)}, u32[]{:S(2)}) collective-permute-start(bf16[9,2,128,128]{3,2,1,0:T(8,128)(2,1)} %copy-done.14), channel_id=1, source_target_pairs={{0,4},{4,8},{8,12},{1,5},{5,9},{9,13},{2,6},{6,10},{10,14},{3,7},{... | collective-permute-start | bytes 1769480 | tf_op jit(solution)/shard_map/ppermute | solution.py:28
  85.7 19.0 %collective-permute-start.16 = (bf16[9,2,128,128]{3,2,1,0:T(8,128)(2,1)}, bf16[9,2,128,128]{3,2,1,0:T(8,128)(2,1)S(1)}, u32[]{:S(2)}, u32[]{:S(2)}) collective-permute-start(bf16[9,2,128,128]{3,2,1,0:T(8,128)(2,1)} %collective-permute-done.6.refs_7_), channel_id=1, source_target_pairs={{1,2},{2,3},{5,6},{6,7},{9,10},{10,11},{13,14},{14,15},{17,18},{18... | collective-permute-start | bytes 1769480 | tf_op jit(solution)/shard_map/ppermute | solution.py:169
  87.2 19.5 %collective-permute-start.8 = (bf16[9,2,128,128]{3,2,1,0:T(8,128)(2,1)}, bf16[9,2,128,128]{3,2,1,0:T(8,128)(2,1)S(1)}, u32[]{:S(2)}, u32[]{:S(2)}) collective-permute-start(bf16[9,2,128,128]{3,2,1,0:T(8,128)(2,1)} %collective-permute-done.6.refs_7_), channel_id=1, source_target_pairs={{0,4},{4,8},{8,12},{1,5},{5,9},{9,13},{2,6},{6,10},{10,14},{3,7},{... | collective-permute-start | bytes 1769480 | tf_op jit(solution)/shard_map/ppermute | solution.py:28
  94.3 17.3 %collective-permute-start.13 = (bf16[9,2,128,128]{3,2,1,0:T(8,128)(2,1)S(1)}, bf16[9,2,128,128]{3,2,1,0:T(8,128)(2,1)S(1)}, u32[]{:S(2)}, u32[]{:S(2)}) collective-permute-start(bf16[9,2,128,128]{3,2,1,0:T(8,128)(2,1)S(1)} %collective-permute-done.3.refs_4_), channel_id=1, source_target_pairs={{1,0},{2,1},{5,4},{6,5},{9,8},{10,9},{13,12},{14,13},{17,16},{18,1... | collective-permute-start | bytes 1769480 | tf_op jit(solution)/shard_map/ppermute | solution.py:170
  97.5 23.0 %copy-start.15 = (bf16[9,2,128,128]{3,2,1,0:T(8,128)(2,1)}, bf16[9,2,128,128]{3,2,1,0:T(8,128)(2,1)S(1)}, u32[]{:S(2)}) copy-start(bf16[9,2,128,128]{3,2,1,0:T(8,128)(2,1)S(1)} %collective-permute-done.17.refs_18_) | copy-start | bytes 1769476
  97.5 19.5 %collective-permute-start.5 = (bf16[9,2,128,128]{3,2,1,0:T(8,128)(2,1)S(1)}, bf16[9,2,128,128]{3,2,1,0:T(8,128)(2,1)S(1)}, u32[]{:S(2)}, u32[]{:S(2)}) collective-permute-start(bf16[9,2,128,128]{3,2,1,0:T(8,128)(2,1)S(1)} %collective-permute-done.3.refs_4_), channel_id=1, source_target_pairs={{4,0},{8,4},{12,8},{5,1},{9,5},{13,9},{6,2},{10,6},{14,10},{7,3},{... | collective-permute-start | bytes 1769480 | tf_op jit(solution)/shard_map/ppermute | solution.py:28
  103.2 24.5 %copy-start.16 = (bf16[9,2,128,128]{3,2,1,0:T(8,128)(2,1)}, bf16[9,2,128,128]{3,2,1,0:T(8,128)(2,1)S(1)}, u32[]{:S(2)}) copy-start(bf16[9,2,128,128]{3,2,1,0:T(8,128)(2,1)S(1)} %collective-permute-done.9.refs_10_) | copy-start | bytes 1769476
  103.2 15.3 %collective-permute-start.12 = (bf16[9,2,128,128]{3,2,1,0:T(8,128)(2,1)S(1)}, bf16[9,2,128,128]{3,2,1,0:T(8,128)(2,1)}, u32[]{:S(2)}, u32[]{:S(2)}) collective-permute-start(bf16[9,2,128,128]{3,2,1,0:T(8,128)(2,1)S(1)} %collective-permute-done.2.refs_3_), channel_id=1, source_target_pairs={{1,2},{2,3},{5,6},{6,7},{9,10},{10,11},{13,14},{14,15},{17,18},{18... | collective-permute-start | bytes 1769480 | tf_op jit(solution)/shard_map/ppermute | solution.py:169
  104.7 24.5 %copy-start.17 = (bf16[9,2,128,128]{3,2,1,0:T(8,128)(2,1)}, bf16[9,2,128,128]{3,2,1,0:T(8,128)(2,1)S(1)}, u32[]{:S(2)}) copy-start(bf16[9,2,128,128]{3,2,1,0:T(8,128)(2,1)S(1)} %collective-permute-done.16.refs_17_) | copy-start | bytes 1769476
  104.7 15.8 %collective-permute-start.4 = (bf16[9,2,128,128]{3,2,1,0:T(8,128)(2,1)S(1)}, bf16[9,2,128,128]{3,2,1,0:T(8,128)(2,1)S(1)}, u32[]{:S(2)}, u32[]{:S(2)}) collective-permute-start(bf16[9,2,128,128]{3,2,1,0:T(8,128)(2,1)S(1)} %collective-permute-done.2.refs_3_), channel_id=1, source_target_pairs={{4,0},{8,4},{12,8},{5,1},{9,5},{13,9},{6,2},{10,6},{14,10},{7,3},{... | collective-permute-start | bytes 1769480 | tf_op jit(solution)/shard_map/ppermute | solution.py:28
  106.6 26.4 %copy-start.18 = (bf16[9,2,128,128]{3,2,1,0:T(8,128)(2,1)}, bf16[9,2,128,128]{3,2,1,0:T(8,128)(2,1)S(1)}, u32[]{:S(2)}) copy-start(bf16[9,2,128,128]{3,2,1,0:T(8,128)(2,1)S(1)} %collective-permute-done.8.refs_9_) | copy-start | bytes 1769476
  106.6 17.7 %collective-permute-start.27 = (bf16[9,2,128,128]{3,2,1,0:T(8,128)(2,1)S(1)}, bf16[9,2,128,128]{3,2,1,0:T(8,128)(2,1)}, u32[]{:S(2)}, u32[]{:S(2)}) collective-permute-start(bf16[9,2,128,128]{3,2,1,0:T(8,128)(2,1)S(1)} %collective-permute-done.17.refs_18_), channel_id=1, source_target_pairs={{1,0},{5,4},{9,8},{13,12},{17,16},{21,20},{25,24},{29,28}} | collective-permute-start | bytes 1769480 | tf_op jit(solution)/shard_map/ppermute | solution.py:170
  111.6 25.1 %copy-start.19 = (bf16[9,2,128,128]{3,2,1,0:T(8,128)(2,1)}, bf16[9,2,128,128]{3,2,1,0:T(8,128)(2,1)S(1)}, u32[]{:S(2)}) copy-start(bf16[9,2,128,128]{3,2,1,0:T(8,128)(2,1)S(1)} %collective-permute-done.13.refs_14_) | copy-start | bytes 1769476
  111.6 16.1 %collective-permute-start.19 = (bf16[9,2,128,128]{3,2,1,0:T(8,128)(2,1)S(1)}, bf16[9,2,128,128]{3,2,1,0:T(8,128)(2,1)S(1)}, u32[]{:S(2)}, u32[]{:S(2)}) collective-permute-start(bf16[9,2,128,128]{3,2,1,0:T(8,128)(2,1)S(1)} %collective-permute-done.17.refs_18_), channel_id=1, source_target_pairs={{0,4},{4,8},{8,12},{1,5},{5,9},{9,13},{2,6},{6,10},{10,14},{3,7},{... | collective-permute-start | bytes 1769480 | tf_op jit(solution)/shard_map/ppermute | solution.py:28
  117.0 14.1 %collective-permute-start.26 = (bf16[9,2,128,128]{3,2,1,0:T(8,128)(2,1)S(1)}, bf16[9,2,128,128]{3,2,1,0:T(8,128)(2,1)}, u32[]{:S(2)}, u32[]{:S(2)}) collective-permute-start(bf16[9,2,128,128]{3,2,1,0:T(8,128)(2,1)S(1)} %collective-permute-done.16.refs_17_), channel_id=1, source_target_pairs={{2,3},{6,7},{10,11},{14,15},{18,19},{22,23},{26,27},{30,31}} | collective-permute-start | bytes 1769480 | tf_op jit(solution)/shard_map/ppermute | solution.py:169
  118.5 14.5 %collective-permute-start.18 = (bf16[9,2,128,128]{3,2,1,0:T(8,128)(2,1)S(1)}, bf16[9,2,128,128]{3,2,1,0:T(8,128)(2,1)S(1)}, u32[]{:S(2)}, u32[]{:S(2)}) collective-permute-start(bf16[9,2,128,128]{3,2,1,0:T(8,128)(2,1)S(1)} %collective-permute-done.16.refs_17_), channel_id=1, source_target_pairs={{0,4},{4,8},{8,12},{1,5},{5,9},{9,13},{2,6},{6,10},{10,14},{3,7},{... | collective-permute-start | bytes 1769480 | tf_op jit(solution)/shard_map/ppermute | solution.py:28
  120.5 16.6 %collective-permute-start.23 = (bf16[9,2,128,128]{3,2,1,0:T(8,128)(2,1)S(1)}, bf16[9,2,128,128]{3,2,1,0:T(8,128)(2,1)}, u32[]{:S(2)}, u32[]{:S(2)}) collective-permute-start(bf16[9,2,128,128]{3,2,1,0:T(8,128)(2,1)S(1)} %collective-permute-done.13.refs_14_), channel_id=1, source_target_pairs={{1,0},{5,4},{9,8},{13,12},{17,16},{21,20},{25,24},{29,28}} | collective-permute-start | bytes 1769480 | tf_op jit(solution)/shard_map/ppermute | solution.py:170
  124.3 16.9 %collective-permute-start.15 = (bf16[9,2,128,128]{3,2,1,0:T(8,128)(2,1)S(1)}, bf16[9,2,128,128]{3,2,1,0:T(8,128)(2,1)S(1)}, u32[]{:S(2)}, u32[]{:S(2)}) collective-permute-start(bf16[9,2,128,128]{3,2,1,0:T(8,128)(2,1)S(1)} %collective-permute-done.13.refs_14_), channel_id=1, source_target_pairs={{4,0},{8,4},{12,8},{5,1},{9,5},{13,9},{6,2},{10,6},{14,10},{7,3},{... | collective-permute-start | bytes 1769480 | tf_op jit(solution)/shard_map/ppermute | solution.py:28
  127.7 13.6 %copy-start.20 = (bf16[9,2,128,128]{3,2,1,0:T(8,128)(2,1)}, bf16[9,2,128,128]{3,2,1,0:T(8,128)(2,1)S(1)}, u32[]{:S(2)}) copy-start(bf16[9,2,128,128]{3,2,1,0:T(8,128)(2,1)S(1)} %collective-permute-done.19.refs_20_) | copy-start | bytes 1769476
  127.7 15.5 %collective-permute-start.22 = (bf16[9,2,128,128]{3,2,1,0:T(8,128)(2,1)}, bf16[9,2,128,128]{3,2,1,0:T(8,128)(2,1)}, u32[]{:S(2)}, u32[]{:S(2)}) collective-permute-start(bf16[9,2,128,128]{3,2,1,0:T(8,128)(2,1)} %collective-permute-done.12.refs_13_), channel_id=1, source_target_pairs={{2,3},{6,7},{10,11},{14,15},{18,19},{22,23},{26,27},{30,31}} | collective-permute-start | bytes 1769480 | tf_op jit(solution)/shard_map/ppermute | solution.py:169
  131.1 59.8 %collective-permute-start.14 = (bf16[9,2,128,128]{3,2,1,0:T(8,128)(2,1)}, bf16[9,2,128,128]{3,2,1,0:T(8,128)(2,1)}, u32[]{:S(2)}, u32[]{:S(2)}) collective-permute-start(bf16[9,2,128,128]{3,2,1,0:T(8,128)(2,1)} %collective-permute-done.12.refs_13_), channel_id=1, source_target_pairs={{4,0},{8,4},{12,8},{5,1},{9,5},{13,9},{6,2},{10,6},{14,10},{7,3},{... | collective-permute-start | bytes 1769480 | tf_op jit(solution)/shard_map/ppermute | solution.py:28
  133.0 10.2 %copy-start.21 = (bf16[9,2,128,128]{3,2,1,0:T(8,128)(2,1)}, bf16[9,2,128,128]{3,2,1,0:T(8,128)(2,1)S(1)}, u32[]{:S(2)}) copy-start(bf16[9,2,128,128]{3,2,1,0:T(8,128)(2,1)S(1)} %collective-permute-done.18.refs_19_) | copy-start | bytes 1769476
  133.0 57.8 %collective-permute-start.29 = (bf16[9,2,128,128]{3,2,1,0:T(8,128)(2,1)}, bf16[9,2,128,128]{3,2,1,0:T(8,128)(2,1)}, u32[]{:S(2)}, u32[]{:S(2)}) collective-permute-start(bf16[9,2,128,128]{3,2,1,0:T(8,128)(2,1)} %collective-permute-done.27.refs_28_), channel_id=1, source_target_pairs={{0,4},{4,8},{8,12},{1,5},{5,9},{9,13},{2,6},{6,10},{10,14},{3,7},{... | collective-permute-start | bytes 1769480 | tf_op jit(solution)/shard_map/ppermute | solution.py:28
  137.1 53.8 %collective-permute-start.28 = (bf16[9,2,128,128]{3,2,1,0:T(8,128)(2,1)}, bf16[9,2,128,128]{3,2,1,0:T(8,128)(2,1)}, u32[]{:S(2)}, u32[]{:S(2)}) collective-permute-start(bf16[9,2,128,128]{3,2,1,0:T(8,128)(2,1)} %collective-permute-done.26.refs_27_), channel_id=1, source_target_pairs={{0,4},{4,8},{8,12},{1,5},{5,9},{9,13},{2,6},{6,10},{10,14},{3,7},{... | collective-permute-start | bytes 1769480 | tf_op jit(solution)/shard_map/ppermute | solution.py:28
  141.2 2.0 copy-start.22
  141.3 49.6 %collective-permute-start.25 = (bf16[9,2,128,128]{3,2,1,0:T(8,128)(2,1)}, bf16[9,2,128,128]{3,2,1,0:T(8,128)(2,1)}, u32[]{:S(2)}, u32[]{:S(2)}) collective-permute-start(bf16[9,2,128,128]{3,2,1,0:T(8,128)(2,1)} %collective-permute-done.23.refs_24_), channel_id=1, source_target_pairs={{4,0},{8,4},{12,8},{5,1},{9,5},{13,9},{6,2},{10,6},{14,10},{7,3},{... | collective-permute-start | bytes 1769480 | tf_op jit(solution)/shard_map/ppermute | solution.py:28
  143.2 47.6 %collective-permute-start.24 = (bf16[9,2,128,128]{3,2,1,0:T(8,128)(2,1)}, bf16[9,2,128,128]{3,2,1,0:T(8,128)(2,1)}, u32[]{:S(2)}, u32[]{:S(2)}) collective-permute-start(bf16[9,2,128,128]{3,2,1,0:T(8,128)(2,1)} %collective-permute-done.22.refs_23_), channel_id=1, source_target_pairs={{4,0},{8,4},{12,8},{5,1},{9,5},{13,9},{6,2},{10,6},{14,10},{7,3},{... | collective-permute-start | bytes 1769480 | tf_op jit(solution)/shard_map/ppermute | solution.py:28
  190.9 1.0 copy-start.1
  191.9 1.0 copy-start.3
  192.9 1.0 copy-start.5
  193.9 1.0 copy-start.7
  194.9 1.0 copy-start.9
  195.9 1.0 copy-start.11
  (8 other events, 5.9 us)

commit v2 on v0

v2 whole, which is shorter than its diff:
```python
import functools

import jax
import jax.numpy as jnp
from jax import lax
from jax.experimental import pallas as pl
from jax.experimental.pallas import tpu as pltpu
from jax.sharding import PartitionSpec as P

W = 10
LEAD = W - 1
SPAN = 2 * W - 1
WIDE = 4 * W
UNROLL = 16
BITS = 10
MASK = (1 << BITS) - 1
OUT_MASK = 127
STAGE_BIT = 27
STAGES = 5
ABSENT = 7
CHUNKS = 4
TABLE = 1024
WEIGHTS = {0: 1, 1: 1, 2: 1, 3: 1 << 33, 4: 1}
LIST_WEIGHT = 1

SMEM = pl.BlockSpec(memory_space=pltpu.SMEM)
VMEM = pl.BlockSpec(memory_space=pltpu.VMEM)
HBM = pl.BlockSpec(memory_space=pltpu.HBM)
ANY = pl.BlockSpec(memory_space=pl.ANY)
SMALL = pltpu.CompilerParams(vmem_limit_bytes=1 << 20)


def stage_of(step, last, edge):
    if step == last and step > 1:
        return 2 + edge
    if edge == 2:
        return 0 if step == 0 else 1
    return 0 if step <= 1 else 1


def quick(weight):
    return pl.CostEstimate(flops=weight, bytes_accessed=weight, transcendentals=0)


def up_pairs(size, step):
    return [(i, i + 1) for i in range(step - 1, size - 1)]


def down_pairs(size, step):
    return [(i + 1, i) for i in range(size - step)]


def row_shift(array, by):
    size = lax.axis_size("rows")
    return lax.ppermute(array, "rows", [(i, i + by) for i in range(size) if 0 <= i + by < size])


def segment_size(part_rows, slot_count):
    most = part_rows * (slot_count * (SPAN + 1) - slot_count * (slot_count - 1) // 2) + 4 * UNROLL
    return -(-most // 256) * 256


def list_kernel(
    row_count,
    own,
    slot_count,
    size,
    total_rows,
    place_ref,
    wanted_ref,
    columns_hbm,
    terms_ref,
    count_ref,
    table_ref,
    at_ref,
    columns_ref,
    sem,
):
    me, first = place_ref[0], place_ref[1]
    slots = size * own
    ext = row_count + 2 * LEAD
    stored = ext * slots
    zero_id = 2 * stored
    part = row_count // CHUNKS
    segment = segment_size(part, slot_count)
    junk = STAGES * CHUNKS * segment
    zero_term = zero_id | (zero_id << BITS)
    spare = WIDE - 1
    absent = ABSENT << STAGE_BIT
    here = first // row_count
    holders = total_rows // row_count

    def fetch(go):
        for near in range(3):
            holder = jnp.clip(here + near - 1, 0, holders - 1)
            source = pl.ds(pl.multiple_of(holder * size * TABLE, TABLE), size * TABLE)
            go(pltpu.make_async_copy(columns_hbm.at[source], columns_ref.at[pl.ds(near * size * TABLE, size * TABLE)], sem))

    fetch(lambda c: c.start())

    def clear(e, _):
        for c in range(WIDE - 1):
            table_ref[e * WIDE + c] = absent
        return 0

    lax.fori_loop(0, ext, clear, 0)

    stages = []
    for k in range(size):
        distance = jnp.abs(k - me)
        picks = []
        for edge in range(3):
            stage = jnp.int32(0)
            for step in range(size):
                stage = jnp.where(distance == step, stage_of(step, size - 1, edge), stage)
            picks.append(stage << STAGE_BIT)
        stages.append(picks)
    fetch(lambda c: c.wait())

    def enter(e, row_id, near, local, stage):
        line = e * WIDE + LEAD
        for k in range(size):
            for s in range(own):
                column = columns_ref[local + ((near * size + k) * TABLE + s * row_count)]
                reach = column - row_id
                good = (column >= 0) & (reach >= 0) & (reach < W)
                code = (e * slots + (k * own + s)) + stage(k)
                table_ref[jnp.where(good, line + reach, spare)] = code
                low = good & (reach > 0) & (e + reach < ext)
                table_ref[jnp.where(low, line + reach * (WIDE - 1), spare)] = code + stored

    @pl.when(first > 0)
    def _():
        def enter_before(r, _):
            at = row_count - LEAD + r
            enter(r, first - LEAD + r, 0, at, lambda k: stages[k][2])
            return 0

        lax.fori_loop(0, LEAD, enter_before, 0)

    def enter_own(r, _):
        edge = (r < LEAD) | (r >= row_count - LEAD)
        enter(r + LEAD, first + r, 1, r, lambda k: jnp.where(edge, stages[k][0], stages[k][1]))
        return 0

    lax.fori_loop(0, row_count, enter_own, 0)

    @pl.when(first + row_count < total_rows)
    def _():
        def enter_after(r, _):
            enter(LEAD + row_count + r, first + row_count + r, 2, r, lambda k: stages[k][2])
            return 0

        lax.fori_loop(0, LEAD, enter_after, 0)

    table_ref[spare] = absent

    lanes = range(CHUNKS)
    lines = ABSENT + 1
    for chunk in lanes:
        for stage in range(STAGES):
            at_ref[chunk * lines + stage] = (stage * CHUNKS + chunk) * segment

    def per_output(number, _):
        local = number // slot_count
        slot = number - local * slot_count
        rows = [chunk * part + local for chunk in lanes]
        wants = [wanted_ref[slot, row] for row in rows]
        distances = [jnp.where(want >= 0, want - first - row, SPAN) for want, row in zip(wants, rows)]
        tags = [(row * slot_count + slot) << (2 * BITS) for row in rows]
        bases = [(row + LEAD) * WIDE + LEAD for row in rows]
        rights_at = [base + d for base, d in zip(bases, distances)]
        for chunk in lanes:
            at_ref[chunk * lines + ABSENT] = junk
        for step in range(-LEAD, W):
            lefts = [table_ref[base + (max(step, 0) * WIDE + step)] for base in bases]
            rights = [table_ref[at + step * (WIDE - 1)] for at in rights_at]
            spots = [
                (jnp.maximum(left, right) >> STAGE_BIT) + chunk * lines
                for chunk, left, right in zip(lanes, lefts, rights)
            ]
            places = [at_ref[spot] for spot in spots]
            for chunk in lanes:
                terms_ref[places[chunk]] = lefts[chunk] + (rights[chunk] << BITS) + tags[chunk]
            for chunk in lanes:
                at_ref[spots[chunk]] = places[chunk] + 1
        for chunk in lanes:
            places = [at_ref[chunk * lines + stage] for stage in range(STAGES)]
            for stage in range(STAGES):
                terms_ref[places[stage]] = zero_term + tags[chunk]
                at_ref[chunk * lines + stage] = places[stage] + (places[stage] & 1)
        return 0

    lax.fori_loop(0, part * slot_count, per_output, 0)

    for stage in range(STAGES):
        for chunk in lanes:
            at = at_ref[chunk * lines + stage]
            tag = (chunk * part * slot_count) << (2 * BITS)
            for extra in range(2 * UNROLL):
                terms_ref[at + extra] = zero_term + tag
            used = at - (stage * CHUNKS + chunk) * segment
            count_ref[stage * CHUNKS + chunk] = (used + 2 * UNROLL - 1) // (2 * UNROLL)


def stage_kernel(stage, plan, ext, size, own, segment, place_ref, *refs):
    count = len(plan)
    first, final = stage == 0, stage == STAGES - 1
    count_ref, terms_hbm = refs[:2]
    pieces = refs[2 : count + 2]
    blocks, sums, out_ref, sem, terms_ref, list_sem = refs[count + (2 if first else 4) :]
    if not final:
        out_ref[0] = 0
    slots = size * own
    stored = ext * slots
    me = place_ref[0]

    def each(go):
        for piece, (source, rows, target, shift) in zip(pieces, plan):
            owner = me + (shift if not isinstance(shift, tuple) else jnp.where(me >= shift[0], -shift[0], shift[0]))

            @pl.when((owner >= 0) & (owner < size))
            def _(piece=piece, source=source, rows=rows, target=target, owner=owner):
                go(piece, source, rows, target, owner)

    shelf = blocks.reshape(blocks.shape[0] // slots, slots, *blocks.shape[1:])

    def copy(piece, source, rows, target, owner):
        return pltpu.make_async_copy(
            piece.at[pl.ds(source, rows)], shelf.at[pl.ds(target, rows), pl.ds(owner * own, own)], sem
        )

    def turn(piece, source, rows, target, owner):
        pace = max(n for n in range(1, 10) if rows % n == 0)

        def some(group, _):
            base = (target + group * pace) * slots + owner * own
            for r in range(pace):
                for s in range(own):
                    at = base + r * slots + s
                    blocks[stored + at] = blocks[at].T
            return 0

        lax.fori_loop(0, rows // pace, some, 0)

        def mirror(group, _):
            spots = [(target + group * 3 + r) * slots for r in range(3)]
            found = []
            for at in spots:
                tile, turned = blocks[at], blocks[stored + at]
                a = lax.broadcasted_iota(jnp.int32, tile.shape, 0)
                b = lax.broadcasted_iota(jnp.int32, tile.shape, 1)
                found.append(jnp.where(a <= b, tile, turned))
            for at, whole in zip(spots, found):
                blocks[at] = whole
                blocks[stored + at] = whole
            return 0

        @pl.when(owner == 0)
        def _():
            lax.fori_loop(0, rows // 3, mirror, 0)

    listing = pltpu.make_async_copy(
        terms_hbm.at[pl.ds(stage * CHUNKS * segment, CHUNKS * segment)], terms_ref, list_sem
    )
    listing.start()
    each(lambda *what: copy(*what).start())
    if first:
        blocks[2 * stored] = jnp.zeros(blocks.shape[1:], blocks.dtype)
        sums[...] = jnp.zeros_like(sums)
    each(lambda *what: copy(*what).wait())
    each(turn)
    listing.wait()

    part = sums.shape[0] // CHUNKS
    for chunk in range(CHUNKS):

        def multiply(group, _):
            found = []
            for u in range(UNROLL):
                at = chunk * segment + (group * UNROLL + u) * 2
                one, two = terms_ref[at], terms_ref[at + 1]
                lhs = jnp.concatenate([blocks[one & MASK], blocks[two & MASK]], axis=1)
                rhs = jnp.concatenate([blocks[(one >> BITS) & MASK], blocks[(two >> BITS) & MASK]], axis=0)
                found.append(((one >> (2 * BITS)) & OUT_MASK, jnp.dot(lhs, rhs, preferred_element_type=jnp.float32)))
            for at, value in found:
                sums[at] += value
            return 0

        lax.fori_loop(0, count_ref[stage * CHUNKS + chunk], multiply, 0)
        if final:
            span = pl.ds(chunk * part, part)
            pltpu.make_async_copy(sums.at[span], out_ref.at[span], sem).start()
    if final:
        pltpu.make_async_copy(sums, out_ref, sem).wait()


def after_all(arrays, tokens):
    count = len(arrays)
    return list(pl.pallas_call(
        lambda *refs: None,
        out_shape=[jax.ShapeDtypeStruct(a.shape, a.dtype) for a in arrays],
        in_specs=[ANY] * (count + len(tokens)),
        out_specs=[ANY] * count,
        input_output_aliases={n: n for n in range(count)},
        compiler_params=SMALL,
        cost_estimate=quick(1),
        name="after_all",
    )(*arrays, *tokens))


def rows_of(arrays, place, step, tokens, spans):
    both = step == 0 and len(arrays) == 2
    shape = arrays[0].shape[1:]

    def kernel(place_ref, *refs):
        given, given_out, sem = refs[: len(arrays)], refs[len(arrays) + len(tokens) : -1], refs[-1]

        def copies(go):
            for target, (start, stop) in zip(given_out, spans):
                rows = stop - start
                if both or len(given) == 1:
                    for n, source in enumerate(given):
                        go(pltpu.make_async_copy(source.at[pl.ds(start, rows)], target.at[pl.ds(n * rows, rows)], sem))
                    continue
                for wanted, source in ((place_ref[0] >= step, given[0]), (place_ref[0] < step, given[1])):

                    @pl.when(wanted)
                    def _(source=source, target=target, start=start, rows=rows):
                        go(pltpu.make_async_copy(source.at[pl.ds(start, rows)], target, sem))

        copies(lambda c: c.start())
        copies(lambda c: c.wait())

    return list(pl.pallas_call(
        kernel,
        out_shape=[
            jax.ShapeDtypeStruct(((2 if both else 1) * (stop - start), *shape), arrays[0].dtype)
            for start, stop in spans
        ],
        in_specs=[SMEM] + [ANY] * (len(arrays) + len(tokens)),
        out_specs=[ANY] * len(spans),
        scratch_shapes=[pltpu.SemaphoreType.DMA],
        compiler_params=SMALL,
        cost_estimate=quick(1),
        name="rows_of",
    )(place, *arrays, *tokens))


def body(block_values, block_columns, product_columns):
    row_count, own, tile, _ = block_values.shape
    dtype = block_values.dtype
    size = lax.axis_size("cols")
    last = size - 1
    slots = size * own
    wanted_slots = product_columns.shape[1]
    ext = row_count + 2 * LEAD
    out_count = row_count * wanted_slots
    segment = segment_size(row_count // CHUNKS, wanted_slots)
    first_row = lax.axis_index("rows") * row_count
    me = lax.axis_index("cols")

    plans = {stage: [] for stage in range(STAGES)}
    pieces = {stage: [] for stage in range(STAGES)}

    def keep(stage, array, source, rows, target, shift):
        plans[stage].append((source, rows, target, shift))
        pieces[stage].append(array)

    def trade(array_low, array_high, shifts, step):
        stage = stage_of(step, last, 2)
        after, before = row_shift(array_low, -1), row_shift(array_high, 1)
        for n, shift in enumerate(shifts):
            keep(stage, after, n * LEAD, LEAD, LEAD + row_count, shift)
            keep(stage, before, n * LEAD, LEAD, 0, shift)

    edges = [(0, LEAD), (row_count - LEAD, row_count)]
    middle = (LEAD, row_count - LEAD)

    place = jnp.stack([me, first_row])
    lists = []
    state = []

    def run(stage):
        count = len(pieces[stage])
        final = stage == STAGES - 1
        given = state[:-1]
        state[:] = pl.pallas_call(
            functools.partial(stage_kernel, stage, tuple(plans[stage]), ext, size, own, segment),
            out_shape=[
                pltpu.VMEM(((2 * ext + 1) * slots, tile, tile), dtype),
                pltpu.VMEM((out_count, tile, tile), jnp.float32),
                jax.ShapeDtypeStruct((out_count, tile, tile), jnp.float32)
                if final
                else jax.ShapeDtypeStruct((1,), jnp.int32),
            ],
            in_specs=[SMEM, SMEM, HBM] + [HBM] * count + [VMEM] * len(given),
            out_specs=[VMEM, VMEM, HBM if final else SMEM],
            input_output_aliases={3 + count + n: n for n in range(len(given))},
            scratch_shapes=[
                pltpu.SemaphoreType.DMA,
                pltpu.SMEM((CHUNKS * segment,), jnp.int32),
                pltpu.SemaphoreType.DMA,
            ],
            compiler_params=pltpu.CompilerParams(vmem_limit_bytes=4 << 20),
            cost_estimate=quick(WEIGHTS[stage]),
            name=f"stage_{stage}",
        )(place, *lists, *pieces[stage], *given)
        return state[-1]

    moving = [block_values, block_values]
    for step in range(1, size):
        ups, downs = up_pairs(size, step), down_pairs(size, step)
        if step == last and step > 1:
            arrived = [lax.ppermute(array, "cols", ups + downs) for array in parts]
            arrived[:2] = after_all(arrived[:2], [state[-1]])
            for array, (start, stop), edge in zip(arrived, [*edges, middle], (0, 0, 1)):
                keep(stage_of(step, last, edge), array, 0, stop - start, LEAD + start, (step,))
            trade(arrived[0], arrived[1], ((step,),), step)
            break
        if len(moving) == 2:
            moving = [lax.ppermute(array, "cols", pairs) for array, pairs in zip(moving, (ups, downs))]
        else:
            moving = [lax.ppermute(moving[0], "cols", ups + downs)]
        if step == 1:
            keep(0, block_values, 0, row_count, LEAD, 0)
            devices = size * lax.axis_size("rows")
            spread = jnp.pad(block_columns.T.reshape(-1), (0, TABLE - own * row_count))
            spread = jnp.broadcast_to(spread.reshape(1, 8, TABLE // 8), (devices, 8, TABLE // 8))
            tables = lax.all_to_all(spread, ("rows", "cols"), 0, 0, tiled=True).reshape(-1)
            trade(*rows_of([block_values], place, 0, [], edges), (0,), 0)
            moving = after_all(moving, [tables, *pieces[0][1:]])
            terms, counts = pl.pallas_call(
                functools.partial(
                    list_kernel, row_count, own, wanted_slots, size, row_count * lax.axis_size("rows")
                ),
                out_shape=[
                    jax.ShapeDtypeStruct(((STAGES * CHUNKS + 2) * segment,), jnp.int32),
                    jax.ShapeDtypeStruct((STAGES * CHUNKS,), jnp.int32),
                ],
                in_specs=[SMEM, SMEM, HBM],
                out_specs=[SMEM] * 2,
                scratch_shapes=[
                    pltpu.SMEM((ext * WIDE,), jnp.int32),
                    pltpu.SMEM(((ABSENT + 1) * CHUNKS,), jnp.int32),
                    pltpu.SMEM((3 * size * TABLE,), jnp.int32),
                    pltpu.SemaphoreType.DMA,
                ],
                compiler_params=SMALL,
                cost_estimate=quick(LIST_WEIGHT),
                name="lists",
            )(place, product_columns.T, tables)
            lists = [counts, terms]
        elif len(moving) == 2 and 2 * step > last:
            pass
        else:
            moving = after_all(moving, [])
        stage = stage_of(step, last, 0)
        shifts = (-step, step) if len(moving) == 2 else ((step,),)
        for array, shift in zip(moving, shifts):
            keep(stage, array, 0, row_count, LEAD, shift)
        if step + 1 == last:
            parts = rows_of(moving, place, step, [counts], [*edges, middle])
            trade(parts[0], parts[1], ((step,),), step)
            run(0)
            run(1)
        elif 2 * step > last:
            if len(moving) == 2:
                moving = rows_of(moving, place, step, [], [(0, row_count)])
            trade(*rows_of(moving, place, step, [], edges), ((step,),), step)
        else:
            trade(*rows_of(moving, place, 0, [], edges), (-step, step), step)
    for stage in range(2, STAGES):
        run(stage)
    return state[-1].reshape(row_count, wanted_slots, tile, tile)


def solution(mesh):
    placed = (
        P(("groups", "rows"), "cols", None, None),
        P(("groups", "rows"), "cols"),
        P(("groups", "rows"), "cols"),
    )
    return jax.shard_map(
        body,
        mesh=mesh,
        in_specs=placed,
        out_specs=P(("groups", "rows"), "cols", None, None),
        check_vma=False,
    )
```

time: 526 us -> 142 us (0.27)
  local copies, waits for them, and re-layouts: 222 us -> 2.19 us
  waiting for transfers between devices: 167 us -> 21.4 us
  matrix products: 66.4 us -> 0 us
  Pallas kernels: 0 us -> 55.5 us
  other arithmetic: 37.7 us -> 0.08 us
  starting transfers between devices: 5.72 us -> 35.1 us
  blocking collectives: 10.2 us -> 26.8 us
  between operations: 13.6 us -> 0.47 us
    gather x13 -> x0, local copies, waits for them, and re-layouts: 203 us -> none  [the longest x8 150 us: block_product(): picked = band_tiles[source_rows, source_cols]]
    all_gather x1 -> x0, waiting for transfers between devices: 109 us -> none  [body(): lax.all_gather(block_values, 'cols', axis=1, tiled=True)]
    dot_general x4 -> x0, matrix products: 66.4 us -> none  [block_product(): jnp.einsum('krab,krbc->rac', left_stack, right_stack, preferred_element_t...]
    pallas_call x0 -> x11, Pallas kernels: none -> 55.5 us  [the longest x5 32 us: run(): pl.pallas_call(functools.partial(stage_kernel, stage, tuple(plans[stage])...]
    ppermute x2 -> x15, waiting for transfers between devices: 57.4 us -> 21.4 us  [the longest x4 13.3 us: body(): lax.ppermute(array, 'cols', pairs)]
    ppermute x2 -> x15, starting transfers between devices: 5.72 us -> 35.1 us  [the longest x8 23 us: row_shift(): lax.ppermute(array, 'rows', [(i, i + by) for i in range(size) if 0 <= i +...]
    all_to_all x0 -> x1, blocking collectives: none -> 26.8 us  [body(): lax.all_to_all(spread, ('rows', 'cols'), 0, 0, tiled=True).reshape(-1)]
    select_n x4 -> x0, other arithmetic: 20.7 us -> none  [the longest x1 16.2 us: block_product(): jnp.where((steps_k < 0)[:, None, None, None], jnp.swapaxes(left_raw, 2, 3...]
  transfers between devices with their start and end apart: 3 -> 15, of which waited for: 3 -> 2; matrix products, arithmetic and copies ran while one was open for 1% -> 1% of each run, Pallas kernels for 0% -> 36%
where the time goes in v2:
time: 142 us
  Pallas kernels  55.5 us (39%)
  starting transfers between devices  35.1 us (25%)
  blocking collectives  26.8 us (19%)
  waiting for transfers between devices  21.4 us (15%)
  local copies, waits for them, and re-layouts  2.19 us (2%)
    pallas_call x5, Pallas kernels, run(): pl.pallas_call(functools.partial(stage_kernel, stage, tuple(plans[stage])...  32 us
    all_to_all x1, blocking collectives, body(): lax.all_to_all(spread, ('rows', 'cols'), 0, 0, tiled=True).reshape(-1)  26.8 us
    ppermute x8, starting transfers between devices, row_shift(): lax.ppermute(array, 'rows', [(i, i + by) for i in range(size) if 0 <= i +...  23 us
    pallas_call x1, Pallas kernels, body(): pl.pallas_call(functools.partial(list_kernel, row_count, own, wanted_slot...  19.2 us
    ppermute x4, waiting for transfers between devices, body(): lax.ppermute(array, 'cols', pairs)  13.3 us
    ppermute x4, starting transfers between devices, body(): lax.ppermute(array, 'cols', pairs)  8.23 us
    ppermute x3, waiting for transfers between devices, body(): arrived = [lax.ppermute(array, 'cols', ups + downs) for array in parts]  8.07 us
    ppermute x3, starting transfers between devices, body(): arrived = [lax.ppermute(array, 'cols', ups + downs) for array in parts]  3.88 us
  transfers between devices with their start and end apart: 15, of which 2 were waited for; matrix products, arithmetic and copies ran while one was open for 1% of the time, Pallas kernels for 36%

profile of v2, /device:TPU:1, one launch (start us, length us, event | category | flops | bytes accessed | tf_op | source)
XLA Modules:
  0.0 141.6 jit_solution(3277231321257427649)
XLA Ops:
  0.0 0.0 copy-start.2
  0.0 1.4 collective-permute-start.1
  1.4 4.8 %collective-permute-start = (bf16[24,2,128,128]{3,2,1,0:T(8,128)(2,1)}, bf16[24,2,128,128]{3,2,1,0:T(8,128)(2,1)S(1)}, u32[]{:S(2)}, u32[]{:S(2)}) collective-permute-start(bf16[24,2,128,128]{3,2,1,0:T(8,128)(2,1)} %refs_2_.1), channel_id=1, source_target_pairs={{0,1},{1,2},{2,3},{4,5},{5,6},{6,7},{8,9},{9,10},{10,11},{12,13},{... | collective-permute-start | bytes 4718600 | tf_op jit(solution)/shard_map/ppermute | solution.py:422
  6.2 0.1 pad_add_fusion.place_ref
  6.3 0.0 copy-start
  6.3 1.4 copy-done
  7.7 1.6 %rows_of.3 = (bf16[9,2,128,128]{3,2,1,0:T(8,128)(2,1)}, bf16[9,2,128,128]{3,2,1,0:T(8,128)(2,1)}) custom-call(s32[2]{0:T(128)S(1)} %pad_add_fusion.place_ref, bf16[24,2,128,128]{3,2,1,0:T(8,128)(2,1)S(1)} %copy-done), custom_call_target="tpu_custom_call" | custom-call | flops 1 | bytes 1 | tf_op jit(solution)/shard_map/rows_of/pallas_call | solution.py:335
  9.3 2.9 %collective-permute-start.2 = (bf16[9,2,128,128]{3,2,1,0:T(8,128)(2,1)}, bf16[9,2,128,128]{3,2,1,0:T(8,128)(2,1)}, u32[]{:S(2)}, u32[]{:S(2)}) collective-permute-start(bf16[9,2,128,128]{3,2,1,0:T(8,128)(2,1)} %get-tuple-element.30), channel_id=1, source_target_pairs={{4,0},{8,4},{12,8},{5,1},{9,5},{13,9},{6,2},{10,6},{14,10},{7,3},{... | collective-permute-start | bytes 1769480 | tf_op jit(solution)/shard_map/ppermute | solution.py:55
  12.2 3.5 %collective-permute-start.3 = (bf16[9,2,128,128]{3,2,1,0:T(8,128)(2,1)}, bf16[9,2,128,128]{3,2,1,0:T(8,128)(2,1)}, u32[]{:S(2)}, u32[]{:S(2)}) collective-permute-start(bf16[9,2,128,128]{3,2,1,0:T(8,128)(2,1)} %get-tuple-element.31), channel_id=1, source_target_pairs={{0,4},{4,8},{8,12},{1,5},{5,9},{9,13},{2,6},{6,10},{10,14},{3,7},{... | collective-permute-start | bytes 1769480 | tf_op jit(solution)/shard_map/ppermute | solution.py:55
  15.6 0.8 reshape.11
  16.4 26.8 %all_to_all.5 = s32[16,8,128]{2,1,0:T(8,128)S(1)} all-to-all(s32[16,8,128]{2,1,0:T(8,128)S(1)} %broadcast_in_dim.8), channel_id=1, replica_groups=mesh['groups'=2,'rows'=4,'cols'=4] {'rows','cols'}, dimensions={0} | all-to-all | bytes 131072 | tf_op jit(solution)/shard_map/all_to_all | solution.py:430
  43.2 0.0 collective-permute-done.2.refs_3_
  43.2 0.0 collective-permute-done.3.refs_4_
  43.2 0.0 collective-permute-done.1.refs_1_
  43.2 0.0 collective-permute-done.refs_0_
  43.2 0.8 collective-permute-start.4
  44.0 1.3 collective-permute-start.5
  45.3 1.0 rows_of.5
  46.4 2.3 %collective-permute-start.8 = (bf16[18,2,128,128]{3,2,1,0:T(8,128)(2,1)S(1)}, bf16[18,2,128,128]{3,2,1,0:T(8,128)(2,1)S(1)}, u32[]{:S(2)}, u32[]{:S(2)}) collective-permute-start(bf16[18,2,128,128]{3,2,1,0:T(8,128)(2,1)S(1)} %get-tuple-element.36), channel_id=1, source_target_pairs={{4,0},{8,4},{12,8},{5,1},{9,5},{13,9},{6,2},{10,6},{14,10},{7,3},{... | collective-permute-start | bytes 3538952 | tf_op jit(solution)/shard_map/ppermute | solution.py:55
  48.7 3.3 %collective-permute-start.9 = (bf16[18,2,128,128]{3,2,1,0:T(8,128)(2,1)S(1)}, bf16[18,2,128,128]{3,2,1,0:T(8,128)(2,1)S(1)}, u32[]{:S(2)}, u32[]{:S(2)}) collective-permute-start(bf16[18,2,128,128]{3,2,1,0:T(8,128)(2,1)S(1)} %get-tuple-element.37), channel_id=1, source_target_pairs={{0,4},{4,8},{8,12},{1,5},{5,9},{9,13},{2,6},{6,10},{10,14},{3,7},{... | collective-permute-start | bytes 3538952 | tf_op jit(solution)/shard_map/ppermute | solution.py:55
  51.9 0.0 copy-done.2
  51.9 19.2 %lists.1 = (s32[11264]{0:T(1024)S(1)}, s32[20]{0:T(128)S(1)}) custom-call(s32[2]{0:T(128)S(1)} %pad_add_fusion.place_ref, s32[4,24]{1,0:T(4,128)S(1)} %bitcast.10, s32[16384]{0:T(1024)S(1)} %bitcast.9), custom_call_target="tpu_custom_call" | custom-call | flops 1 | bytes 1 | tf_op jit(solution)/shard_map/lists/pallas_call | solution.py:433
  71.1 0.0 collective-permute-done.4.refs_0_.refs_6_
  71.1 13.3 %collective-permute-done.5.refs_1_.refs_7_ = bf16[24,2,128,128]{3,2,1,0:T(8,128)(2,1)S(1)} collective-permute-done((bf16[24,2,128,128]{3,2,1,0:T(8,128)(2,1)S(1)}, bf16[24,2,128,128]{3,2,1,0:T(8,128)(2,1)S(1)}, u32[]{:S(2)}, u32[]{:S(2)}) %collective-permute-start.5) | collective-permute-done | bytes 1572896 | tf_op jit(solution)/shard_map/ppermute | solution.py:422
  84.5 1.0 rows_of.4
  85.5 3.1 %collective-permute-start.10 = (bf16[9,2,128,128]{3,2,1,0:T(8,128)(2,1)S(1)}, bf16[9,2,128,128]{3,2,1,0:T(8,128)(2,1)S(1)}, u32[]{:S(2)}, u32[]{:S(2)}) collective-permute-start(bf16[9,2,128,128]{3,2,1,0:T(8,128)(2,1)S(1)} %get-tuple-element.34), channel_id=1, source_target_pairs={{4,0},{8,4},{12,8},{5,1},{9,5},{13,9},{6,2},{10,6},{14,10},{7,3},{... | collective-permute-start | bytes 1769480 | tf_op jit(solution)/shard_map/ppermute | solution.py:55
  88.6 2.4 %collective-permute-start.11 = (bf16[9,2,128,128]{3,2,1,0:T(8,128)(2,1)S(1)}, bf16[9,2,128,128]{3,2,1,0:T(8,128)(2,1)S(1)}, u32[]{:S(2)}, u32[]{:S(2)}) collective-permute-start(bf16[9,2,128,128]{3,2,1,0:T(8,128)(2,1)S(1)} %get-tuple-element.35), channel_id=1, source_target_pairs={{0,4},{4,8},{8,12},{1,5},{5,9},{9,13},{2,6},{6,10},{10,14},{3,7},{... | collective-permute-start | bytes 1769480 | tf_op jit(solution)/shard_map/ppermute | solution.py:55
  91.1 1.3 collective-permute-start.6
  92.4 0.0 collective-permute-done.8.refs_2_.refs_4_
  92.4 1.3 collective-permute-start.7
  93.7 0.0 collective-permute-done.9.refs_3_.refs_5_
  93.7 1.3 collective-permute-start.14
  95.0 0.0 copy-done.1
  95.0 8.7 %stage_0.1 = (bf16[680,128,128]{2,1,0:T(8,128)(2,1)S(1)}, f32[96,128,128]{2,1,0:T(8,128)S(1)}, s32[1]{0:T(128)}) custom-call(s32[2]{0:T(128)S(1)} %pad_add_fusion.place_ref, s32[20]{0:T(128)S(1)} %get-tuple-element.28.refs_2_.refs_0_, s32[11264]{0:T(1024)S(1)} %get-tuple-element.29.refs_1_, bf16[24,2,128,128]{3,2,1,0:T(8,128)(2,1)S(1)} %copy-done.1, ...), custom_call_target="tpu_custom_call" | custom-call | flops 1 | bytes 1 | tf_op jit(solution)/shard_map/stage_0/pallas_call | solution.py:388
  103.7 0.0 collective-permute-done.10.refs_8_
  103.7 0.0 collective-permute-done.11.refs_9_
  103.7 8.7 %stage_1.1 = (bf16[680,128,128]{2,1,0:T(8,128)(2,1)S(1)}, f32[96,128,128]{2,1,0:T(8,128)S(1)}, s32[1]{0:T(128)}) custom-call(s32[2]{0:T(128)S(1)} %pad_add_fusion.place_ref, s32[20]{0:T(128)S(1)} %get-tuple-element.28.refs_2_.refs_0_, s32[11264]{0:T(1024)S(1)} %get-tuple-element.29.refs_1_, ...), custom_call_target="tpu_custom_call", output_to_operand_aliasing={{0}: (11, {}), {1}: (12, {})} | custom-call | flops 1 | bytes 1 | tf_op jit(solution)/shard_map/stage_1/pallas_call | solution.py:388
  112.5 0.0 collective-permute-done.6.refs_0_
  112.5 8.1 %collective-permute-done.7.refs_1_ = bf16[9,2,128,128]{3,2,1,0:T(8,128)(2,1)S(1)} collective-permute-done((bf16[9,2,128,128]{3,2,1,0:T(8,128)(2,1)S(1)}, bf16[9,2,128,128]{3,2,1,0:T(8,128)(2,1)S(1)}, u32[]{:S(2)}, u32[]{:S(2)}) %collective-permute-start.7) | collective-permute-done | bytes 589856 | tf_op jit(solution)/shard_map/ppermute | solution.py:415
  120.5 0.6 after_all.3
  121.2 3.1 %collective-permute-start.12 = (bf16[9,2,128,128]{3,2,1,0:T(8,128)(2,1)S(1)}, bf16[9,2,128,128]{3,2,1,0:T(8,128)(2,1)S(1)}, u32[]{:S(2)}, u32[]{:S(2)}) collective-permute-start(bf16[9,2,128,128]{3,2,1,0:T(8,128)(2,1)S(1)} %get-tuple-element.41.refs_2_), channel_id=1, source_target_pairs={{4,0},{8,4},{12,8},{5,1},{9,5},{13,9},{6,2},{10,6},{14,10},{7,3},{... | collective-permute-start | bytes 1769480 | tf_op jit(solution)/shard_map/ppermute | solution.py:55
  124.3 2.4 %collective-permute-start.13 = (bf16[9,2,128,128]{3,2,1,0:T(8,128)(2,1)S(1)}, bf16[9,2,128,128]{3,2,1,0:T(8,128)(2,1)S(1)}, u32[]{:S(2)}, u32[]{:S(2)}) collective-permute-start(bf16[9,2,128,128]{3,2,1,0:T(8,128)(2,1)S(1)} %get-tuple-element.42.refs_3_), channel_id=1, source_target_pairs={{0,4},{4,8},{8,12},{1,5},{5,9},{9,13},{2,6},{6,10},{10,14},{3,7},{... | collective-permute-start | bytes 1769480 | tf_op jit(solution)/shard_map/ppermute | solution.py:55
  126.8 5.9 %stage_2.1 = (bf16[680,128,128]{2,1,0:T(8,128)(2,1)S(1)}, f32[96,128,128]{2,1,0:T(8,128)S(1)}, s32[1]{0:T(128)}) custom-call(s32[2]{0:T(128)S(1)} %pad_add_fusion.place_ref, s32[20]{0:T(128)S(1)} %get-tuple-element.28.refs_2_.refs_0_, s32[11264]{0:T(1024)S(1)} %get-tuple-element.29.refs_1_, ...), custom_call_target="tpu_custom_call", output_to_operand_aliasing={{0}: (5, {}), {1}: (6, {})} | custom-call | flops 1 | bytes 1 | tf_op jit(solution)/shard_map/stage_2/pallas_call | solution.py:388
  132.7 0.0 collective-permute-done.14.refs_2_
  132.7 4.0 %stage_3.1 = (bf16[680,128,128]{2,1,0:T(8,128)(2,1)S(1)}, f32[96,128,128]{2,1,0:T(8,128)S(1)}, s32[1]{0:T(128)}) custom-call(s32[2]{0:T(128)S(1)} %pad_add_fusion.place_ref, s32[20]{0:T(128)S(1)} %get-tuple-element.28.refs_2_.refs_0_, s32[11264]{0:T(1024)S(1)} %get-tuple-element.29.refs_1_, ...), custom_call_target="tpu_custom_call", output_to_operand_aliasing={{0}: (4, {}), {1}: (5, {})} | custom-call | flops 8589934592 | bytes 8589934592 | tf_op jit(solution)/shard_map/stage_3/pallas_call | solution.py:388
  136.7 0.0 collective-permute-done.12.refs_2_
  136.8 0.0 collective-permute-done.13.refs_3_
  136.8 4.7 %stage_4.1 = (bf16[680,128,128]{2,1,0:T(8,128)(2,1)S(1)}, f32[96,128,128]{2,1,0:T(8,128)S(1)}, f32[96,128,128]{2,1,0:T(8,128)}) custom-call(s32[2]{0:T(128)S(1)} %pad_add_fusion.place_ref, s32[20]{0:T(128)S(1)} %get-tuple-element.28.refs_2_.refs_0_, s32[11264]{0:T(1024)S(1)} %get-tuple-element.29.refs_1_, ...), custom_call_target="tpu_custom_call", output_to_operand_aliasing={{0}: (5, {}), {1}: (6, {})} | custom-call | flops 1 | bytes 1 | tf_op jit(solution)/shard_map/stage_4/pallas_call | solution.py:388
  (4 shorter events, 0.0 us)
Async XLA Ops:
  0.0 51.9 %copy-start.2 = (s32[24,4]{0,1:T(4,128)S(1)}, s32[24,4]{0,1:T(4,128)}, u32[]{:S(2)}) copy-start(s32[24,4]{0,1:T(4,128)} %param.5) | copy-start | bytes 1156
  0.0 43.2 %collective-permute-start.1 = (bf16[24,2,128,128]{3,2,1,0:T(8,128)(2,1)}, bf16[24,2,128,128]{3,2,1,0:T(8,128)(2,1)S(1)}, u32[]{:S(2)}, u32[]{:S(2)}) collective-permute-start(bf16[24,2,128,128]{3,2,1,0:T(8,128)(2,1)} %refs_2_.1), channel_id=1, source_target_pairs={{1,0},{2,1},{3,2},{5,4},{6,5},{7,6},{9,8},{10,9},{11,10},{13,12},{... | collective-permute-start | bytes 4718600 | tf_op jit(solution)/shard_map/ppermute | solution.py:422
  1.4 41.8 %collective-permute-start = (bf16[24,2,128,128]{3,2,1,0:T(8,128)(2,1)}, bf16[24,2,128,128]{3,2,1,0:T(8,128)(2,1)S(1)}, u32[]{:S(2)}, u32[]{:S(2)}) collective-permute-start(bf16[24,2,128,128]{3,2,1,0:T(8,128)(2,1)} %refs_2_.1), channel_id=1, source_target_pairs={{0,1},{1,2},{2,3},{4,5},{5,6},{6,7},{8,9},{9,10},{10,11},{12,13},{... | collective-permute-start | bytes 4718600 | tf_op jit(solution)/shard_map/ppermute | solution.py:422
  6.3 1.4 copy-start
  9.3 33.9 %collective-permute-start.2 = (bf16[9,2,128,128]{3,2,1,0:T(8,128)(2,1)}, bf16[9,2,128,128]{3,2,1,0:T(8,128)(2,1)}, u32[]{:S(2)}, u32[]{:S(2)}) collective-permute-start(bf16[9,2,128,128]{3,2,1,0:T(8,128)(2,1)} %get-tuple-element.30), channel_id=1, source_target_pairs={{4,0},{8,4},{12,8},{5,1},{9,5},{13,9},{6,2},{10,6},{14,10},{7,3},{... | collective-permute-start | bytes 1769480 | tf_op jit(solution)/shard_map/ppermute | solution.py:55
  12.2 31.1 %collective-permute-start.3 = (bf16[9,2,128,128]{3,2,1,0:T(8,128)(2,1)}, bf16[9,2,128,128]{3,2,1,0:T(8,128)(2,1)}, u32[]{:S(2)}, u32[]{:S(2)}) collective-permute-start(bf16[9,2,128,128]{3,2,1,0:T(8,128)(2,1)} %get-tuple-element.31), channel_id=1, source_target_pairs={{0,4},{4,8},{8,12},{1,5},{5,9},{9,13},{2,6},{6,10},{10,14},{3,7},{... | collective-permute-start | bytes 1769480 | tf_op jit(solution)/shard_map/ppermute | solution.py:55
  16.4 78.6 %copy-start.1 = (bf16[24,2,128,128]{3,2,1,0:T(8,128)(2,1)S(1)}, bf16[24,2,128,128]{3,2,1,0:T(8,128)(2,1)}, u32[]{:S(2)}) copy-start(bf16[24,2,128,128]{3,2,1,0:T(8,128)(2,1)} %refs_2_.1) | copy-start | bytes 4718596
  43.2 27.9 %collective-permute-start.4 = (bf16[24,2,128,128]{3,2,1,0:T(8,128)(2,1)S(1)}, bf16[24,2,128,128]{3,2,1,0:T(8,128)(2,1)S(1)}, u32[]{:S(2)}, u32[]{:S(2)}) collective-permute-start(bf16[24,2,128,128]{3,2,1,0:T(8,128)(2,1)S(1)} %get-tuple-element.32.refs_0_.refs_5_), channel_id=1, source_target_pairs={{1,2},{2,3},{5,6},{6,7},{9,10},{10,11},{13,14},{14,15},{17,18},{18... | collective-permute-start | bytes 4718600 | tf_op jit(solution)/shard_map/ppermute | solution.py:422
  44.0 40.4 %collective-permute-start.5 = (bf16[24,2,128,128]{3,2,1,0:T(8,128)(2,1)S(1)}, bf16[24,2,128,128]{3,2,1,0:T(8,128)(2,1)S(1)}, u32[]{:S(2)}, u32[]{:S(2)}) collective-permute-start(bf16[24,2,128,128]{3,2,1,0:T(8,128)(2,1)S(1)} %get-tuple-element.33.refs_1_.refs_6_), channel_id=1, source_target_pairs={{1,0},{2,1},{5,4},{6,5},{9,8},{10,9},{13,12},{14,13},{17,16},{18,1... | collective-permute-start | bytes 4718600 | tf_op jit(solution)/shard_map/ppermute | solution.py:422
  46.4 46.0 %collective-permute-start.8 = (bf16[18,2,128,128]{3,2,1,0:T(8,128)(2,1)S(1)}, bf16[18,2,128,128]{3,2,1,0:T(8,128)(2,1)S(1)}, u32[]{:S(2)}, u32[]{:S(2)}) collective-permute-start(bf16[18,2,128,128]{3,2,1,0:T(8,128)(2,1)S(1)} %get-tuple-element.36), channel_id=1, source_target_pairs={{4,0},{8,4},{12,8},{5,1},{9,5},{13,9},{6,2},{10,6},{14,10},{7,3},{... | collective-permute-start | bytes 3538952 | tf_op jit(solution)/shard_map/ppermute | solution.py:55
  48.7 45.0 %collective-permute-start.9 = (bf16[18,2,128,128]{3,2,1,0:T(8,128)(2,1)S(1)}, bf16[18,2,128,128]{3,2,1,0:T(8,128)(2,1)S(1)}, u32[]{:S(2)}, u32[]{:S(2)}) collective-permute-start(bf16[18,2,128,128]{3,2,1,0:T(8,128)(2,1)S(1)} %get-tuple-element.37), channel_id=1, source_target_pairs={{0,4},{4,8},{8,12},{1,5},{5,9},{9,13},{2,6},{6,10},{10,14},{3,7},{... | collective-permute-start | bytes 3538952 | tf_op jit(solution)/shard_map/ppermute | solution.py:55
  85.5 18.2 %collective-permute-start.10 = (bf16[9,2,128,128]{3,2,1,0:T(8,128)(2,1)S(1)}, bf16[9,2,128,128]{3,2,1,0:T(8,128)(2,1)S(1)}, u32[]{:S(2)}, u32[]{:S(2)}) collective-permute-start(bf16[9,2,128,128]{3,2,1,0:T(8,128)(2,1)S(1)} %get-tuple-element.34), channel_id=1, source_target_pairs={{4,0},{8,4},{12,8},{5,1},{9,5},{13,9},{6,2},{10,6},{14,10},{7,3},{... | collective-permute-start | bytes 1769480 | tf_op jit(solution)/shard_map/ppermute | solution.py:55
  88.6 15.1 %collective-permute-start.11 = (bf16[9,2,128,128]{3,2,1,0:T(8,128)(2,1)S(1)}, bf16[9,2,128,128]{3,2,1,0:T(8,128)(2,1)S(1)}, u32[]{:S(2)}, u32[]{:S(2)}) collective-permute-start(bf16[9,2,128,128]{3,2,1,0:T(8,128)(2,1)S(1)} %get-tuple-element.35), channel_id=1, source_target_pairs={{0,4},{4,8},{8,12},{1,5},{5,9},{9,13},{2,6},{6,10},{10,14},{3,7},{... | collective-permute-start | bytes 1769480 | tf_op jit(solution)/shard_map/ppermute | solution.py:55
  91.1 21.4 %collective-permute-start.6 = (bf16[9,2,128,128]{3,2,1,0:T(8,128)(2,1)S(1)}, bf16[9,2,128,128]{3,2,1,0:T(8,128)(2,1)S(1)}, u32[]{:S(2)}, u32[]{:S(2)}) collective-permute-start(bf16[9,2,128,128]{3,2,1,0:T(8,128)(2,1)S(1)} %get-tuple-element.34), channel_id=1, source_target_pairs={{2,3},{1,0},{6,7},{5,4},{10,11},{9,8},{14,15},{13,12},{18,19},{17,... | collective-permute-start | bytes 1769480 | tf_op jit(solution)/shard_map/ppermute | solution.py:415
  92.4 28.2 %collective-permute-start.7 = (bf16[9,2,128,128]{3,2,1,0:T(8,128)(2,1)S(1)}, bf16[9,2,128,128]{3,2,1,0:T(8,128)(2,1)S(1)}, u32[]{:S(2)}, u32[]{:S(2)}) collective-permute-start(bf16[9,2,128,128]{3,2,1,0:T(8,128)(2,1)S(1)} %get-tuple-element.35), channel_id=1, source_target_pairs={{2,3},{1,0},{6,7},{5,4},{10,11},{9,8},{14,15},{13,12},{18,19},{17,... | collective-permute-start | bytes 1769480 | tf_op jit(solution)/shard_map/ppermute | solution.py:415
  93.7 39.0 %collective-permute-start.14 = (bf16[6,2,128,128]{3,2,1,0:T(8,128)(2,1)S(1)}, bf16[6,2,128,128]{3,2,1,0:T(8,128)(2,1)S(1)}, u32[]{:S(2)}, u32[]{:S(2)}) collective-permute-start(bf16[6,2,128,128]{3,2,1,0:T(8,128)(2,1)S(1)} %get-tuple-element.43), channel_id=1, source_target_pairs={{2,3},{1,0},{6,7},{5,4},{10,11},{9,8},{14,15},{13,12},{18,19},{17,... | collective-permute-start | bytes 1179656 | tf_op jit(solution)/shard_map/ppermute | solution.py:415
  121.2 15.5 %collective-permute-start.12 = (bf16[9,2,128,128]{3,2,1,0:T(8,128)(2,1)S(1)}, bf16[9,2,128,128]{3,2,1,0:T(8,128)(2,1)S(1)}, u32[]{:S(2)}, u32[]{:S(2)}) collective-permute-start(bf16[9,2,128,128]{3,2,1,0:T(8,128)(2,1)S(1)} %get-tuple-element.41.refs_2_), channel_id=1, source_target_pairs={{4,0},{8,4},{12,8},{5,1},{9,5},{13,9},{6,2},{10,6},{14,10},{7,3},{... | collective-permute-start | bytes 1769480 | tf_op jit(solution)/shard_map/ppermute | solution.py:55
  124.3 12.4 %collective-permute-start.13 = (bf16[9,2,128,128]{3,2,1,0:T(8,128)(2,1)S(1)}, bf16[9,2,128,128]{3,2,1,0:T(8,128)(2,1)S(1)}, u32[]{:S(2)}, u32[]{:S(2)}) collective-permute-start(bf16[9,2,128,128]{3,2,1,0:T(8,128)(2,1)S(1)} %get-tuple-element.42.refs_3_), channel_id=1, source_target_pairs={{0,4},{4,8},{8,12},{1,5},{5,9},{9,13},{2,6},{6,10},{10,14},{3,7},{... | collective-permute-start | bytes 1769480 | tf_op jit(solution)/shard_map/ppermute | solution.py:55

commit v3 on v2

--- a/solution.py
+++ b/solution.py
@@ -16,12 +16,13 @@
 MASK = (1 << BITS) - 1
 OUT_MASK = 127
 STAGE_BIT = 27
-STAGES = 5
+STAGES = 6
 ABSENT = 7
 CHUNKS = 4
 TABLE = 1024
-WEIGHTS = {0: 1, 1: 1, 2: 1, 3: 1 << 33, 4: 1}
+WEIGHTS = {0: 1, 1: 1, 2: 1, 3: 1, 4: 1 << 32, 5: 1}
 LIST_WEIGHT = 1
+EARLY = 1 << 34
 
 SMEM = pl.BlockSpec(memory_space=pltpu.SMEM)
 VMEM = pl.BlockSpec(memory_space=pltpu.VMEM)
@@ -30,11 +31,14 @@
 SMALL = pltpu.CompilerParams(vmem_limit_bytes=1 << 20)
 
 
-def stage_of(step, last, edge):
+LOW, HIGH, MIDDLE, AFTER, BEFORE = range(5)
+
+
+def stage_of(step, last, kind):
     if step == last and step > 1:
-        return 2 + edge
-    if edge == 2:
-        return 0 if step == 0 else 1
+        return {LOW: 2, HIGH: 3, MIDDLE: 4, AFTER: 3, BEFORE: 5}[kind]
+    if kind in (AFTER, BEFORE):
+        return 0 if step == 0 else 2 if step == last - 1 else 1
     return 0 if step <= 1 else 1
 
 
@@ -69,8 +73,8 @@
     place_ref,
     wanted_ref,
     columns_hbm,
+    count_ref,
     terms_ref,
-    count_ref,
     table_ref,
     at_ref,
     columns_ref,
@@ -109,10 +113,10 @@
     for k in range(size):
         distance = jnp.abs(k - me)
         picks = []
-        for edge in range(3):
+        for kind in range(5):
             stage = jnp.int32(0)
             for step in range(size):
-                stage = jnp.where(distance == step, stage_of(step, size - 1, edge), stage)
+                stage = jnp.where(distance == step, stage_of(step, size - 1, kind), stage)
             picks.append(stage << STAGE_BIT)
         stages.append(picks)
     fetch(lambda c: c.wait())
@@ -133,14 +137,18 @@
     def _():
         def enter_before(r, _):
             at = row_count - LEAD + r
-            enter(r, first - LEAD + r, 0, at, lambda k: stages[k][2])
+            enter(r, first - LEAD + r, 0, at, lambda k: stages[k][BEFORE])
             return 0
 
         lax.fori_loop(0, LEAD, enter_before, 0)
 
     def enter_own(r, _):
-        edge = (r < LEAD) | (r >= row_count - LEAD)
-        enter(r + LEAD, first + r, 1, r, lambda k: jnp.where(edge, stages[k][0], stages[k][1]))
+        low, high = r < LEAD, r >= row_count - LEAD
+
+        def stage(k):
+            return jnp.where(low, stages[k][LOW], jnp.where(high, stages[k][HIGH], stages[k][MIDDLE]))
+
+        enter(r + LEAD, first + r, 1, r, stage)
         return 0
 
     lax.fori_loop(0, row_count, enter_own, 0)
@@ -148,7 +156,7 @@
     @pl.when(first + row_count < total_rows)
     def _():
         def enter_after(r, _):
-            enter(LEAD + row_count + r, first + row_count + r, 2, r, lambda k: stages[k][2])
+            enter(LEAD + row_count + r, first + row_count + r, 2, r, lambda k: stages[k][AFTER])
             return 0
 
         lax.fori_loop(0, LEAD, enter_after, 0)
@@ -295,7 +303,7 @@
         pltpu.make_async_copy(sums, out_ref, sem).wait()
 
 
-def after_all(arrays, tokens):
+def after_all(arrays, tokens, weight=1):
     count = len(arrays)
     return list(pl.pallas_call(
         lambda *refs: None,
@@ -304,30 +312,38 @@
         out_specs=[ANY] * count,
         input_output_aliases={n: n for n in range(count)},
         compiler_params=SMALL,
-        cost_estimate=quick(1),
+        cost_estimate=quick(weight),
         name="after_all",
     )(*arrays, *tokens))
 
 
-def rows_of(arrays, place, step, tokens, spans):
-    both = step == 0 and len(arrays) == 2
+def rows_of(groups, place, step, tokens, wanted, weight=1):
+    arrays = [array for group in groups for array in group]
     shape = arrays[0].shape[1:]
+    first_of = [sum(len(g) for g in groups[:n]) for n in range(len(groups))]
+    folds = [len(group) if step == 0 else 1 for group in groups]
 
     def kernel(place_ref, *refs):
-        given, given_out, sem = refs[: len(arrays)], refs[len(arrays) + len(tokens) : -1], refs[-1]
+        results, sem = refs[len(arrays) + len(tokens) : -1], refs[-1]
 
         def copies(go):
-            for target, (start, stop) in zip(given_out, spans):
-                rows = stop - start
-                if both or len(given) == 1:
-                    for n, source in enumerate(given):
-                        go(pltpu.make_async_copy(source.at[pl.ds(start, rows)], target.at[pl.ds(n * rows, rows)], sem))
-                    continue
-                for wanted, source in ((place_ref[0] >= step, given[0]), (place_ref[0] < step, given[1])):
-
-                    @pl.when(wanted)
-                    def _(source=source, target=target, start=start, rows=rows):
-                        go(pltpu.make_async_copy(source.at[pl.ds(start, rows)], target, sem))
+            for target, spans in zip(results, wanted):
+                at = 0
+                for group, start, stop in spans:
+                    rows = stop - start
+                    sources = refs[first_of[group] : first_of[group] + len(groups[group])]
+                    if folds[group] == len(sources):
+                        for source in sources:
+                            go(pltpu.make_async_copy(source.at[pl.ds(start, rows)], target.at[pl.ds(at, rows)], sem))
+                            at += rows
+                        continue
+                    for chosen, source in ((place_ref[0] >= step, sources[0]), (place_ref[0] < step, sources[1])):
+
+                        @pl.when(chosen)
+                        def _(source=source, target=target, start=start, rows=rows, at=at):
+                            go(pltpu.make_async_copy(source.at[pl.ds(start, rows)], target.at[pl.ds(at, rows)], sem))
+
+                    at += rows
 
         copies(lambda c: c.start())
         copies(lambda c: c.wait())
@@ -335,14 +351,14 @@
     return list(pl.pallas_call(
         kernel,
         out_shape=[
-            jax.ShapeDtypeStruct(((2 if both else 1) * (stop - start), *shape), arrays[0].dtype)
-            for start, stop in spans
+            jax.ShapeDtypeStruct((sum(folds[g] * (stop - start) for g, start, stop in spans), *shape), arrays[0].dtype)
+            for spans in wanted
         ],
         in_specs=[SMEM] + [ANY] * (len(arrays) + len(tokens)),
-        out_specs=[ANY] * len(spans),
+        out_specs=[ANY] * len(wanted),
         scratch_shapes=[pltpu.SemaphoreType.DMA],
         compiler_params=SMALL,
-        cost_estimate=quick(1),
+        cost_estimate=quick(weight),
         name="rows_of",
     )(place, *arrays, *tokens))
 
@@ -367,18 +383,13 @@
         plans[stage].append((source, rows, target, shift))
         pieces[stage].append(array)
 
-    def trade(array_low, array_high, shifts, step):
-        stage = stage_of(step, last, 2)
-        after, before = row_shift(array_low, -1), row_shift(array_high, 1)
+    def trade(array, by, shifts, step):
+        kind, target = (AFTER, LEAD + row_count) if by < 0 else (BEFORE, 0)
+        moved = row_shift(array, by)
         for n, shift in enumerate(shifts):
-            keep(stage, after, n * LEAD, LEAD, LEAD + row_count, shift)
-            keep(stage, before, n * LEAD, LEAD, 0, shift)
-
-    edges = [(0, LEAD), (row_count - LEAD, row_count)]
-    middle = (LEAD, row_count - LEAD)
+            keep(stage_of(step, last, kind), moved, n * LEAD, LEAD, target, shift)
 
     place = jnp.stack([me, first_row])
-    lists = []
     state = []
 
     def run(stage):
@@ -408,69 +419,67 @@
         )(place, *lists, *pieces[stage], *given)
         return state[-1]
 
+    low, high, middle = (0, LEAD), (row_count - LEAD, row_count), (LEAD, row_count - LEAD)
+    keep(0, block_values, 0, row_count, LEAD, 0)
+    low_rows, high_rows = rows_of([[block_values]], place, 0, [], [[(0, *low)], [(0, *high)]])
+    trade(low_rows, -1, (0,), 0)
+    trade(high_rows, 1, (0,), 0)
+
+    devices = size * lax.axis_size("rows")
+    spread = jnp.pad(block_columns.T.reshape(-1), (0, TABLE - own * row_count))
+    spread = jnp.broadcast_to(spread.reshape(1, 8, TABLE // 8), (devices, 8, TABLE // 8))
+    tables = lax.all_to_all(spread, ("rows", "cols"), 0, 0, tiled=True).reshape(-1)
+    lists = pl.pallas_call(
+        functools.partial(list_kernel, row_count, own, wanted_slots, size, row_count * lax.axis_size("rows")),
+        out_shape=[
+            jax.ShapeDtypeStruct((STAGES * CHUNKS,), jnp.int32),
+            jax.ShapeDtypeStruct(((STAGES * CHUNKS + 2) * segment,), jnp.int32),
+        ],
+        in_specs=[SMEM, SMEM, HBM],
+        out_specs=[SMEM] * 2,
+        scratch_shapes=[
+            pltpu.SMEM((ext * WIDE,), jnp.int32),
+            pltpu.SMEM(((ABSENT + 1) * CHUNKS,), jnp.int32),
+            pltpu.SMEM((3 * size * TABLE,), jnp.int32),
+            pltpu.SemaphoreType.DMA,
+        ],
+        compiler_params=SMALL,
+        cost_estimate=quick(LIST_WEIGHT),
+        name="lists",
+    )(place, product_columns.T, tables)
+
     moving = [block_values, block_values]
-    for step in range(1, size):
+    for step in range(1, last):
         ups, downs = up_pairs(size, step), down_pairs(size, step)
-        if step == last and step > 1:
-            arrived = [lax.ppermute(array, "cols", ups + downs) for array in parts]
-            arrived[:2] = after_all(arrived[:2], [state[-1]])
-            for array, (start, stop), edge in zip(arrived, [*edges, middle], (0, 0, 1)):
-                keep(stage_of(step, last, edge), array, 0, stop - start, LEAD + start, (step,))
-            trade(arrived[0], arrived[1], ((step,),), step)
-            break
-        if len(moving) == 2:
-            moving = [lax.ppermute(array, "cols", pairs) for array, pairs in zip(moving, (ups, downs))]
-        else:
-            moving = [lax.ppermute(moving[0], "cols", ups + downs)]
+        if 2 * (step - 1) > last and len(moving) == 2:
+            moving = rows_of([moving], place, step - 1, [], [[(0, 0, row_count)]])
+        pairs = [ups, downs] if len(moving) == 2 else [ups + downs]
+        moving = [lax.ppermute(array, "cols", pair) for array, pair in zip(moving, pairs)]
         if step == 1:
-            keep(0, block_values, 0, row_count, LEAD, 0)
-            devices = size * lax.axis_size("rows")
-            spread = jnp.pad(block_columns.T.reshape(-1), (0, TABLE - own * row_count))
-            spread = jnp.broadcast_to(spread.reshape(1, 8, TABLE // 8), (devices, 8, TABLE // 8))
-            tables = lax.all_to_all(spread, ("rows", "cols"), 0, 0, tiled=True).reshape(-1)
-            trade(*rows_of([block_values], place, 0, [], edges), (0,), 0)
-            moving = after_all(moving, [tables, *pieces[0][1:]])
-            terms, counts = pl.pallas_call(
-                functools.partial(
-                    list_kernel, row_count, own, wanted_slots, size, row_count * lax.axis_size("rows")
-                ),
-                out_shape=[
-                    jax.ShapeDtypeStruct(((STAGES * CHUNKS + 2) * segment,), jnp.int32),
-                    jax.ShapeDtypeStruct((STAGES * CHUNKS,), jnp.int32),
-                ],
-                in_specs=[SMEM, SMEM, HBM],
-                out_specs=[SMEM] * 2,
-                scratch_shapes=[
-                    pltpu.SMEM((ext * WIDE,), jnp.int32),
-                    pltpu.SMEM(((ABSENT + 1) * CHUNKS,), jnp.int32),
-                    pltpu.SMEM((3 * size * TABLE,), jnp.int32),
-                    pltpu.SemaphoreType.DMA,
-                ],
-                compiler_params=SMALL,
-                cost_estimate=quick(LIST_WEIGHT),
-                name="lists",
-            )(place, product_columns.T, tables)
-            lists = [counts, terms]
-        elif len(moving) == 2 and 2 * step > last:
-            pass
-        else:
-            moving = after_all(moving, [])
-        stage = stage_of(step, last, 0)
+            moving = after_all(moving, [tables, *pieces[0][-2:]])
         shifts = (-step, step) if len(moving) == 2 else ((step,),)
         for array, shift in zip(moving, shifts):
-            keep(stage, array, 0, row_count, LEAD, shift)
-        if step + 1 == last:
-            parts = rows_of(moving, place, step, [counts], [*edges, middle])
-            trade(parts[0], parts[1], ((step,),), step)
-            run(0)
-            run(1)
-        elif 2 * step > last:
-            if len(moving) == 2:
-                moving = rows_of(moving, place, step, [], [(0, row_count)])
-            trade(*rows_of(moving, place, step, [], edges), ((step,),), step)
-        else:
-            trade(*rows_of(moving, place, 0, [], edges), (-step, step), step)
-    for stage in range(2, STAGES):
+            keep(stage_of(step, last, LOW), array, 0, row_count, LEAD, shift)
+        if step < last - 1:
+            shifts, way = (((step,),), step) if 2 * step > last else ((-step, step), 0)
+            low_rows, high_rows = rows_of([moving], place, way, [], [[(0, *low)], [(0, *high)]])
+            trade(low_rows, -1, shifts, step)
+            trade(high_rows, 1, shifts, step)
+
+    step = last - 1
+    parts = rows_of([moving], place, step, [run(0)], [[(0, *low)], [(0, *high)], [(0, *middle)]])
+    pairs = up_pairs(size, last) + down_pairs(size, last)
+    arrived = [lax.ppermute(array, "cols", pairs) for array in parts]
+    trade(parts[0], -1, ((step,),), step)
+    trade(parts[1], 1, ((step,),), step)
+    arrived[:1] = after_all(arrived[:1], [run(1)], EARLY)
+    keep(stage_of(last, last, LOW), arrived[0], 0, LEAD, LEAD, (last,))
+    trade(arrived[0], -1, ((last,),), last)
+    arrived[1:2] = after_all(arrived[1:2], [run(2)])
+    keep(stage_of(last, last, HIGH), arrived[1], 0, LEAD, row_count, (last,))
+    trade(arrived[1], 1, ((last,),), last)
+    keep(stage_of(last, last, MIDDLE), arrived[2], 0, row_count - 2 * LEAD, 2 * LEAD, (last,))
+    for stage in range(3, STAGES):
         run(stage)
     return state[-1].reshape(row_count, wanted_slots, tile, tile)
 

time: 142 us -> 135 us (0.951)
  waiting for transfers between devices: 21.4 us -> 8.06 us
  Pallas kernels: 55.5 us -> 58.6 us
  starting transfers between devices: 35.1 us -> 38.2 us
    ppermute x7, waiting for transfers between devices: 21.4 us -> 8.04 us  [the longest x4 4.5 us: body(): lax.ppermute(array, 'cols', pair)]
    ppermute x8, starting transfers between devices: 23 us -> 26.1 us  [row_shift(): lax.ppermute(array, 'rows', [(i, i + by) for i in range(size) if 0 <= i +...]
    pallas_call x5 -> x6, Pallas kernels: 32 us -> 33.3 us  [run(): pl.pallas_call(functools.partial(stage_kernel, stage, tuple(plans[stage])...]
  transfers between devices with their start and end apart: 15 -> 15, of which waited for: 2 -> 3; matrix products, arithmetic and copies ran while one was open for 1% -> 1% of each run, Pallas kernels for 36% -> 40%
where the time goes in v3:
time: 135 us; the launch traced here: 134 us
  Pallas kernels  58.6 us (43%)
  starting transfers between devices  38.2 us (28%)
  blocking collectives  26.8 us (20%)
  waiting for transfers between devices  8.06 us (6%)
  local copies, waits for them, and re-layouts  2.19 us (2%)
    pallas_call x6, Pallas kernels, run(): pl.pallas_call(functools.partial(stage_kernel, stage, tuple(plans[stage])...  33.3 us
    all_to_all x1, blocking collectives, body(): lax.all_to_all(spread, ('rows', 'cols'), 0, 0, tiled=True).reshape(-1)  26.8 us
    ppermute x8, starting transfers between devices, row_shift(): lax.ppermute(array, 'rows', [(i, i + by) for i in range(size) if 0 <= i +...  26.1 us
    pallas_call x1, Pallas kernels, body(): pl.pallas_call(functools.partial(list_kernel, row_count, own, wanted_slot...  19.8 us
    ppermute x4, starting transfers between devices, body(): lax.ppermute(array, 'cols', pair)  8.23 us
    ppermute x4, waiting for transfers between devices, body(): lax.ppermute(array, 'cols', pair)  4.5 us
    pallas_call x3, Pallas kernels, rows_of(): pl.pallas_call(kernel, out_shape=[jax.ShapeDtypeStruct((sum((folds[g] * (...  4.29 us
    ppermute x3, starting transfers between devices, body(): arrived = [lax.ppermute(array, 'cols', pairs) for array in parts]  3.88 us
  transfers between devices with their start and end apart: 15, of which 3 were waited for; matrix products, arithmetic and copies ran while one was open for 1% of the time, Pallas kernels for 40%

profile of v3, /device:TPU:1, one launch (start us, length us, event | category | flops | bytes accessed | tf_op | source)
XLA Modules:
  0.0 134.5 jit_solution(9038318450181599917)
XLA Ops:
  0.0 1.4 %collective-permute-start.1 = (bf16[24,2,128,128]{3,2,1,0:T(8,128)(2,1)}, bf16[24,2,128,128]{3,2,1,0:T(8,128)(2,1)S(1)}, u32[]{:S(2)}, u32[]{:S(2)}) collective-permute-start(bf16[24,2,128,128]{3,2,1,0:T(8,128)(2,1)} %refs_2_.1), channel_id=1, source_target_pairs={{1,0},{2,1},{3,2},{5,4},{6,5},{7,6},{9,8},{10,9},{11,10},{13,12},{... | collective-permute-start | bytes 4718600 | tf_op jit(solution)/shard_map/ppermute | solution.py:457
  1.4 4.8 %collective-permute-start = (bf16[24,2,128,128]{3,2,1,0:T(8,128)(2,1)}, bf16[24,2,128,128]{3,2,1,0:T(8,128)(2,1)S(1)}, u32[]{:S(2)}, u32[]{:S(2)}) collective-permute-start(bf16[24,2,128,128]{3,2,1,0:T(8,128)(2,1)} %refs_2_.1), channel_id=1, source_target_pairs={{0,1},{1,2},{2,3},{4,5},{5,6},{6,7},{8,9},{9,10},{10,11},{12,13},{... | collective-permute-start | bytes 4718600 | tf_op jit(solution)/shard_map/ppermute | solution.py:457
  6.2 0.1 pad_add_fusion.place_ref
  6.3 1.4 %copy-done = bf16[24,2,128,128]{3,2,1,0:T(8,128)(2,1)S(1)} copy-done((bf16[24,2,128,128]{3,2,1,0:T(8,128)(2,1)S(1)}, bf16[24,2,128,128]{3,2,1,0:T(8,128)(2,1)}, u32[]{:S(2)}) %copy-start) | copy-done | bytes 1572888
  7.7 1.6 %rows_of.3 = (bf16[9,2,128,128]{3,2,1,0:T(8,128)(2,1)}, bf16[9,2,128,128]{3,2,1,0:T(8,128)(2,1)}) custom-call(s32[2]{0:T(128)S(1)} %pad_add_fusion.place_ref, bf16[24,2,128,128]{3,2,1,0:T(8,128)(2,1)S(1)} %copy-done), custom_call_target="tpu_custom_call" | custom-call | flops 1 | bytes 1 | tf_op jit(solution)/shard_map/rows_of/pallas_call | solution.py:351
  9.3 2.9 %collective-permute-start.2 = (bf16[9,2,128,128]{3,2,1,0:T(8,128)(2,1)}, bf16[9,2,128,128]{3,2,1,0:T(8,128)(2,1)}, u32[]{:S(2)}, u32[]{:S(2)}) collective-permute-start(bf16[9,2,128,128]{3,2,1,0:T(8,128)(2,1)} %get-tuple-element.32), channel_id=1, source_target_pairs={{4,0},{8,4},{12,8},{5,1},{9,5},{13,9},{6,2},{10,6},{14,10},{7,3},{... | collective-permute-start | bytes 1769480 | tf_op jit(solution)/shard_map/ppermute | solution.py:59
  12.2 3.5 %collective-permute-start.3 = (bf16[9,2,128,128]{3,2,1,0:T(8,128)(2,1)}, bf16[9,2,128,128]{3,2,1,0:T(8,128)(2,1)}, u32[]{:S(2)}, u32[]{:S(2)}) collective-permute-start(bf16[9,2,128,128]{3,2,1,0:T(8,128)(2,1)} %get-tuple-element.33), channel_id=1, source_target_pairs={{0,4},{4,8},{8,12},{1,5},{5,9},{9,13},{2,6},{6,10},{10,14},{3,7},{... | collective-permute-start | bytes 1769480 | tf_op jit(solution)/shard_map/ppermute | solution.py:59
  15.6 0.8 reshape.11
  16.4 26.8 %all_to_all.5 = s32[16,8,128]{2,1,0:T(8,128)S(1)} all-to-all(s32[16,8,128]{2,1,0:T(8,128)S(1)} %broadcast_in_dim.8), channel_id=1, replica_groups=mesh['groups'=2,'rows'=4,'cols'=4] {'rows','cols'}, dimensions={0} | all-to-all | bytes 131072 | tf_op jit(solution)/shard_map/all_to_all | solution.py:431
  43.2 0.0 collective-permute-done.2.refs_3_
  43.2 0.0 collective-permute-done.3.refs_4_
  43.2 0.0 collective-permute-done.1.refs_1_
  43.2 0.0 collective-permute-done.refs_0_
  43.2 0.8 collective-permute-start.4
  44.0 1.3 collective-permute-start.5
  45.3 1.0 rows_of.5
  46.4 2.3 %collective-permute-start.10 = (bf16[18,2,128,128]{3,2,1,0:T(8,128)(2,1)S(1)}, bf16[18,2,128,128]{3,2,1,0:T(8,128)(2,1)S(1)}, u32[]{:S(2)}, u32[]{:S(2)}) collective-permute-start(bf16[18,2,128,128]{3,2,1,0:T(8,128)(2,1)S(1)} %get-tuple-element.39), channel_id=1, source_target_pairs={{4,0},{8,4},{12,8},{5,1},{9,5},{13,9},{6,2},{10,6},{14,10},{7,3},{... | collective-permute-start | bytes 3538952 | tf_op jit(solution)/shard_map/ppermute | solution.py:59
  48.7 3.3 %collective-permute-start.11 = (bf16[18,2,128,128]{3,2,1,0:T(8,128)(2,1)S(1)}, bf16[18,2,128,128]{3,2,1,0:T(8,128)(2,1)S(1)}, u32[]{:S(2)}, u32[]{:S(2)}) collective-permute-start(bf16[18,2,128,128]{3,2,1,0:T(8,128)(2,1)S(1)} %get-tuple-element.40), channel_id=1, source_target_pairs={{0,4},{4,8},{8,12},{1,5},{5,9},{9,13},{2,6},{6,10},{10,14},{3,7},{... | collective-permute-start | bytes 3538952 | tf_op jit(solution)/shard_map/ppermute | solution.py:59
  51.9 0.0 copy-done.2
  51.9 19.8 %lists.1 = (s32[24]{0:T(128)S(1)}, s32[13312]{0:T(1024)S(1)}) custom-call(s32[2]{0:T(128)S(1)} %pad_add_fusion.place_ref, s32[4,24]{1,0:T(4,128)S(1)} %bitcast.10, s32[16384]{0:T(1024)S(1)} %bitcast.9), custom_call_target="tpu_custom_call" | custom-call | flops 1 | bytes 1 | tf_op jit(solution)/shard_map/lists/pallas_call | solution.py:432
  71.7 0.0 copy-done.1
  71.7 8.2 %stage_0.1 = (bf16[680,128,128]{2,1,0:T(8,128)(2,1)S(1)}, f32[96,128,128]{2,1,0:T(8,128)S(1)}, s32[1]{0:T(128)}) custom-call(s32[2]{0:T(128)S(1)} %pad_add_fusion.place_ref, s32[24]{0:T(128)S(1)} %get-tuple-element.30.refs_0_, s32[13312]{0:T(1024)S(1)} %get-tuple-element.31.refs_1_, bf16[24,2,128,128]{3,2,1,0:T(8,128)(2,1)S(1)} %copy-done.1, ...), custom_call_target="tpu_custom_call" | custom-call | flops 1 | bytes 1 | tf_op jit(solution)/shard_map/stage_0/pallas_call | solution.py:399
  80.0 0.0 collective-permute-done.4.refs_0_.refs_6_
  80.0 4.5 %collective-permute-done.5.refs_1_.refs_7_ = bf16[24,2,128,128]{3,2,1,0:T(8,128)(2,1)S(1)} collective-permute-done((bf16[24,2,128,128]{3,2,1,0:T(8,128)(2,1)S(1)}, bf16[24,2,128,128]{3,2,1,0:T(8,128)(2,1)S(1)}, u32[]{:S(2)}, u32[]{:S(2)}) %collective-permute-start.5) | collective-permute-done | bytes 1572896 | tf_op jit(solution)/shard_map/ppermute | solution.py:457
  84.5 1.7 %rows_of.4 = (bf16[9,2,128,128]{3,2,1,0:T(8,128)(2,1)S(1)}, bf16[9,2,128,128]{3,2,1,0:T(8,128)(2,1)S(1)}, bf16[6,2,128,128]{3,2,1,0:T(8,128)(2,1)S(1)}) custom-call(s32[2]{0:T(128)S(1)} %pad_add_fusion.place_ref, bf16[24,2,128,128]{3,2,1,0:T(8,128)(2,1)S(1)} %collective-permute-done.4.refs_0_.refs_6_, ...), custom_call_target="tpu_custom_call" | custom-call | flops 1 | bytes 1 | tf_op jit(solution)/shard_map/rows_of/pallas_call | solution.py:351
  86.1 1.3 collective-permute-start.9
  87.4 3.3 %collective-permute-start.8 = (bf16[9,2,128,128]{3,2,1,0:T(8,128)(2,1)S(1)}, bf16[9,2,128,128]{3,2,1,0:T(8,128)(2,1)S(1)}, u32[]{:S(2)}, u32[]{:S(2)}) collective-permute-start(bf16[9,2,128,128]{3,2,1,0:T(8,128)(2,1)S(1)} %get-tuple-element.37), channel_id=1, source_target_pairs={{0,4},{4,8},{8,12},{1,5},{5,9},{9,13},{2,6},{6,10},{10,14},{3,7},{... | collective-permute-start | bytes 1769480 | tf_op jit(solution)/shard_map/ppermute | solution.py:59
  90.7 1.3 collective-permute-start.6
  92.0 0.0 collective-permute-done.10.refs_2_.refs_3_
  92.0 1.9 %collective-permute-start.7 = (bf16[9,2,128,128]{3,2,1,0:T(8,128)(2,1)S(1)}, bf16[9,2,128,128]{3,2,1,0:T(8,128)(2,1)S(1)}, u32[]{:S(2)}, u32[]{:S(2)}) collective-permute-start(bf16[9,2,128,128]{3,2,1,0:T(8,128)(2,1)S(1)} %get-tuple-element.38), channel_id=1, source_target_pairs={{4,0},{8,4},{12,8},{5,1},{9,5},{13,9},{6,2},{10,6},{14,10},{7,3},{... | collective-permute-start | bytes 1769480 | tf_op jit(solution)/shard_map/ppermute | solution.py:59
  94.0 0.0 collective-permute-done.11.refs_4_.refs_5_
  94.0 6.9 %stage_1.1 = (bf16[680,128,128]{2,1,0:T(8,128)(2,1)S(1)}, f32[96,128,128]{2,1,0:T(8,128)S(1)}, s32[1]{0:T(128)}) custom-call(s32[2]{0:T(128)S(1)} %pad_add_fusion.place_ref, s32[24]{0:T(128)S(1)} %get-tuple-element.30.refs_0_, s32[13312]{0:T(1024)S(1)} %get-tuple-element.31.refs_1_, ...), custom_call_target="tpu_custom_call", output_to_operand_aliasing={{0}: (9, {}), {1}: (10, {})} | custom-call | flops 1 | bytes 1 | tf_op jit(solution)/shard_map/stage_1/pallas_call | solution.py:399
  100.9 2.1 %collective-permute-done.9.refs_0_ = bf16[9,2,128,128]{3,2,1,0:T(8,128)(2,1)S(1)} collective-permute-done((bf16[9,2,128,128]{3,2,1,0:T(8,128)(2,1)S(1)}, bf16[9,2,128,128]{3,2,1,0:T(8,128)(2,1)S(1)}, u32[]{:S(2)}, u32[]{:S(2)}) %collective-permute-start.9) | collective-permute-done | bytes 589856 | tf_op jit(solution)/shard_map/ppermute | solution.py:472
  103.0 0.6 after_all.4.refs_4_
  103.6 4.4 %collective-permute-start.14 = (bf16[9,2,128,128]{3,2,1,0:T(8,128)(2,1)S(1)}, bf16[9,2,128,128]{3,2,1,0:T(8,128)(2,1)S(1)}, u32[]{:S(2)}, u32[]{:S(2)}) collective-permute-start(bf16[9,2,128,128]{3,2,1,0:T(8,128)(2,1)S(1)} %after_all.4.refs_4_), channel_id=1, source_target_pairs={{4,0},{8,4},{12,8},{5,1},{9,5},{13,9},{6,2},{10,6},{14,10},{7,3},{... | collective-permute-start | bytes 1769480 | tf_op jit(solution)/shard_map/ppermute | solution.py:59
  108.0 1.3 collective-permute-start.13
  109.3 0.0 collective-permute-done.8.refs_3_
  109.4 0.0 collective-permute-done.7.refs_2_
  109.4 4.8 %stage_2.1 = (bf16[680,128,128]{2,1,0:T(8,128)(2,1)S(1)}, f32[96,128,128]{2,1,0:T(8,128)S(1)}, s32[1]{0:T(128)}) custom-call(s32[2]{0:T(128)S(1)} %pad_add_fusion.place_ref, s32[24]{0:T(128)S(1)} %get-tuple-element.30.refs_0_, s32[13312]{0:T(1024)S(1)} %get-tuple-element.31.refs_1_, ...), custom_call_target="tpu_custom_call", output_to_operand_aliasing={{0}: (6, {}), {1}: (7, {})} | custom-call | flops 1 | bytes 1 | tf_op jit(solution)/shard_map/stage_2/pallas_call | solution.py:399
  114.2 1.5 %collective-permute-done.6.refs_0_ = bf16[9,2,128,128]{3,2,1,0:T(8,128)(2,1)S(1)} collective-permute-done((bf16[9,2,128,128]{3,2,1,0:T(8,128)(2,1)S(1)}, bf16[9,2,128,128]{3,2,1,0:T(8,128)(2,1)S(1)}, u32[]{:S(2)}, u32[]{:S(2)}) %collective-permute-start.6) | collective-permute-done | bytes 589856 | tf_op jit(solution)/shard_map/ppermute | solution.py:472
  115.6 0.6 after_all.5.refs_3_
  116.3 4.6 %collective-permute-start.12 = (bf16[9,2,128,128]{3,2,1,0:T(8,128)(2,1)S(1)}, bf16[9,2,128,128]{3,2,1,0:T(8,128)(2,1)S(1)}, u32[]{:S(2)}, u32[]{:S(2)}) collective-permute-start(bf16[9,2,128,128]{3,2,1,0:T(8,128)(2,1)S(1)} %after_all.5.refs_3_), channel_id=1, source_target_pairs={{0,4},{4,8},{8,12},{1,5},{5,9},{9,13},{2,6},{6,10},{10,14},{3,7},{... | collective-permute-start | bytes 1769480 | tf_op jit(solution)/shard_map/ppermute | solution.py:59
  120.9 0.0 collective-permute-done.14.refs_2_
  120.9 5.0 %stage_3.1 = (bf16[680,128,128]{2,1,0:T(8,128)(2,1)S(1)}, f32[96,128,128]{2,1,0:T(8,128)S(1)}, s32[1]{0:T(128)}) custom-call(s32[2]{0:T(128)S(1)} %pad_add_fusion.place_ref, s32[24]{0:T(128)S(1)} %get-tuple-element.30.refs_0_, s32[13312]{0:T(1024)S(1)} %get-tuple-element.31.refs_1_, ...), custom_call_target="tpu_custom_call", output_to_operand_aliasing={{0}: (5, {}), {1}: (6, {})} | custom-call | flops 1 | bytes 1 | tf_op jit(solution)/shard_map/stage_3/pallas_call | solution.py:399
  125.9 0.0 collective-permute-done.13.refs_2_
  125.9 4.0 %stage_4.1 = (bf16[680,128,128]{2,1,0:T(8,128)(2,1)S(1)}, f32[96,128,128]{2,1,0:T(8,128)S(1)}, s32[1]{0:T(128)}) custom-call(s32[2]{0:T(128)S(1)} %pad_add_fusion.place_ref, s32[24]{0:T(128)S(1)} %get-tuple-element.30.refs_0_, s32[13312]{0:T(1024)S(1)} %get-tuple-element.31.refs_1_, ...), custom_call_target="tpu_custom_call", output_to_operand_aliasing={{0}: (4, {}), {1}: (5, {})} | custom-call | flops 4294967296 | bytes 4294967296 | tf_op jit(solution)/shard_map/stage_4/pallas_call | solution.py:399
  129.9 0.0 collective-permute-done.12.refs_2_
  129.9 4.4 %stage_5.1 = (bf16[680,128,128]{2,1,0:T(8,128)(2,1)S(1)}, f32[96,128,128]{2,1,0:T(8,128)S(1)}, f32[96,128,128]{2,1,0:T(8,128)}) custom-call(s32[2]{0:T(128)S(1)} %pad_add_fusion.place_ref, s32[24]{0:T(128)S(1)} %get-tuple-element.30.refs_0_, s32[13312]{0:T(1024)S(1)} %get-tuple-element.31.refs_1_, ...), custom_call_target="tpu_custom_call", output_to_operand_aliasing={{0}: (4, {}), {1}: (5, {})} | custom-call | flops 1 | bytes 1 | tf_op jit(solution)/shard_map/stage_5/pallas_call | solution.py:399
  (6 shorter events, 0.0 us)
Async XLA Ops:
  0.0 51.9 %copy-start.2 = (s32[24,4]{0,1:T(4,128)S(1)}, s32[24,4]{0,1:T(4,128)}, u32[]{:S(2)}) copy-start(s32[24,4]{0,1:T(4,128)} %param.5) | copy-start | bytes 1156
  0.0 43.2 %collective-permute-start.1 = (bf16[24,2,128,128]{3,2,1,0:T(8,128)(2,1)}, bf16[24,2,128,128]{3,2,1,0:T(8,128)(2,1)S(1)}, u32[]{:S(2)}, u32[]{:S(2)}) collective-permute-start(bf16[24,2,128,128]{3,2,1,0:T(8,128)(2,1)} %refs_2_.1), channel_id=1, source_target_pairs={{1,0},{2,1},{3,2},{5,4},{6,5},{7,6},{9,8},{10,9},{11,10},{13,12},{... | collective-permute-start | bytes 4718600 | tf_op jit(solution)/shard_map/ppermute | solution.py:457
  1.4 41.8 %collective-permute-start = (bf16[24,2,128,128]{3,2,1,0:T(8,128)(2,1)}, bf16[24,2,128,128]{3,2,1,0:T(8,128)(2,1)S(1)}, u32[]{:S(2)}, u32[]{:S(2)}) collective-permute-start(bf16[24,2,128,128]{3,2,1,0:T(8,128)(2,1)} %refs_2_.1), channel_id=1, source_target_pairs={{0,1},{1,2},{2,3},{4,5},{5,6},{6,7},{8,9},{9,10},{10,11},{12,13},{... | collective-permute-start | bytes 4718600 | tf_op jit(solution)/shard_map/ppermute | solution.py:457
  6.3 1.4 %copy-start = (bf16[24,2,128,128]{3,2,1,0:T(8,128)(2,1)S(1)}, bf16[24,2,128,128]{3,2,1,0:T(8,128)(2,1)}, u32[]{:S(2)}) copy-start(bf16[24,2,128,128]{3,2,1,0:T(8,128)(2,1)} %refs_2_.1) | copy-start | bytes 4718596
  9.3 33.9 %collective-permute-start.2 = (bf16[9,2,128,128]{3,2,1,0:T(8,128)(2,1)}, bf16[9,2,128,128]{3,2,1,0:T(8,128)(2,1)}, u32[]{:S(2)}, u32[]{:S(2)}) collective-permute-start(bf16[9,2,128,128]{3,2,1,0:T(8,128)(2,1)} %get-tuple-element.32), channel_id=1, source_target_pairs={{4,0},{8,4},{12,8},{5,1},{9,5},{13,9},{6,2},{10,6},{14,10},{7,3},{... | collective-permute-start | bytes 1769480 | tf_op jit(solution)/shard_map/ppermute | solution.py:59
  12.2 31.1 %collective-permute-start.3 = (bf16[9,2,128,128]{3,2,1,0:T(8,128)(2,1)}, bf16[9,2,128,128]{3,2,1,0:T(8,128)(2,1)}, u32[]{:S(2)}, u32[]{:S(2)}) collective-permute-start(bf16[9,2,128,128]{3,2,1,0:T(8,128)(2,1)} %get-tuple-element.33), channel_id=1, source_target_pairs={{0,4},{4,8},{8,12},{1,5},{5,9},{9,13},{2,6},{6,10},{10,14},{3,7},{... | collective-permute-start | bytes 1769480 | tf_op jit(solution)/shard_map/ppermute | solution.py:59
  16.4 55.3 %copy-start.1 = (bf16[24,2,128,128]{3,2,1,0:T(8,128)(2,1)S(1)}, bf16[24,2,128,128]{3,2,1,0:T(8,128)(2,1)}, u32[]{:S(2)}) copy-start(bf16[24,2,128,128]{3,2,1,0:T(8,128)(2,1)} %refs_2_.1) | copy-start | bytes 4718596
  43.2 36.7 %collective-permute-start.4 = (bf16[24,2,128,128]{3,2,1,0:T(8,128)(2,1)S(1)}, bf16[24,2,128,128]{3,2,1,0:T(8,128)(2,1)S(1)}, u32[]{:S(2)}, u32[]{:S(2)}) collective-permute-start(bf16[24,2,128,128]{3,2,1,0:T(8,128)(2,1)S(1)} %get-tuple-element.34.refs_5_.refs_0_), channel_id=1, source_target_pairs={{1,2},{2,3},{5,6},{6,7},{9,10},{10,11},{13,14},{14,15},{17,18},{18... | collective-permute-start | bytes 4718600 | tf_op jit(solution)/shard_map/ppermute | solution.py:457
  44.0 40.4 %collective-permute-start.5 = (bf16[24,2,128,128]{3,2,1,0:T(8,128)(2,1)S(1)}, bf16[24,2,128,128]{3,2,1,0:T(8,128)(2,1)S(1)}, u32[]{:S(2)}, u32[]{:S(2)}) collective-permute-start(bf16[24,2,128,128]{3,2,1,0:T(8,128)(2,1)S(1)} %get-tuple-element.35.refs_6_.refs_1_), channel_id=1, source_target_pairs={{1,0},{2,1},{5,4},{6,5},{9,8},{10,9},{13,12},{14,13},{17,16},{18,1... | collective-permute-start | bytes 4718600 | tf_op jit(solution)/shard_map/ppermute | solution.py:457
  46.4 45.7 %collective-permute-start.10 = (bf16[18,2,128,128]{3,2,1,0:T(8,128)(2,1)S(1)}, bf16[18,2,128,128]{3,2,1,0:T(8,128)(2,1)S(1)}, u32[]{:S(2)}, u32[]{:S(2)}) collective-permute-start(bf16[18,2,128,128]{3,2,1,0:T(8,128)(2,1)S(1)} %get-tuple-element.39), channel_id=1, source_target_pairs={{4,0},{8,4},{12,8},{5,1},{9,5},{13,9},{6,2},{10,6},{14,10},{7,3},{... | collective-permute-start | bytes 3538952 | tf_op jit(solution)/shard_map/ppermute | solution.py:59
  48.7 45.3 %collective-permute-start.11 = (bf16[18,2,128,128]{3,2,1,0:T(8,128)(2,1)S(1)}, bf16[18,2,128,128]{3,2,1,0:T(8,128)(2,1)S(1)}, u32[]{:S(2)}, u32[]{:S(2)}) collective-permute-start(bf16[18,2,128,128]{3,2,1,0:T(8,128)(2,1)S(1)} %get-tuple-element.40), channel_id=1, source_target_pairs={{0,4},{4,8},{8,12},{1,5},{5,9},{9,13},{2,6},{6,10},{10,14},{3,7},{... | collective-permute-start | bytes 3538952 | tf_op jit(solution)/shard_map/ppermute | solution.py:59
  86.1 16.8 %collective-permute-start.9 = (bf16[9,2,128,128]{3,2,1,0:T(8,128)(2,1)S(1)}, bf16[9,2,128,128]{3,2,1,0:T(8,128)(2,1)S(1)}, u32[]{:S(2)}, u32[]{:S(2)}) collective-permute-start(bf16[9,2,128,128]{3,2,1,0:T(8,128)(2,1)S(1)} %get-tuple-element.38), channel_id=1, source_target_pairs={{2,3},{1,0},{6,7},{5,4},{10,11},{9,8},{14,15},{13,12},{18,19},{17,... | collective-permute-start | bytes 1769480 | tf_op jit(solution)/shard_map/ppermute | solution.py:472
  87.4 21.9 %collective-permute-start.8 = (bf16[9,2,128,128]{3,2,1,0:T(8,128)(2,1)S(1)}, bf16[9,2,128,128]{3,2,1,0:T(8,128)(2,1)S(1)}, u32[]{:S(2)}, u32[]{:S(2)}) collective-permute-start(bf16[9,2,128,128]{3,2,1,0:T(8,128)(2,1)S(1)} %get-tuple-element.37), channel_id=1, source_target_pairs={{0,4},{4,8},{8,12},{1,5},{5,9},{9,13},{2,6},{6,10},{10,14},{3,7},{... | collective-permute-start | bytes 1769480 | tf_op jit(solution)/shard_map/ppermute | solution.py:59
  90.7 24.9 %collective-permute-start.6 = (bf16[9,2,128,128]{3,2,1,0:T(8,128)(2,1)S(1)}, bf16[9,2,128,128]{3,2,1,0:T(8,128)(2,1)S(1)}, u32[]{:S(2)}, u32[]{:S(2)}) collective-permute-start(bf16[9,2,128,128]{3,2,1,0:T(8,128)(2,1)S(1)} %get-tuple-element.37), channel_id=1, source_target_pairs={{2,3},{1,0},{6,7},{5,4},{10,11},{9,8},{14,15},{13,12},{18,19},{17,... | collective-permute-start | bytes 1769480 | tf_op jit(solution)/shard_map/ppermute | solution.py:472
  92.0 17.3 %collective-permute-start.7 = (bf16[9,2,128,128]{3,2,1,0:T(8,128)(2,1)S(1)}, bf16[9,2,128,128]{3,2,1,0:T(8,128)(2,1)S(1)}, u32[]{:S(2)}, u32[]{:S(2)}) collective-permute-start(bf16[9,2,128,128]{3,2,1,0:T(8,128)(2,1)S(1)} %get-tuple-element.38), channel_id=1, source_target_pairs={{4,0},{8,4},{12,8},{5,1},{9,5},{13,9},{6,2},{10,6},{14,10},{7,3},{... | collective-permute-start | bytes 1769480 | tf_op jit(solution)/shard_map/ppermute | solution.py:59
  103.6 17.3 %collective-permute-start.14 = (bf16[9,2,128,128]{3,2,1,0:T(8,128)(2,1)S(1)}, bf16[9,2,128,128]{3,2,1,0:T(8,128)(2,1)S(1)}, u32[]{:S(2)}, u32[]{:S(2)}) collective-permute-start(bf16[9,2,128,128]{3,2,1,0:T(8,128)(2,1)S(1)} %after_all.4.refs_4_), channel_id=1, source_target_pairs={{4,0},{8,4},{12,8},{5,1},{9,5},{13,9},{6,2},{10,6},{14,10},{7,3},{... | collective-permute-start | bytes 1769480 | tf_op jit(solution)/shard_map/ppermute | solution.py:59
  108.0 17.8 %collective-permute-start.13 = (bf16[6,2,128,128]{3,2,1,0:T(8,128)(2,1)S(1)}, bf16[6,2,128,128]{3,2,1,0:T(8,128)(2,1)S(1)}, u32[]{:S(2)}, u32[]{:S(2)}) collective-permute-start(bf16[6,2,128,128]{3,2,1,0:T(8,128)(2,1)S(1)} %get-tuple-element.47), channel_id=1, source_target_pairs={{2,3},{1,0},{6,7},{5,4},{10,11},{9,8},{14,15},{13,12},{18,19},{17,... | collective-permute-start | bytes 1179656 | tf_op jit(solution)/shard_map/ppermute | solution.py:472
  116.3 13.7 %collective-permute-start.12 = (bf16[9,2,128,128]{3,2,1,0:T(8,128)(2,1)S(1)}, bf16[9,2,128,128]{3,2,1,0:T(8,128)(2,1)S(1)}, u32[]{:S(2)}, u32[]{:S(2)}) collective-permute-start(bf16[9,2,128,128]{3,2,1,0:T(8,128)(2,1)S(1)} %after_all.5.refs_3_), channel_id=1, source_target_pairs={{0,4},{4,8},{8,12},{1,5},{5,9},{9,13},{2,6},{6,10},{10,14},{3,7},{... | collective-permute-start | bytes 1769480 | tf_op jit(solution)/shard_map/ppermute | solution.py:59

commit v4 on v3

--- a/solution.py
+++ b/solution.py
@@ -12,6 +12,7 @@
 SPAN = 2 * W - 1
 WIDE = 4 * W
 UNROLL = 16
+FEW = 8
 BITS = 10
 MASK = (1 << BITS) - 1
 OUT_MASK = 127
@@ -52,6 +53,25 @@
 
 def down_pairs(size, step):
     return [(i + 1, i) for i in range(size - step)]
+
+
+def from_below(size, step):
+    return tuple(i - step if i >= step else -1 for i in range(size))
+
+
+def from_above(size, step):
+    return tuple(i + step if i + step < size else -1 for i in range(size))
+
+
+def either(one, other):
+    return tuple(max(a, b) for a, b in zip(one, other))
+
+
+def pick(me, values):
+    found = jnp.int32(values[0])
+    for i, value in enumerate(values[1:], 1):
+        found = jnp.where(me == i, value, found)
+    return found
 
 
 def row_shift(array, by):
@@ -208,26 +228,26 @@
             for extra in range(2 * UNROLL):
                 terms_ref[at + extra] = zero_term + tag
             used = at - (stage * CHUNKS + chunk) * segment
-            count_ref[stage * CHUNKS + chunk] = (used + 2 * UNROLL - 1) // (2 * UNROLL)
-
-
-def stage_kernel(stage, plan, ext, size, own, segment, place_ref, *refs):
+            count_ref[stage * CHUNKS + chunk] = (used + 2 * FEW - 1) // (2 * FEW)
+    count_ref[STAGES * CHUNKS] = me
+
+
+def stage_kernel(stage, plan, ext, size, own, segment, count_ref, terms_hbm, *refs):
     count = len(plan)
-    first, final = stage == 0, stage == STAGES - 1
-    count_ref, terms_hbm = refs[:2]
-    pieces = refs[2 : count + 2]
-    blocks, sums, out_ref, sem, terms_ref, list_sem = refs[count + (2 if first else 4) :]
-    if not final:
+    first, final, writes = stage == 0, stage == STAGES - 1, stage >= STAGES - 2
+    pieces = refs[:count]
+    blocks, sums, out_ref, sem, terms_ref, list_sem = refs[count + (0 if first else 3 if final else 2) :]
+    if not writes:
         out_ref[0] = 0
     slots = size * own
     stored = ext * slots
-    me = place_ref[0]
+    me = count_ref[STAGES * CHUNKS]
 
     def each(go):
-        for piece, (source, rows, target, shift) in zip(pieces, plan):
-            owner = me + (shift if not isinstance(shift, tuple) else jnp.where(me >= shift[0], -shift[0], shift[0]))
-
-            @pl.when((owner >= 0) & (owner < size))
+        for piece, (source, rows, target, owners) in zip(pieces, plan):
+            owner = pick(me, owners)
+
+            @pl.when(owner >= 0)
             def _(piece=piece, source=source, rows=rows, target=target, owner=owner):
                 go(piece, source, rows, target, owner)
 
@@ -280,27 +300,50 @@
     each(turn)
     listing.wait()
 
+    def multiply(base, entries):
+        found = []
+        for u in range(entries):
+            one, two = terms_ref[base + 2 * u], terms_ref[base + 2 * u + 1]
+            lhs = jnp.concatenate([blocks[one & MASK], blocks[two & MASK]], axis=1)
+            rhs = jnp.concatenate([blocks[(one >> BITS) & MASK], blocks[(two >> BITS) & MASK]], axis=0)
+            found.append(((one >> (2 * BITS)) & OUT_MASK, jnp.dot(lhs, rhs, preferred_element_type=jnp.float32)))
+        for at, value in found:
+            sums[at] += value
+
+    def work(chunk, _):
+        amount = count_ref[stage * CHUNKS + chunk]
+        many = UNROLL // FEW
+        start = chunk * segment
+
+        def group(n, _):
+            multiply(start + n * (2 * UNROLL), UNROLL)
+            return 0
+
+        lax.fori_loop(0, amount // many, group, 0)
+
+        def rest(n, _):
+            multiply(start + n * (2 * FEW), FEW)
+            return 0
+
+        lax.fori_loop(amount // many * many, amount, rest, 0)
+        return 0
+
+    if not writes:
+        lax.fori_loop(0, CHUNKS, work, 0)
+        return
     part = sums.shape[0] // CHUNKS
-    for chunk in range(CHUNKS):
-
-        def multiply(group, _):
-            found = []
-            for u in range(UNROLL):
-                at = chunk * segment + (group * UNROLL + u) * 2
-                one, two = terms_ref[at], terms_ref[at + 1]
-                lhs = jnp.concatenate([blocks[one & MASK], blocks[two & MASK]], axis=1)
-                rhs = jnp.concatenate([blocks[(one >> BITS) & MASK], blocks[(two >> BITS) & MASK]], axis=0)
-                found.append(((one >> (2 * BITS)) & OUT_MASK, jnp.dot(lhs, rhs, preferred_element_type=jnp.float32)))
-            for at, value in found:
-                sums[at] += value
-            return 0
-
-        lax.fori_loop(0, count_ref[stage * CHUNKS + chunk], multiply, 0)
-        if final:
-            span = pl.ds(chunk * part, part)
-            pltpu.make_async_copy(sums.at[span], out_ref.at[span], sem).start()
+    reached = -(-LEAD // ((ext - 2 * LEAD) // CHUNKS))
+    spans = pl.ds(0, reached * part), pl.ds(reached * part, (CHUNKS - reached) * part)
+    mine = spans[0] if final else spans[1]
+    copying = pltpu.make_async_copy(sums.at[mine], out_ref.at[mine], sem)
     if final:
-        pltpu.make_async_copy(sums, out_ref, sem).wait()
+        lax.fori_loop(0, reached, work, 0)
+        copying.start()
+    else:
+        lax.fori_loop(reached, CHUNKS, work, 0)
+        copying.start()
+        lax.fori_loop(0, reached, work, 0)
+    copying.wait()
 
 
 def after_all(arrays, tokens, weight=1):
@@ -317,11 +360,11 @@
     )(*arrays, *tokens))
 
 
-def rows_of(groups, place, step, tokens, wanted, weight=1):
+def rows_of(groups, place, choice, tokens, wanted):
     arrays = [array for group in groups for array in group]
     shape = arrays[0].shape[1:]
     first_of = [sum(len(g) for g in groups[:n]) for n in range(len(groups))]
-    folds = [len(group) if step == 0 else 1 for group in groups]
+    folds = [len(group) if choice is None else 1 for group in groups]
 
     def kernel(place_ref, *refs):
         results, sem = refs[len(arrays) + len(tokens) : -1], refs[-1]
@@ -337,9 +380,9 @@
                             go(pltpu.make_async_copy(source.at[pl.ds(start, rows)], target.at[pl.ds(at, rows)], sem))
                             at += rows
                         continue
-                    for chosen, source in ((place_ref[0] >= step, sources[0]), (place_ref[0] < step, sources[1])):
-
-                        @pl.when(chosen)
+                    for n, source in enumerate(sources):
+
+                        @pl.when(pick(place_ref[0], choice) == n)
                         def _(source=source, target=target, start=start, rows=rows, at=at):
                             go(pltpu.make_async_copy(source.at[pl.ds(start, rows)], target.at[pl.ds(at, rows)], sem))
 
@@ -358,7 +401,7 @@
         out_specs=[ANY] * len(wanted),
         scratch_shapes=[pltpu.SemaphoreType.DMA],
         compiler_params=SMALL,
-        cost_estimate=quick(weight),
+        cost_estimate=quick(1),
         name="rows_of",
     )(place, *arrays, *tokens))
 
@@ -379,35 +422,35 @@
     plans = {stage: [] for stage in range(STAGES)}
     pieces = {stage: [] for stage in range(STAGES)}
 
-    def keep(stage, array, source, rows, target, shift):
-        plans[stage].append((source, rows, target, shift))
+    def keep(stage, array, source, rows, target, owners):
+        plans[stage].append((source, rows, target, owners))
         pieces[stage].append(array)
 
-    def trade(array, by, shifts, step):
+    def trade(array, by, holders, step):
         kind, target = (AFTER, LEAD + row_count) if by < 0 else (BEFORE, 0)
         moved = row_shift(array, by)
-        for n, shift in enumerate(shifts):
-            keep(stage_of(step, last, kind), moved, n * LEAD, LEAD, target, shift)
+        for n, owners in enumerate(holders):
+            keep(stage_of(step, last, kind), moved, n * LEAD, LEAD, target, owners)
 
     place = jnp.stack([me, first_row])
     state = []
 
     def run(stage):
         count = len(pieces[stage])
-        final = stage == STAGES - 1
-        given = state[:-1]
+        final, writes = stage == STAGES - 1, stage >= STAGES - 2
+        given = state if final else state[:2]
         state[:] = pl.pallas_call(
             functools.partial(stage_kernel, stage, tuple(plans[stage]), ext, size, own, segment),
             out_shape=[
                 pltpu.VMEM(((2 * ext + 1) * slots, tile, tile), dtype),
                 pltpu.VMEM((out_count, tile, tile), jnp.float32),
                 jax.ShapeDtypeStruct((out_count, tile, tile), jnp.float32)
-                if final
+                if writes
                 else jax.ShapeDtypeStruct((1,), jnp.int32),
             ],
-            in_specs=[SMEM, SMEM, HBM] + [HBM] * count + [VMEM] * len(given),
-            out_specs=[VMEM, VMEM, HBM if final else SMEM],
-            input_output_aliases={3 + count + n: n for n in range(len(given))},
+            in_specs=[SMEM, HBM] + [HBM] * count + [VMEM, VMEM, HBM][: len(given)],
+            out_specs=[VMEM, VMEM, HBM if writes else SMEM],
+            input_output_aliases={2 + count + n: n for n in range(len(given))},
             scratch_shapes=[
                 pltpu.SemaphoreType.DMA,
                 pltpu.SMEM((CHUNKS * segment,), jnp.int32),
@@ -416,14 +459,15 @@
             compiler_params=pltpu.CompilerParams(vmem_limit_bytes=4 << 20),
             cost_estimate=quick(WEIGHTS[stage]),
             name=f"stage_{stage}",
-        )(place, *lists, *pieces[stage], *given)
+        )(*lists, *pieces[stage], *given)
         return state[-1]
 
     low, high, middle = (0, LEAD), (row_count - LEAD, row_count), (LEAD, row_count - LEAD)
-    keep(0, block_values, 0, row_count, LEAD, 0)
-    low_rows, high_rows = rows_of([[block_values]], place, 0, [], [[(0, *low)], [(0, *high)]])
-    trade(low_rows, -1, (0,), 0)
-    trade(high_rows, 1, (0,), 0)
+    itself = tuple(range(size))
+    keep(0, block_values, 0, row_count, LEAD, itself)
+    low_rows, high_rows = rows_of([[block_values]], place, None, [], [[(0, *low)], [(0, *high)]])
+    trade(low_rows, -1, (itself,), 0)
+    trade(high_rows, 1, (itself,), 0)
 
     devices = size * lax.axis_size("rows")
     spread = jnp.pad(block_columns.T.reshape(-1), (0, TABLE - own * row_count))
@@ -432,7 +476,7 @@
     lists = pl.pallas_call(
         functools.partial(list_kernel, row_count, own, wanted_slots, size, row_count * lax.axis_size("rows")),
         out_shape=[
-            jax.ShapeDtypeStruct((STAGES * CHUNKS,), jnp.int32),
+            jax.ShapeDtypeStruct((STAGES * CHUNKS + 1,), jnp.int32),
             jax.ShapeDtypeStruct(((STAGES * CHUNKS + 2) * segment,), jnp.int32),
         ],
         in_specs=[SMEM, SMEM, HBM],
@@ -448,37 +492,51 @@
         name="lists",
     )(place, product_columns.T, tables)
 
-    moving = [block_values, block_values]
-    for step in range(1, last):
-        ups, downs = up_pairs(size, step), down_pairs(size, step)
-        if 2 * (step - 1) > last and len(moving) == 2:
-            moving = rows_of([moving], place, step - 1, [], [[(0, 0, row_count)]])
-        pairs = [ups, downs] if len(moving) == 2 else [ups + downs]
-        moving = [lax.ppermute(array, "cols", pair) for array, pair in zip(moving, pairs)]
+    def steps():
+        if size == 4:
+            yield [(0, [(0, 1), (1, 0), (2, 3), (3, 2)], (1, 0, 3, 2)), (0, [(1, 2), (2, 1)], (-1, 2, 1, -1))]
+            yield [(1, [(1, 0), (2, 3)], (2, -1, -1, 1)), (0, [(1, 2), (2, 1)], (-1, 3, 0, -1))]
+            return
+        for step in range(1, last):
+            below, above = from_below(size, step), from_above(size, step)
+            ups, downs = up_pairs(size, step), down_pairs(size, step)
+            if 2 * (step - 1) > last:
+                yield [(0, ups + downs, either(below, above))]
+            else:
+                yield [(0, ups, below), (-1, downs, above)]
+
+    moving = [block_values]
+    for step, moves in enumerate(steps(), 1):
+        if len(moves) < len(moving):
+            moving = rows_of([moving], place, choice, [], [[(0, 0, row_count)]])
+        moving = [lax.ppermute(moving[source], "cols", pairs) for source, pairs, _ in moves]
         if step == 1:
             moving = after_all(moving, [tables, *pieces[0][-2:]])
-        shifts = (-step, step) if len(moving) == 2 else ((step,),)
-        for array, shift in zip(moving, shifts):
-            keep(stage_of(step, last, LOW), array, 0, row_count, LEAD, shift)
+        holders = [owners for _, _, owners in moves]
+        choice = tuple(max(range(len(holders)), key=lambda n: holders[n][i]) for i in range(size))
+        for array, owners in zip(moving, holders):
+            keep(stage_of(step, last, LOW), array, 0, row_count, LEAD, owners)
+        if 2 * step > last:
+            holders = [functools.reduce(either, holders)]
         if step < last - 1:
-            shifts, way = (((step,),), step) if 2 * step > last else ((-step, step), 0)
+            way = choice if 2 * step > last else None
             low_rows, high_rows = rows_of([moving], place, way, [], [[(0, *low)], [(0, *high)]])
-            trade(low_rows, -1, shifts, step)
-            trade(high_rows, 1, shifts, step)
-
-    step = last - 1
-    parts = rows_of([moving], place, step, [run(0)], [[(0, *low)], [(0, *high)], [(0, *middle)]])
+            trade(low_rows, -1, holders, step)
+            trade(high_rows, 1, holders, step)
+
+    parts = rows_of([moving], place, choice, [run(0)], [[(0, *low)], [(0, *high)], [(0, *middle)]])
     pairs = up_pairs(size, last) + down_pairs(size, last)
     arrived = [lax.ppermute(array, "cols", pairs) for array in parts]
-    trade(parts[0], -1, ((step,),), step)
-    trade(parts[1], 1, ((step,),), step)
+    trade(parts[0], -1, holders, step)
+    trade(parts[1], 1, holders, step)
+    holders = [either(from_below(size, last), from_above(size, last))]
     arrived[:1] = after_all(arrived[:1], [run(1)], EARLY)
-    keep(stage_of(last, last, LOW), arrived[0], 0, LEAD, LEAD, (last,))
-    trade(arrived[0], -1, ((last,),), last)
+    keep(stage_of(last, last, LOW), arrived[0], 0, LEAD, LEAD, holders[0])
+    trade(arrived[0], -1, holders, last)
     arrived[1:2] = after_all(arrived[1:2], [run(2)])
-    keep(stage_of(last, last, HIGH), arrived[1], 0, LEAD, row_count, (last,))
-    trade(arrived[1], 1, ((last,),), last)
-    keep(stage_of(last, last, MIDDLE), arrived[2], 0, row_count - 2 * LEAD, 2 * LEAD, (last,))
+    keep(stage_of(last, last, HIGH), arrived[1], 0, LEAD, row_count, holders[0])
+    trade(arrived[1], 1, holders, last)
+    keep(stage_of(last, last, MIDDLE), arrived[2], 0, row_count - 2 * LEAD, 2 * LEAD, holders[0])
     for stage in range(3, STAGES):
         run(stage)
     return state[-1].reshape(row_count, wanted_slots, tile, tile)

time: 135 us -> 132 us (0.978)
  starting transfers between devices: 38.2 us -> 32.4 us
  waiting for transfers between devices: 8.06 us -> 10.9 us
    ppermute x3, waiting for transfers between devices: 3.54 us -> 10.1 us  [body(): arrived = [lax.ppermute(array, 'cols', pairs) for array in parts]]
    ppermute x8, starting transfers between devices: 26.1 us -> 20.9 us  [row_shift(): lax.ppermute(array, 'rows', [(i, i + by) for i in range(size) if 0 <= i +...]
    ppermute x4, waiting for transfers between devices: 4.5 us -> 0.82 us  [body(): lax.ppermute(moving[source], 'cols', pairs)]
  transfers between devices with their start and end apart: 15 -> 15, of which waited for: 3 -> 4; matrix products, arithmetic and copies ran while one was open for 1% -> 1% of each run, Pallas kernels for 40% -> 41%
where the time goes in v4:
time: 132 us; the launch traced here: 131 us
  Pallas kernels  57.5 us (44%)
  starting transfers between devices  32.4 us (25%)
  blocking collectives  27.9 us (21%)
  waiting for transfers between devices  10.9 us (8%)
  local copies, waits for them, and re-layouts  2.19 us (2%)
    pallas_call x6, Pallas kernels, run(): pl.pallas_call(functools.partial(stage_kernel, stage, tuple(plans[stage])...  32.1 us
    all_to_all x1, blocking collectives, body(): lax.all_to_all(spread, ('rows', 'cols'), 0, 0, tiled=True).reshape(-1)  27.9 us
    ppermute x8, starting transfers between devices, row_shift(): lax.ppermute(array, 'rows', [(i, i + by) for i in range(size) if 0 <= i +...  20.9 us
    pallas_call x1, Pallas kernels, body(): pl.pallas_call(functools.partial(list_kernel, row_count, own, wanted_slot...  19.8 us
    ppermute x3, waiting for transfers between devices, body(): arrived = [lax.ppermute(array, 'cols', pairs) for array in parts]  10.1 us
    ppermute x4, starting transfers between devices, body(): lax.ppermute(moving[source], 'cols', pairs)  7.57 us
    pallas_call x3, Pallas kernels, rows_of(): pl.pallas_call(kernel, out_shape=[jax.ShapeDtypeStruct((sum((folds[g] * (...  4.34 us
    ppermute x3, starting transfers between devices, body(): arrived = [lax.ppermute(array, 'cols', pairs) for array in parts]  3.88 us
  transfers between devices with their start and end apart: 15, of which 4 were waited for; matrix products, arithmetic and copies ran while one was open for 1% of the time, Pallas kernels for 41%

profile of v4, /device:TPU:1, one launch (start us, length us, event | category | flops | bytes accessed | tf_op | source)
XLA Modules:
  0.0 131.4 jit_solution(1030000126345996812)
XLA Ops:
  0.0 0.9 collective-permute-start.1
  0.9 4.6 %collective-permute-start = (bf16[24,2,128,128]{3,2,1,0:T(8,128)(2,1)}, bf16[24,2,128,128]{3,2,1,0:T(8,128)(2,1)S(1)}, u32[]{:S(2)}, u32[]{:S(2)}) collective-permute-start(bf16[24,2,128,128]{3,2,1,0:T(8,128)(2,1)} %refs_0_.3), channel_id=1, source_target_pairs={{0,1},{1,0},{2,3},{3,2},{4,5},{5,4},{6,7},{7,6},{8,9},{9,8},{10,11... | collective-permute-start | bytes 4718600 | tf_op jit(solution)/shard_map/ppermute | solution.py:512
  5.5 0.1 pad_add_fusion.place_ref
  5.6 1.4 %copy-done = bf16[24,2,128,128]{3,2,1,0:T(8,128)(2,1)S(1)} copy-done((bf16[24,2,128,128]{3,2,1,0:T(8,128)(2,1)S(1)}, bf16[24,2,128,128]{3,2,1,0:T(8,128)(2,1)}, u32[]{:S(2)}) %copy-start) | copy-done | bytes 1572888
  7.0 1.6 %rows_of.3 = (bf16[9,2,128,128]{3,2,1,0:T(8,128)(2,1)}, bf16[9,2,128,128]{3,2,1,0:T(8,128)(2,1)}) custom-call(s32[2]{0:T(128)S(1)} %pad_add_fusion.place_ref, bf16[24,2,128,128]{3,2,1,0:T(8,128)(2,1)S(1)} %copy-done), custom_call_target="tpu_custom_call" | custom-call | flops 1 | bytes 1 | tf_op jit(solution)/shard_map/rows_of/pallas_call | solution.py:394
  8.6 3.1 %collective-permute-start.2 = (bf16[9,2,128,128]{3,2,1,0:T(8,128)(2,1)}, bf16[9,2,128,128]{3,2,1,0:T(8,128)(2,1)}, u32[]{:S(2)}, u32[]{:S(2)}) collective-permute-start(bf16[9,2,128,128]{3,2,1,0:T(8,128)(2,1)} %get-tuple-element.33), channel_id=1, source_target_pairs={{4,0},{8,4},{12,8},{5,1},{9,5},{13,9},{6,2},{10,6},{14,10},{7,3},{... | collective-permute-start | bytes 1769480 | tf_op jit(solution)/shard_map/ppermute | solution.py:79
  11.8 3.0 %collective-permute-start.3 = (bf16[9,2,128,128]{3,2,1,0:T(8,128)(2,1)}, bf16[9,2,128,128]{3,2,1,0:T(8,128)(2,1)}, u32[]{:S(2)}, u32[]{:S(2)}) collective-permute-start(bf16[9,2,128,128]{3,2,1,0:T(8,128)(2,1)} %get-tuple-element.34), channel_id=1, source_target_pairs={{0,4},{4,8},{8,12},{1,5},{5,9},{9,13},{2,6},{6,10},{10,14},{3,7},{... | collective-permute-start | bytes 1769480 | tf_op jit(solution)/shard_map/ppermute | solution.py:79
  14.8 0.8 reshape.11
  15.6 27.9 %all_to_all.5 = s32[16,8,128]{2,1,0:T(8,128)S(1)} all-to-all(s32[16,8,128]{2,1,0:T(8,128)S(1)} %broadcast_in_dim.8), channel_id=1, replica_groups=mesh['groups'=2,'rows'=4,'cols'=4] {'rows','cols'}, dimensions={0} | all-to-all | bytes 131072 | tf_op jit(solution)/shard_map/all_to_all | solution.py:475
  43.5 0.0 collective-permute-done.2.refs_3_.refs_1_
  43.5 0.0 collective-permute-done.3.refs_4_.refs_2_
  43.5 0.0 collective-permute-done.1.refs_1_
  43.5 0.0 collective-permute-done.refs_0_
  43.5 1.3 collective-permute-start.4
  44.8 0.8 collective-permute-start.5
  45.6 1.0 rows_of.5
  46.6 2.3 %collective-permute-start.10 = (bf16[18,2,128,128]{3,2,1,0:T(8,128)(2,1)S(1)}, bf16[18,2,128,128]{3,2,1,0:T(8,128)(2,1)S(1)}, u32[]{:S(2)}, u32[]{:S(2)}) collective-permute-start(bf16[18,2,128,128]{3,2,1,0:T(8,128)(2,1)S(1)} %get-tuple-element.40), channel_id=1, source_target_pairs={{4,0},{8,4},{12,8},{5,1},{9,5},{13,9},{6,2},{10,6},{14,10},{7,3},{... | collective-permute-start | bytes 3538952 | tf_op jit(solution)/shard_map/ppermute | solution.py:79
  48.9 3.3 %collective-permute-start.11 = (bf16[18,2,128,128]{3,2,1,0:T(8,128)(2,1)S(1)}, bf16[18,2,128,128]{3,2,1,0:T(8,128)(2,1)S(1)}, u32[]{:S(2)}, u32[]{:S(2)}) collective-permute-start(bf16[18,2,128,128]{3,2,1,0:T(8,128)(2,1)S(1)} %get-tuple-element.41), channel_id=1, source_target_pairs={{0,4},{4,8},{8,12},{1,5},{5,9},{9,13},{2,6},{6,10},{10,14},{3,7},{... | collective-permute-start | bytes 3538952 | tf_op jit(solution)/shard_map/ppermute | solution.py:79
  52.2 0.0 copy-done.2
  52.2 19.8 %lists.1 = (s32[25]{0:T(128)S(1)}, s32[13312]{0:T(1024)S(1)}) custom-call(s32[2]{0:T(128)S(1)} %pad_add_fusion.place_ref, s32[4,24]{1,0:T(4,128)S(1)} %bitcast.10, s32[16384]{0:T(1024)S(1)} %bitcast.9), custom_call_target="tpu_custom_call" | custom-call | flops 1 | bytes 1 | tf_op jit(solution)/shard_map/lists/pallas_call | solution.py:476
  72.0 0.0 copy-done.1
  72.0 8.2 %stage_0.1 = (bf16[680,128,128]{2,1,0:T(8,128)(2,1)S(1)}, f32[96,128,128]{2,1,0:T(8,128)S(1)}, s32[1]{0:T(128)}) custom-call(s32[25]{0:T(128)S(1)} %get-tuple-element.31.count_ref, s32[13312]{0:T(1024)S(1)} %get-tuple-element.32.terms_hbm, bf16[24,2,128,128]{3,2,1,0:T(8,128)(2,1)S(1)} %copy-done.1, ...), custom_call_target="tpu_custom_call" | custom-call | flops 1 | bytes 1 | tf_op jit(solution)/shard_map/stage_0/pallas_call | solution.py:442
  80.2 0.8 collective-permute-done.4.refs_0_.refs_4_
  81.0 0.0 collective-permute-done.5.refs_1_.refs_5_
  81.0 1.7 %rows_of.4 = (bf16[9,2,128,128]{3,2,1,0:T(8,128)(2,1)S(1)}, bf16[9,2,128,128]{3,2,1,0:T(8,128)(2,1)S(1)}, bf16[6,2,128,128]{3,2,1,0:T(8,128)(2,1)S(1)}) custom-call(s32[2]{0:T(128)S(1)} %pad_add_fusion.place_ref, bf16[24,2,128,128]{3,2,1,0:T(8,128)(2,1)S(1)} %collective-permute-done.4.refs_0_.refs_4_, ...), custom_call_target="tpu_custom_call" | custom-call | flops 1 | bytes 1 | tf_op jit(solution)/shard_map/rows_of/pallas_call | solution.py:394
  82.7 1.3 collective-permute-start.9
  84.0 3.3 %collective-permute-start.8 = (bf16[9,2,128,128]{3,2,1,0:T(8,128)(2,1)S(1)}, bf16[9,2,128,128]{3,2,1,0:T(8,128)(2,1)S(1)}, u32[]{:S(2)}, u32[]{:S(2)}) collective-permute-start(bf16[9,2,128,128]{3,2,1,0:T(8,128)(2,1)S(1)} %get-tuple-element.38), channel_id=1, source_target_pairs={{0,4},{4,8},{8,12},{1,5},{5,9},{9,13},{2,6},{6,10},{10,14},{3,7},{... | collective-permute-start | bytes 1769480 | tf_op jit(solution)/shard_map/ppermute | solution.py:79
  87.3 1.3 collective-permute-start.6
  88.6 0.0 collective-permute-done.10.refs_0_.refs_1_
  88.6 1.9 %collective-permute-start.7 = (bf16[9,2,128,128]{3,2,1,0:T(8,128)(2,1)S(1)}, bf16[9,2,128,128]{3,2,1,0:T(8,128)(2,1)S(1)}, u32[]{:S(2)}, u32[]{:S(2)}) collective-permute-start(bf16[9,2,128,128]{3,2,1,0:T(8,128)(2,1)S(1)} %get-tuple-element.39), channel_id=1, source_target_pairs={{4,0},{8,4},{12,8},{5,1},{9,5},{13,9},{6,2},{10,6},{14,10},{7,3},{... | collective-permute-start | bytes 1769480 | tf_op jit(solution)/shard_map/ppermute | solution.py:79
  90.5 0.0 collective-permute-done.11.refs_2_.refs_3_
  90.5 6.7 %stage_1.1 = (bf16[680,128,128]{2,1,0:T(8,128)(2,1)S(1)}, f32[96,128,128]{2,1,0:T(8,128)S(1)}, s32[1]{0:T(128)}) custom-call(s32[25]{0:T(128)S(1)} %get-tuple-element.31.count_ref, s32[13312]{0:T(1024)S(1)} %get-tuple-element.32.terms_hbm, ...), custom_call_target="tpu_custom_call", output_to_operand_aliasing={{0}: (8, {}), {1}: (9, {})} | custom-call | flops 1 | bytes 1 | tf_op jit(solution)/shard_map/stage_1/pallas_call | solution.py:442
  97.2 6.1 %collective-permute-done.9.refs_0_ = bf16[9,2,128,128]{3,2,1,0:T(8,128)(2,1)S(1)} collective-permute-done((bf16[9,2,128,128]{3,2,1,0:T(8,128)(2,1)S(1)}, bf16[9,2,128,128]{3,2,1,0:T(8,128)(2,1)S(1)}, u32[]{:S(2)}, u32[]{:S(2)}) %collective-permute-start.9) | collective-permute-done | bytes 589856 | tf_op jit(solution)/shard_map/ppermute | solution.py:529
  103.3 0.6 after_all.4.refs_2_
  104.0 1.9 %collective-permute-start.14 = (bf16[9,2,128,128]{3,2,1,0:T(8,128)(2,1)S(1)}, bf16[9,2,128,128]{3,2,1,0:T(8,128)(2,1)S(1)}, u32[]{:S(2)}, u32[]{:S(2)}) collective-permute-start(bf16[9,2,128,128]{3,2,1,0:T(8,128)(2,1)S(1)} %after_all.4.refs_2_), channel_id=1, source_target_pairs={{4,0},{8,4},{12,8},{5,1},{9,5},{13,9},{6,2},{10,6},{14,10},{7,3},{... | collective-permute-start | bytes 1769480 | tf_op jit(solution)/shard_map/ppermute | solution.py:79
  105.9 1.3 collective-permute-start.13
  107.2 0.0 collective-permute-done.8.refs_1_
  107.2 0.0 collective-permute-done.7.refs_0_
  107.2 5.0 %stage_2.1 = (bf16[680,128,128]{2,1,0:T(8,128)(2,1)S(1)}, f32[96,128,128]{2,1,0:T(8,128)S(1)}, s32[1]{0:T(128)}) custom-call(s32[25]{0:T(128)S(1)} %get-tuple-element.31.count_ref, s32[13312]{0:T(1024)S(1)} %get-tuple-element.32.terms_hbm, bf16[9,2,128,128]{3,2,1,0:T(8,128)(2,1)S(1)} %collective-permute-done.7.refs_0_, ...), custom_call_target="tpu_custom_call", output_to_operand_aliasing={{0}: (5, {}), {1}: (6, {})} | custom-call | flops 1 | bytes 1 | tf_op jit(solution)/shard_map/stage_2/pallas_call | solution.py:442
  112.2 3.8 %collective-permute-done.6.refs_0_ = bf16[9,2,128,128]{3,2,1,0:T(8,128)(2,1)S(1)} collective-permute-done((bf16[9,2,128,128]{3,2,1,0:T(8,128)(2,1)S(1)}, bf16[9,2,128,128]{3,2,1,0:T(8,128)(2,1)S(1)}, u32[]{:S(2)}, u32[]{:S(2)}) %collective-permute-start.6) | collective-permute-done | bytes 589856 | tf_op jit(solution)/shard_map/ppermute | solution.py:529
  116.0 0.6 after_all.5.refs_1_
  116.6 2.1 %collective-permute-start.12 = (bf16[9,2,128,128]{3,2,1,0:T(8,128)(2,1)S(1)}, bf16[9,2,128,128]{3,2,1,0:T(8,128)(2,1)S(1)}, u32[]{:S(2)}, u32[]{:S(2)}) collective-permute-start(bf16[9,2,128,128]{3,2,1,0:T(8,128)(2,1)S(1)} %after_all.5.refs_1_), channel_id=1, source_target_pairs={{0,4},{4,8},{8,12},{1,5},{5,9},{9,13},{2,6},{6,10},{10,14},{3,7},{... | collective-permute-start | bytes 1769480 | tf_op jit(solution)/shard_map/ppermute | solution.py:79
  118.7 0.0 collective-permute-done.14.refs_0_
  118.7 4.6 %stage_3.1 = (bf16[680,128,128]{2,1,0:T(8,128)(2,1)S(1)}, f32[96,128,128]{2,1,0:T(8,128)S(1)}, s32[1]{0:T(128)}) custom-call(s32[25]{0:T(128)S(1)} %get-tuple-element.31.count_ref, s32[13312]{0:T(1024)S(1)} %get-tuple-element.32.terms_hbm, ...), custom_call_target="tpu_custom_call", output_to_operand_aliasing={{0}: (4, {}), {1}: (5, {})} | custom-call | flops 1 | bytes 1 | tf_op jit(solution)/shard_map/stage_3/pallas_call | solution.py:442
  123.3 0.2 collective-permute-done.13.refs_0_
  123.5 4.0 %stage_4.1 = (bf16[680,128,128]{2,1,0:T(8,128)(2,1)S(1)}, f32[96,128,128]{2,1,0:T(8,128)S(1)}, f32[96,128,128]{2,1,0:T(8,128)}) custom-call(s32[25]{0:T(128)S(1)} %get-tuple-element.31.count_ref, s32[13312]{0:T(1024)S(1)} %get-tuple-element.32.terms_hbm, ...), custom_call_target="tpu_custom_call", output_to_operand_aliasing={{0}: (3, {}), {1}: (4, {})} | custom-call | flops 4294967296 | bytes 4294967296 | tf_op jit(solution)/shard_map/stage_4/pallas_call | solution.py:442
  127.5 0.0 collective-permute-done.12.refs_0_
  127.5 3.7 %stage_5.1 = (bf16[680,128,128]{2,1,0:T(8,128)(2,1)S(1)}, f32[96,128,128]{2,1,0:T(8,128)S(1)}, f32[96,128,128]{2,1,0:T(8,128)}) custom-call(s32[25]{0:T(128)S(1)} %get-tuple-element.31.count_ref, s32[13312]{0:T(1024)S(1)} %get-tuple-element.32.terms_hbm, ...), custom_call_target="tpu_custom_call", output_to_operand_aliasing={{0}: (3, {}), {1}: (4, {}), {2}: (5, {})} | custom-call | flops 1 | bytes 1 | tf_op jit(solution)/shard_map/stage_5/pallas_call | solution.py:442
  (6 shorter events, 0.0 us)
Async XLA Ops:
  0.0 52.2 %copy-start.2 = (s32[24,4]{0,1:T(4,128)S(1)}, s32[24,4]{0,1:T(4,128)}, u32[]{:S(2)}) copy-start(s32[24,4]{0,1:T(4,128)} %param.5) | copy-start | bytes 1156
  0.0 43.5 %collective-permute-start.1 = (bf16[24,2,128,128]{3,2,1,0:T(8,128)(2,1)}, bf16[24,2,128,128]{3,2,1,0:T(8,128)(2,1)S(1)}, u32[]{:S(2)}, u32[]{:S(2)}) collective-permute-start(bf16[24,2,128,128]{3,2,1,0:T(8,128)(2,1)} %refs_0_.3), channel_id=1, source_target_pairs={{1,2},{2,1},{5,6},{6,5},{9,10},{10,9},{13,14},{14,13},{17,18},{18,... | collective-permute-start | bytes 4718600 | tf_op jit(solution)/shard_map/ppermute | solution.py:512
  0.9 42.6 %collective-permute-start = (bf16[24,2,128,128]{3,2,1,0:T(8,128)(2,1)}, bf16[24,2,128,128]{3,2,1,0:T(8,128)(2,1)S(1)}, u32[]{:S(2)}, u32[]{:S(2)}) collective-permute-start(bf16[24,2,128,128]{3,2,1,0:T(8,128)(2,1)} %refs_0_.3), channel_id=1, source_target_pairs={{0,1},{1,0},{2,3},{3,2},{4,5},{5,4},{6,7},{7,6},{8,9},{9,8},{10,11... | collective-permute-start | bytes 4718600 | tf_op jit(solution)/shard_map/ppermute | solution.py:512
  5.6 1.4 %copy-start = (bf16[24,2,128,128]{3,2,1,0:T(8,128)(2,1)S(1)}, bf16[24,2,128,128]{3,2,1,0:T(8,128)(2,1)}, u32[]{:S(2)}) copy-start(bf16[24,2,128,128]{3,2,1,0:T(8,128)(2,1)} %refs_0_.3) | copy-start | bytes 4718596
  8.6 34.9 %collective-permute-start.2 = (bf16[9,2,128,128]{3,2,1,0:T(8,128)(2,1)}, bf16[9,2,128,128]{3,2,1,0:T(8,128)(2,1)}, u32[]{:S(2)}, u32[]{:S(2)}) collective-permute-start(bf16[9,2,128,128]{3,2,1,0:T(8,128)(2,1)} %get-tuple-element.33), channel_id=1, source_target_pairs={{4,0},{8,4},{12,8},{5,1},{9,5},{13,9},{6,2},{10,6},{14,10},{7,3},{... | collective-permute-start | bytes 1769480 | tf_op jit(solution)/shard_map/ppermute | solution.py:79
  11.8 31.7 %collective-permute-start.3 = (bf16[9,2,128,128]{3,2,1,0:T(8,128)(2,1)}, bf16[9,2,128,128]{3,2,1,0:T(8,128)(2,1)}, u32[]{:S(2)}, u32[]{:S(2)}) collective-permute-start(bf16[9,2,128,128]{3,2,1,0:T(8,128)(2,1)} %get-tuple-element.34), channel_id=1, source_target_pairs={{0,4},{4,8},{8,12},{1,5},{5,9},{9,13},{2,6},{6,10},{10,14},{3,7},{... | collective-permute-start | bytes 1769480 | tf_op jit(solution)/shard_map/ppermute | solution.py:79
  15.5 56.4 %copy-start.1 = (bf16[24,2,128,128]{3,2,1,0:T(8,128)(2,1)S(1)}, bf16[24,2,128,128]{3,2,1,0:T(8,128)(2,1)}, u32[]{:S(2)}) copy-start(bf16[24,2,128,128]{3,2,1,0:T(8,128)(2,1)} %refs_0_.3) | copy-start | bytes 4718596
  43.5 37.5 %collective-permute-start.4 = (bf16[24,2,128,128]{3,2,1,0:T(8,128)(2,1)S(1)}, bf16[24,2,128,128]{3,2,1,0:T(8,128)(2,1)S(1)}, u32[]{:S(2)}, u32[]{:S(2)}) collective-permute-start(bf16[24,2,128,128]{3,2,1,0:T(8,128)(2,1)S(1)} %get-tuple-element.35.refs_4_.refs_1_), channel_id=1, source_target_pairs={{1,0},{2,3},{5,4},{6,7},{9,8},{10,11},{13,12},{14,15},{17,16},{18,... | collective-permute-start | bytes 4718600 | tf_op jit(solution)/shard_map/ppermute | solution.py:512
  44.8 36.2 %collective-permute-start.5 = (bf16[24,2,128,128]{3,2,1,0:T(8,128)(2,1)S(1)}, bf16[24,2,128,128]{3,2,1,0:T(8,128)(2,1)S(1)}, u32[]{:S(2)}, u32[]{:S(2)}) collective-permute-start(bf16[24,2,128,128]{3,2,1,0:T(8,128)(2,1)S(1)} %get-tuple-element.36.refs_3_.refs_0_), channel_id=1, source_target_pairs={{1,2},{2,1},{5,6},{6,5},{9,10},{10,9},{13,14},{14,13},{17,18},{18,... | collective-permute-start | bytes 4718600 | tf_op jit(solution)/shard_map/ppermute | solution.py:512
  46.6 42.0 %collective-permute-start.10 = (bf16[18,2,128,128]{3,2,1,0:T(8,128)(2,1)S(1)}, bf16[18,2,128,128]{3,2,1,0:T(8,128)(2,1)S(1)}, u32[]{:S(2)}, u32[]{:S(2)}) collective-permute-start(bf16[18,2,128,128]{3,2,1,0:T(8,128)(2,1)S(1)} %get-tuple-element.40), channel_id=1, source_target_pairs={{4,0},{8,4},{12,8},{5,1},{9,5},{13,9},{6,2},{10,6},{14,10},{7,3},{... | collective-permute-start | bytes 3538952 | tf_op jit(solution)/shard_map/ppermute | solution.py:79
  48.9 41.6 %collective-permute-start.11 = (bf16[18,2,128,128]{3,2,1,0:T(8,128)(2,1)S(1)}, bf16[18,2,128,128]{3,2,1,0:T(8,128)(2,1)S(1)}, u32[]{:S(2)}, u32[]{:S(2)}) collective-permute-start(bf16[18,2,128,128]{3,2,1,0:T(8,128)(2,1)S(1)} %get-tuple-element.41), channel_id=1, source_target_pairs={{0,4},{4,8},{8,12},{1,5},{5,9},{9,13},{2,6},{6,10},{10,14},{3,7},{... | collective-permute-start | bytes 3538952 | tf_op jit(solution)/shard_map/ppermute | solution.py:79
  82.7 20.6 %collective-permute-start.9 = (bf16[9,2,128,128]{3,2,1,0:T(8,128)(2,1)S(1)}, bf16[9,2,128,128]{3,2,1,0:T(8,128)(2,1)S(1)}, u32[]{:S(2)}, u32[]{:S(2)}) collective-permute-start(bf16[9,2,128,128]{3,2,1,0:T(8,128)(2,1)S(1)} %get-tuple-element.39), channel_id=1, source_target_pairs={{2,3},{1,0},{6,7},{5,4},{10,11},{9,8},{14,15},{13,12},{18,19},{17,... | collective-permute-start | bytes 1769480 | tf_op jit(solution)/shard_map/ppermute | solution.py:529
  84.0 23.2 %collective-permute-start.8 = (bf16[9,2,128,128]{3,2,1,0:T(8,128)(2,1)S(1)}, bf16[9,2,128,128]{3,2,1,0:T(8,128)(2,1)S(1)}, u32[]{:S(2)}, u32[]{:S(2)}) collective-permute-start(bf16[9,2,128,128]{3,2,1,0:T(8,128)(2,1)S(1)} %get-tuple-element.38), channel_id=1, source_target_pairs={{0,4},{4,8},{8,12},{1,5},{5,9},{9,13},{2,6},{6,10},{10,14},{3,7},{... | collective-permute-start | bytes 1769480 | tf_op jit(solution)/shard_map/ppermute | solution.py:79
  87.3 28.7 %collective-permute-start.6 = (bf16[9,2,128,128]{3,2,1,0:T(8,128)(2,1)S(1)}, bf16[9,2,128,128]{3,2,1,0:T(8,128)(2,1)S(1)}, u32[]{:S(2)}, u32[]{:S(2)}) collective-permute-start(bf16[9,2,128,128]{3,2,1,0:T(8,128)(2,1)S(1)} %get-tuple-element.38), channel_id=1, source_target_pairs={{2,3},{1,0},{6,7},{5,4},{10,11},{9,8},{14,15},{13,12},{18,19},{17,... | collective-permute-start | bytes 1769480 | tf_op jit(solution)/shard_map/ppermute | solution.py:529
  88.6 18.6 %collective-permute-start.7 = (bf16[9,2,128,128]{3,2,1,0:T(8,128)(2,1)S(1)}, bf16[9,2,128,128]{3,2,1,0:T(8,128)(2,1)S(1)}, u32[]{:S(2)}, u32[]{:S(2)}) collective-permute-start(bf16[9,2,128,128]{3,2,1,0:T(8,128)(2,1)S(1)} %get-tuple-element.39), channel_id=1, source_target_pairs={{4,0},{8,4},{12,8},{5,1},{9,5},{13,9},{6,2},{10,6},{14,10},{7,3},{... | collective-permute-start | bytes 1769480 | tf_op jit(solution)/shard_map/ppermute | solution.py:79
  104.0 14.7 %collective-permute-start.14 = (bf16[9,2,128,128]{3,2,1,0:T(8,128)(2,1)S(1)}, bf16[9,2,128,128]{3,2,1,0:T(8,128)(2,1)S(1)}, u32[]{:S(2)}, u32[]{:S(2)}) collective-permute-start(bf16[9,2,128,128]{3,2,1,0:T(8,128)(2,1)S(1)} %after_all.4.refs_2_), channel_id=1, source_target_pairs={{4,0},{8,4},{12,8},{5,1},{9,5},{13,9},{6,2},{10,6},{14,10},{7,3},{... | collective-permute-start | bytes 1769480 | tf_op jit(solution)/shard_map/ppermute | solution.py:79
  105.9 17.6 %collective-permute-start.13 = (bf16[6,2,128,128]{3,2,1,0:T(8,128)(2,1)S(1)}, bf16[6,2,128,128]{3,2,1,0:T(8,128)(2,1)S(1)}, u32[]{:S(2)}, u32[]{:S(2)}) collective-permute-start(bf16[6,2,128,128]{3,2,1,0:T(8,128)(2,1)S(1)} %get-tuple-element.48), channel_id=1, source_target_pairs={{2,3},{1,0},{6,7},{5,4},{10,11},{9,8},{14,15},{13,12},{18,19},{17,... | collective-permute-start | bytes 1179656 | tf_op jit(solution)/shard_map/ppermute | solution.py:529
  116.6 10.9 %collective-permute-start.12 = (bf16[9,2,128,128]{3,2,1,0:T(8,128)(2,1)S(1)}, bf16[9,2,128,128]{3,2,1,0:T(8,128)(2,1)S(1)}, u32[]{:S(2)}, u32[]{:S(2)}) collective-permute-start(bf16[9,2,128,128]{3,2,1,0:T(8,128)(2,1)S(1)} %after_all.5.refs_1_), channel_id=1, source_target_pairs={{0,4},{4,8},{8,12},{1,5},{5,9},{9,13},{2,6},{6,10},{10,14},{3,7},{... | collective-permute-start | bytes 1769480 | tf_op jit(solution)/shard_map/ppermute | solution.py:79

commit v5 on v4

--- a/solution.py
+++ b/solution.py
@@ -22,7 +22,7 @@
 CHUNKS = 4
 TABLE = 1024
 WEIGHTS = {0: 1, 1: 1, 2: 1, 3: 1, 4: 1 << 32, 5: 1}
-LIST_WEIGHT = 1
+LIST_WEIGHT = 1 << 33
 EARLY = 1 << 34
 
 SMEM = pl.BlockSpec(memory_space=pltpu.SMEM)
@@ -74,9 +74,13 @@
     return found
 
 
-def row_shift(array, by):
-    size = lax.axis_size("rows")
-    return lax.ppermute(array, "rows", [(i, i + by) for i in range(size) if 0 <= i + by < size])
+def row_shift(array, by, holders):
+    rows, size = lax.axis_size("rows"), lax.axis_size("cols")
+    cols = [c for c in range(size) if any(owners[c] >= 0 for owners in holders)]
+    steps = [i for i in range(rows) if 0 <= i + by < rows]
+    if len(cols) == size:
+        return lax.ppermute(array, "rows", [(i, i + by) for i in steps])
+    return lax.ppermute(array, ("rows", "cols"), [(i * size + c, (i + by) * size + c) for i in steps for c in cols])
 
 
 def segment_size(part_rows, slot_count):
@@ -244,21 +248,22 @@
     me = count_ref[STAGES * CHUNKS]
 
     def each(go):
-        for piece, (source, rows, target, owners) in zip(pieces, plan):
+        for n, (piece, (source, rows, target, owners)) in enumerate(zip(pieces, plan)):
             owner = pick(me, owners)
 
             @pl.when(owner >= 0)
-            def _(piece=piece, source=source, rows=rows, target=target, owner=owner):
-                go(piece, source, rows, target, owner)
+            def _(n=n, piece=piece, source=source, rows=rows, target=target, owner=owner):
+                go(n, piece, source, rows, target, owner)
 
     shelf = blocks.reshape(blocks.shape[0] // slots, slots, *blocks.shape[1:])
 
-    def copy(piece, source, rows, target, owner):
+    def copy(n, piece, source, rows, target, owner):
         return pltpu.make_async_copy(
-            piece.at[pl.ds(source, rows)], shelf.at[pl.ds(target, rows), pl.ds(owner * own, own)], sem
+            piece.at[pl.ds(source, rows)], shelf.at[pl.ds(target, rows), pl.ds(owner * own, own)], sem.at[n]
         )
 
-    def turn(piece, source, rows, target, owner):
+    def turn(n, piece, source, rows, target, owner):
+        copy(n, piece, source, rows, target, owner).wait()
         pace = max(n for n in range(1, 10) if rows % n == 0)
 
         def some(group, _):
@@ -296,7 +301,6 @@
     if first:
         blocks[2 * stored] = jnp.zeros(blocks.shape[1:], blocks.dtype)
         sums[...] = jnp.zeros_like(sums)
-    each(lambda *what: copy(*what).wait())
     each(turn)
     listing.wait()
 
@@ -335,7 +339,7 @@
     reached = -(-LEAD // ((ext - 2 * LEAD) // CHUNKS))
     spans = pl.ds(0, reached * part), pl.ds(reached * part, (CHUNKS - reached) * part)
     mine = spans[0] if final else spans[1]
-    copying = pltpu.make_async_copy(sums.at[mine], out_ref.at[mine], sem)
+    copying = pltpu.make_async_copy(sums.at[mine], out_ref.at[mine], sem.at[0])
     if final:
         lax.fori_loop(0, reached, work, 0)
         copying.start()
@@ -360,7 +364,7 @@
     )(*arrays, *tokens))
 
 
-def rows_of(groups, place, choice, tokens, wanted):
+def rows_of(groups, place, choice, tokens, wanted, shifts=None):
     arrays = [array for group in groups for array in group]
     shape = arrays[0].shape[1:]
     first_of = [sum(len(g) for g in groups[:n]) for n in range(len(groups))]
@@ -374,6 +378,7 @@
                 at = 0
                 for group, start, stop in spans:
                     rows = stop - start
+                    more = shifts or {}
                     sources = refs[first_of[group] : first_of[group] + len(groups[group])]
                     if folds[group] == len(sources):
                         for source in sources:
@@ -383,7 +388,7 @@
                     for n, source in enumerate(sources):
 
                         @pl.when(pick(place_ref[0], choice) == n)
-                        def _(source=source, target=target, start=start, rows=rows, at=at):
+                        def _(source=source, target=target, start=start - more.get((group, n), 0), rows=rows, at=at):
                             go(pltpu.make_async_copy(source.at[pl.ds(start, rows)], target.at[pl.ds(at, rows)], sem))
 
                     at += rows
@@ -428,7 +433,7 @@
 
     def trade(array, by, holders, step):
         kind, target = (AFTER, LEAD + row_count) if by < 0 else (BEFORE, 0)
-        moved = row_shift(array, by)
+        moved = row_shift(array, by, holders)
         for n, owners in enumerate(holders):
             keep(stage_of(step, last, kind), moved, n * LEAD, LEAD, target, owners)
 
@@ -452,7 +457,7 @@
             out_specs=[VMEM, VMEM, HBM if writes else SMEM],
             input_output_aliases={2 + count + n: n for n in range(len(given))},
             scratch_shapes=[
-                pltpu.SemaphoreType.DMA,
+                pltpu.SemaphoreType.DMA((count,)),
                 pltpu.SMEM((CHUNKS * segment,), jnp.int32),
                 pltpu.SemaphoreType.DMA,
             ],
@@ -492,45 +497,72 @@
         name="lists",
     )(place, product_columns.T, tables)
 
-    def steps():
-        if size == 4:
-            yield [(0, [(0, 1), (1, 0), (2, 3), (3, 2)], (1, 0, 3, 2)), (0, [(1, 2), (2, 1)], (-1, 2, 1, -1))]
-            yield [(1, [(1, 0), (2, 3)], (2, -1, -1, 1)), (0, [(1, 2), (2, 1)], (-1, 3, 0, -1))]
-            return
+    pairs = up_pairs(size, last) + down_pairs(size, last)
+
+    def along_line():
+        moving = [block_values]
         for step in range(1, last):
             below, above = from_below(size, step), from_above(size, step)
             ups, downs = up_pairs(size, step), down_pairs(size, step)
             if 2 * (step - 1) > last:
-                yield [(0, ups + downs, either(below, above))]
+                if len(moving) == 2:
+                    moving = rows_of([moving], place, choice, [], [[(0, 0, row_count)]])
+                moving, holders = [lax.ppermute(moving[0], "cols", ups + downs)], [either(below, above)]
             else:
-                yield [(0, ups, below), (-1, downs, above)]
-
-    moving = [block_values]
-    for step, moves in enumerate(steps(), 1):
-        if len(moves) < len(moving):
-            moving = rows_of([moving], place, choice, [], [[(0, 0, row_count)]])
-        moving = [lax.ppermute(moving[source], "cols", pairs) for source, pairs, _ in moves]
-        if step == 1:
-            moving = after_all(moving, [tables, *pieces[0][-2:]])
-        holders = [owners for _, _, owners in moves]
-        choice = tuple(max(range(len(holders)), key=lambda n: holders[n][i]) for i in range(size))
-        for array, owners in zip(moving, holders):
-            keep(stage_of(step, last, LOW), array, 0, row_count, LEAD, owners)
-        if 2 * step > last:
-            holders = [functools.reduce(either, holders)]
-        if step < last - 1:
-            way = choice if 2 * step > last else None
-            low_rows, high_rows = rows_of([moving], place, way, [], [[(0, *low)], [(0, *high)]])
-            trade(low_rows, -1, holders, step)
-            trade(high_rows, 1, holders, step)
-
-    parts = rows_of([moving], place, choice, [run(0)], [[(0, *low)], [(0, *high)], [(0, *middle)]])
-    pairs = up_pairs(size, last) + down_pairs(size, last)
-    arrived = [lax.ppermute(array, "cols", pairs) for array in parts]
-    trade(parts[0], -1, holders, step)
-    trade(parts[1], 1, holders, step)
+                moving = [lax.ppermute(array, "cols", p) for array, p in ((moving[0], ups), (moving[-1], downs))]
+                holders = [below, above]
+            if step == 1:
+                moving = after_all(moving, [tables, *pieces[0][-2:]])
+            choice = tuple(0 if i >= step else 1 for i in range(size))
+            for array, owners in zip(moving, holders):
+                keep(stage_of(step, last, LOW), array, 0, row_count, LEAD, owners)
+            if 2 * step > last:
+                holders = [functools.reduce(either, holders)]
+            if step < last - 1:
+                way = choice if 2 * step > last else None
+                low_rows, high_rows = rows_of([moving], place, way, [], [[(0, *low)], [(0, *high)]])
+                trade(low_rows, -1, holders, step)
+                trade(high_rows, 1, holders, step)
+        parts = rows_of([moving], place, choice, [run(0)], [[(0, *low)], [(0, *high)], [(0, *middle)]])
+        arrived = [lax.ppermute(array, "cols", pairs) for array in parts]
+        trade(parts[0], -1, holders, last - 1)
+        trade(parts[1], 1, holders, last - 1)
+        return arrived, run(1)
+
+    def along_four():
+        swaps = [(0, 1), (1, 0), (2, 3), (3, 2)], [(1, 2), (2, 1)]
+        near = [lax.ppermute(block_values, "cols", p) for p in swaps]
+        owners = (1, 0, 3, 2), (-1, 2, 1, -1)
+        near = after_all(near, [tables, *pieces[0][-2:]])
+        for array, whose in zip(near, owners):
+            keep(stage_of(1, last, LOW), array, 0, row_count, LEAD, whose)
+        outer = lax.ppermute(near[1], "cols", [(1, 0), (2, 3)])
+        keep(stage_of(2, last, LOW), outer, 0, row_count, LEAD, (2, -1, -1, 1))
+        spans = low, high, middle
+        inner = rows_of([near[:1]], place, None, [], [[(0, *span)] for span in spans])
+        inner = [lax.ppermute(array, "cols", swaps[1]) for array in inner]
+        inner[:1] = after_all(inner[:1], lists[:1])
+        for array, (start, stop) in zip(inner, spans):
+            keep(stage_of(2, last, LOW), array, 0, stop - start, LEAD + start, (-1, 3, 0, -1))
+        arrived = [lax.ppermute(array, "cols", pairs) for array in inner]
+        low_rows, high_rows = rows_of([near], place, None, [], [[(0, *low)], [(0, *high)]])
+        trade(low_rows, -1, owners, 1)
+        trade(high_rows, 1, owners, 1)
+        low_rows, high_rows = rows_of(
+            [[outer, inner[0]], [outer, inner[1]]],
+            place,
+            (0, 1, 1, 0),
+            [run(0)],
+            [[(0, *low)], [(1, *high)]],
+            {(1, 1): high[0]},
+        )
+        trade(low_rows, -1, [(2, 3, 0, 1)], 2)
+        trade(high_rows, 1, [(2, 3, 0, 1)], 2)
+        return arrived, run(1)
+
+    arrived, token = along_four() if size == 4 else along_line()
     holders = [either(from_below(size, last), from_above(size, last))]
-    arrived[:1] = after_all(arrived[:1], [run(1)], EARLY)
+    arrived[:1] = after_all(arrived[:1], [token], EARLY)
     keep(stage_of(last, last, LOW), arrived[0], 0, LEAD, LEAD, holders[0])
     trade(arrived[0], -1, holders, last)
     arrived[1:2] = after_all(arrived[1:2], [run(2)])

time: 132 us -> 129 us (0.977)
  waiting for transfers between devices: 10.9 us -> 5.42 us
  starting transfers between devices: 32.4 us -> 34.7 us
    ppermute x15 -> x17, waiting for transfers between devices: 10.9 us -> 5.42 us  [the longest x3 5.38 us: along_four(): arrived = [lax.ppermute(array, 'cols', pairs) for array in inner]]
    ppermute x15 -> x17, starting transfers between devices: 32.4 us -> 34.7 us  [the longest x6 17.3 us: row_shift(): return lax.ppermute(array, 'rows', [(i, i + by) for i in steps])]
    pallas_call x3 -> x4, Pallas kernels: 4.34 us -> 5.07 us  [rows_of(): pl.pallas_call(kernel, out_shape=[jax.ShapeDtypeStruct((sum((folds[g] * (...]
  transfers between devices with their start and end apart: 15 -> 17, of which waited for: 4 -> 2; matrix products, arithmetic and copies ran while one was open for 1% -> 1% of each run, Pallas kernels for 41% -> 42%
where the time goes in v5:
time: 129 us
  Pallas kernels  58 us (45%)
  starting transfers between devices  34.7 us (27%)
  blocking collectives  27.9 us (22%)
  waiting for transfers between devices  5.42 us (4%)
  local copies, waits for them, and re-layouts  2.19 us (2%)
    pallas_call x6, Pallas kernels, run(): pl.pallas_call(functools.partial(stage_kernel, stage, tuple(plans[stage])...  31.9 us
    all_to_all x1, blocking collectives, body(): lax.all_to_all(spread, ('rows', 'cols'), 0, 0, tiled=True).reshape(-1)  27.9 us
    pallas_call x1, Pallas kernels, body(): pl.pallas_call(functools.partial(list_kernel, row_count, own, wanted_slot...  19.8 us
    ppermute x6, starting transfers between devices, row_shift(): return lax.ppermute(array, 'rows', [(i, i + by) for i in steps])  17.3 us
    ppermute x2, starting transfers between devices, along_four(): near = [lax.ppermute(block_values, 'cols', p) for p in swaps]  5.52 us
    ppermute x3, waiting for transfers between devices, along_four(): arrived = [lax.ppermute(array, 'cols', pairs) for array in inner]  5.38 us
    pallas_call x4, Pallas kernels, rows_of(): pl.pallas_call(kernel, out_shape=[jax.ShapeDtypeStruct((sum((folds[g] * (...  5.07 us
    ppermute x2, starting transfers between devices, row_shift(): lax.ppermute(array, ('rows', 'cols'), [(i * size + c, (i + by) * size + c...  4.64 us
  transfers between devices with their start and end apart: 17, of which 2 were waited for; matrix products, arithmetic and copies ran while one was open for 1% of the time, Pallas kernels for 42%

profile of v5, /device:TPU:1, one launch (start us, length us, event | category | flops | bytes accessed | tf_op | source)
XLA Modules:
  0.0 128.9 jit_solution(15111737212851617310)
XLA Ops:
  0.0 0.9 collective-permute-start.1
  0.9 4.6 %collective-permute-start = (bf16[24,2,128,128]{3,2,1,0:T(8,128)(2,1)}, bf16[24,2,128,128]{3,2,1,0:T(8,128)(2,1)S(1)}, u32[]{:S(2)}, u32[]{:S(2)}) collective-permute-start(bf16[24,2,128,128]{3,2,1,0:T(8,128)(2,1)} %refs_0_.3), channel_id=1, source_target_pairs={{0,1},{1,0},{2,3},{3,2},{4,5},{5,4},{6,7},{7,6},{8,9},{9,8},{10,11... | collective-permute-start | bytes 4718600 | tf_op jit(solution)/shard_map/ppermute | solution.py:534
  5.5 0.1 pad_add_fusion.place_ref
  5.6 1.4 %copy-done = bf16[24,2,128,128]{3,2,1,0:T(8,128)(2,1)S(1)} copy-done((bf16[24,2,128,128]{3,2,1,0:T(8,128)(2,1)S(1)}, bf16[24,2,128,128]{3,2,1,0:T(8,128)(2,1)}, u32[]{:S(2)}) %copy-start) | copy-done | bytes 1572888
  7.0 1.6 %rows_of.4 = (bf16[9,2,128,128]{3,2,1,0:T(8,128)(2,1)}, bf16[9,2,128,128]{3,2,1,0:T(8,128)(2,1)}) custom-call(s32[2]{0:T(128)S(1)} %pad_add_fusion.place_ref, bf16[24,2,128,128]{3,2,1,0:T(8,128)(2,1)S(1)} %copy-done), custom_call_target="tpu_custom_call" | custom-call | flops 1 | bytes 1 | tf_op jit(solution)/shard_map/rows_of/pallas_call | solution.py:399
  8.6 3.1 %collective-permute-start.2 = (bf16[9,2,128,128]{3,2,1,0:T(8,128)(2,1)}, bf16[9,2,128,128]{3,2,1,0:T(8,128)(2,1)}, u32[]{:S(2)}, u32[]{:S(2)}) collective-permute-start(bf16[9,2,128,128]{3,2,1,0:T(8,128)(2,1)} %get-tuple-element.35), channel_id=1, source_target_pairs={{4,0},{8,4},{12,8},{5,1},{9,5},{13,9},{6,2},{10,6},{14,10},{7,3},{... | collective-permute-start | bytes 1769480 | tf_op jit(solution)/shard_map/ppermute | solution.py:82
  11.7 3.0 %collective-permute-start.3 = (bf16[9,2,128,128]{3,2,1,0:T(8,128)(2,1)}, bf16[9,2,128,128]{3,2,1,0:T(8,128)(2,1)}, u32[]{:S(2)}, u32[]{:S(2)}) collective-permute-start(bf16[9,2,128,128]{3,2,1,0:T(8,128)(2,1)} %get-tuple-element.36), channel_id=1, source_target_pairs={{0,4},{4,8},{8,12},{1,5},{5,9},{9,13},{2,6},{6,10},{10,14},{3,7},{... | collective-permute-start | bytes 1769480 | tf_op jit(solution)/shard_map/ppermute | solution.py:82
  14.8 0.8 reshape.11
  15.5 27.9 %all_to_all.5 = s32[16,8,128]{2,1,0:T(8,128)S(1)} all-to-all(s32[16,8,128]{2,1,0:T(8,128)S(1)} %broadcast_in_dim.8), channel_id=1, replica_groups=mesh['groups'=2,'rows'=4,'cols'=4] {'rows','cols'}, dimensions={0} | all-to-all | bytes 131072 | tf_op jit(solution)/shard_map/all_to_all | solution.py:480
  43.5 0.0 collective-permute-done.2.refs_3_.refs_1_
  43.5 0.0 collective-permute-done.3.refs_4_.refs_2_
  43.5 0.0 collective-permute-done.1.refs_1_
  43.5 0.0 collective-permute-done.refs_0_
  43.5 1.3 %collective-permute-start.6 = (bf16[24,2,128,128]{3,2,1,0:T(8,128)(2,1)S(1)}, bf16[24,2,128,128]{3,2,1,0:T(8,128)(2,1)S(1)}, u32[]{:S(2)}, u32[]{:S(2)}) collective-permute-start(bf16[24,2,128,128]{3,2,1,0:T(8,128)(2,1)S(1)} %get-tuple-element.39.refs_4_.refs_1_), channel_id=1, source_target_pairs={{1,0},{2,3},{5,4},{6,7},{9,8},{10,11},{13,12},{14,15},{17,16},{18,... | collective-permute-start | bytes 4718600 | tf_op jit(solution)/shard_map/ppermute | solution.py:539
  44.8 1.0 rows_of.5
  45.8 1.0 rows_of.7
  46.8 0.7 collective-permute-start.4
  47.5 0.7 collective-permute-start.7
  48.2 2.3 %collective-permute-start.12 = (bf16[18,2,128,128]{3,2,1,0:T(8,128)(2,1)S(1)}, bf16[18,2,128,128]{3,2,1,0:T(8,128)(2,1)S(1)}, u32[]{:S(2)}, u32[]{:S(2)}) collective-permute-start(bf16[18,2,128,128]{3,2,1,0:T(8,128)(2,1)S(1)} %get-tuple-element.45), channel_id=1, source_target_pairs={{4,0},{8,4},{12,8},{5,1},{9,5},{13,9},{6,2},{10,6},{14,10},{7,3},{... | collective-permute-start | bytes 3538952 | tf_op jit(solution)/shard_map/ppermute | solution.py:82
  50.6 3.3 %collective-permute-start.13 = (bf16[18,2,128,128]{3,2,1,0:T(8,128)(2,1)S(1)}, bf16[18,2,128,128]{3,2,1,0:T(8,128)(2,1)S(1)}, u32[]{:S(2)}, u32[]{:S(2)}) collective-permute-start(bf16[18,2,128,128]{3,2,1,0:T(8,128)(2,1)S(1)} %get-tuple-element.46), channel_id=1, source_target_pairs={{0,4},{4,8},{8,12},{1,5},{5,9},{9,13},{2,6},{6,10},{10,14},{3,7},{... | collective-permute-start | bytes 3538952 | tf_op jit(solution)/shard_map/ppermute | solution.py:82
  53.8 0.0 copy-start.1
  53.8 19.8 %lists.1 = (s32[25]{0:T(128)S(1)}, s32[13312]{0:T(1024)S(1)}) custom-call(s32[2]{0:T(128)S(1)} %pad_add_fusion.place_ref, s32[4,24]{1,0:T(4,128)S(1)} %bitcast.10, s32[16384]{0:T(1024)S(1)} %bitcast.9), custom_call_target="tpu_custom_call" | custom-call | flops 8589934592 | bytes 8589934592 | tf_op jit(solution)/shard_map/lists/pallas_call | solution.py:481
  73.6 0.0 collective-permute-done.7.refs_0_
  73.6 1.3 %collective-permute-start.10 = (bf16[9,2,128,128]{3,2,1,0:T(8,128)(2,1)S(1)}, bf16[9,2,128,128]{3,2,1,0:T(8,128)(2,1)S(1)}, u32[]{:S(2)}, u32[]{:S(2)}) collective-permute-start(bf16[9,2,128,128]{3,2,1,0:T(8,128)(2,1)S(1)} %after_all.5.refs_1_), channel_id=1, source_target_pairs={{2,3},{1,0},{6,7},{5,4},{10,11},{9,8},{14,15},{13,12},{18,19},{17,... | collective-permute-start | bytes 1769480 | tf_op jit(solution)/shard_map/ppermute | solution.py:547
  74.9 0.0 collective-permute-done.4.refs_3_.refs_2_
  75.0 0.7 collective-permute-start.11
  75.7 7.8 %stage_0.1 = (bf16[680,128,128]{2,1,0:T(8,128)(2,1)S(1)}, f32[96,128,128]{2,1,0:T(8,128)S(1)}, s32[1]{0:T(128)}) custom-call(s32[25]{0:T(128)S(1)} %get-tuple-element.33.refs_1_.count_ref, s32[13312]{0:T(1024)S(1)} %get-tuple-element.34.terms_hbm, bf16[24,2,128,128]{3,2,1,0:T(8,128)(2,1)S(1)} %copy-done.1, ...), custom_call_target="tpu_custom_call" | custom-call | flops 1 | bytes 1 | tf_op jit(solution)/shard_map/stage_0/pallas_call | solution.py:447
  83.5 1.3 %collective-permute-start.5 = (bf16[9,2,128,128]{3,2,1,0:T(8,128)(2,1)S(1)}, bf16[9,2,128,128]{3,2,1,0:T(8,128)(2,1)S(1)}, u32[]{:S(2)}, u32[]{:S(2)}) collective-permute-start(bf16[9,2,128,128]{3,2,1,0:T(8,128)(2,1)S(1)} %collective-permute-done.4.refs_3_.refs_2_), channel_id=1, source_target_pairs={{2,3},{1,0},{6,7},{5,4},{10,11},{9,8},{14,15},{13,12},{18,19},{17,... | collective-permute-start | bytes 1769480 | tf_op jit(solution)/shard_map/ppermute | solution.py:547
  84.8 1.5 %rows_of.6 = (bf16[9,2,128,128]{3,2,1,0:T(8,128)(2,1)S(1)}, bf16[9,2,128,128]{3,2,1,0:T(8,128)(2,1)S(1)}) custom-call(s32[2]{0:T(128)S(1)} %pad_add_fusion.place_ref, bf16[24,2,128,128]{3,2,1,0:T(8,128)(2,1)S(1)} %collective-permute-done.6.refs_0_.refs_2_, bf16[9,2,128,128]{3,2,1,0:T(8,128)(2,1)S(1)} %after_all.5.refs_1_, ...), custom_call_target="tpu_custom_call" | custom-call | flops 1 | bytes 1 | tf_op jit(solution)/shard_map/rows_of/pallas_call | solution.py:399
  86.3 0.0 collective-permute-done.11.refs_3_
  86.3 1.9 %collective-permute-start.8 = (bf16[9,2,128,128]{3,2,1,0:T(8,128)(2,1)S(1)}, bf16[9,2,128,128]{3,2,1,0:T(8,128)(2,1)S(1)}, u32[]{:S(2)}, u32[]{:S(2)}) collective-permute-start(bf16[9,2,128,128]{3,2,1,0:T(8,128)(2,1)S(1)} %get-tuple-element.42), channel_id=1, source_target_pairs={{4,0},{8,4},{12,8},{5,1},{9,5},{13,9},{6,2},{10,6},{14,10},{7,3},{... | collective-permute-start | bytes 1769480 | tf_op jit(solution)/shard_map/ppermute | solution.py:82
  88.2 3.6 %collective-permute-start.9 = (bf16[9,2,128,128]{3,2,1,0:T(8,128)(2,1)S(1)}, bf16[9,2,128,128]{3,2,1,0:T(8,128)(2,1)S(1)}, u32[]{:S(2)}, u32[]{:S(2)}) collective-permute-start(bf16[9,2,128,128]{3,2,1,0:T(8,128)(2,1)S(1)} %get-tuple-element.43), channel_id=1, source_target_pairs={{0,4},{4,8},{8,12},{1,5},{5,9},{9,13},{2,6},{6,10},{10,14},{3,7},{... | collective-permute-start | bytes 1769480 | tf_op jit(solution)/shard_map/ppermute | solution.py:82
  91.9 0.0 collective-permute-done.13.refs_6_.refs_7_
  91.9 7.2 %stage_1.1 = (bf16[680,128,128]{2,1,0:T(8,128)(2,1)S(1)}, f32[96,128,128]{2,1,0:T(8,128)S(1)}, s32[1]{0:T(128)}) custom-call(s32[25]{0:T(128)S(1)} %get-tuple-element.33.refs_1_.count_ref, s32[13312]{0:T(1024)S(1)} %get-tuple-element.34.terms_hbm, ...), custom_call_target="tpu_custom_call", output_to_operand_aliasing={{0}: (10, {}), {1}: (11, {})} | custom-call | flops 1 | bytes 1 | tf_op jit(solution)/shard_map/stage_1/pallas_call | solution.py:447
  99.1 0.0 collective-permute-done.10.refs_0_
  99.1 0.6 after_all.6.refs_2_
  99.8 1.9 %collective-permute-start.16 = (bf16[9,2,128,128]{3,2,1,0:T(8,128)(2,1)S(1)}, bf16[9,2,128,128]{3,2,1,0:T(8,128)(2,1)S(1)}, u32[]{:S(2)}, u32[]{:S(2)}) collective-permute-start(bf16[9,2,128,128]{3,2,1,0:T(8,128)(2,1)S(1)} %after_all.6.refs_2_), channel_id=1, source_target_pairs={{4,0},{7,3},{8,4},{11,7},{12,8},{15,11},{20,16},{23,19},{24,20},{2... | collective-permute-start | bytes 1769480 | tf_op jit(solution)/shard_map/ppermute | solution.py:83
  101.7 1.3 %collective-permute-start.15 = (bf16[6,2,128,128]{3,2,1,0:T(8,128)(2,1)S(1)}, bf16[6,2,128,128]{3,2,1,0:T(8,128)(2,1)S(1)}, u32[]{:S(2)}, u32[]{:S(2)}) collective-permute-start(bf16[6,2,128,128]{3,2,1,0:T(8,128)(2,1)S(1)} %collective-permute-done.11.refs_3_), channel_id=1, source_target_pairs={{2,3},{1,0},{6,7},{5,4},{10,11},{9,8},{14,15},{13,12},{18,19},{17,... | collective-permute-start | bytes 1179656 | tf_op jit(solution)/shard_map/ppermute | solution.py:547
  103.0 0.0 collective-permute-done.8.refs_0_
  103.0 4.6 %stage_2.1 = (bf16[680,128,128]{2,1,0:T(8,128)(2,1)S(1)}, f32[96,128,128]{2,1,0:T(8,128)S(1)}, s32[1]{0:T(128)}) custom-call(s32[25]{0:T(128)S(1)} %get-tuple-element.33.refs_1_.count_ref, s32[13312]{0:T(1024)S(1)} %get-tuple-element.34.terms_hbm, ...), custom_call_target="tpu_custom_call", output_to_operand_aliasing={{0}: (5, {}), {1}: (6, {})} | custom-call | flops 1 | bytes 1 | tf_op jit(solution)/shard_map/stage_2/pallas_call | solution.py:447
  107.6 1.1 collective-permute-done.5.refs_0_
  108.6 0.6 after_all.7.refs_1_
  109.3 2.7 %collective-permute-start.14 = (bf16[9,2,128,128]{3,2,1,0:T(8,128)(2,1)S(1)}, bf16[9,2,128,128]{3,2,1,0:T(8,128)(2,1)S(1)}, u32[]{:S(2)}, u32[]{:S(2)}) collective-permute-start(bf16[9,2,128,128]{3,2,1,0:T(8,128)(2,1)S(1)} %after_all.7.refs_1_), channel_id=1, source_target_pairs={{0,4},{3,7},{4,8},{7,11},{8,12},{11,15},{16,20},{19,23},{20,24},{2... | collective-permute-start | bytes 1769480 | tf_op jit(solution)/shard_map/ppermute | solution.py:83
  112.0 0.0 collective-permute-done.16.refs_0_
  112.0 4.9 %stage_3.1 = (bf16[680,128,128]{2,1,0:T(8,128)(2,1)S(1)}, f32[96,128,128]{2,1,0:T(8,128)S(1)}, s32[1]{0:T(128)}) custom-call(s32[25]{0:T(128)S(1)} %get-tuple-element.33.refs_1_.count_ref, s32[13312]{0:T(1024)S(1)} %get-tuple-element.34.terms_hbm, ...), custom_call_target="tpu_custom_call", output_to_operand_aliasing={{0}: (4, {}), {1}: (5, {})} | custom-call | flops 1 | bytes 1 | tf_op jit(solution)/shard_map/stage_3/pallas_call | solution.py:447
  117.0 4.3 %collective-permute-done.15.refs_0_ = bf16[6,2,128,128]{3,2,1,0:T(8,128)(2,1)S(1)} collective-permute-done((bf16[6,2,128,128]{3,2,1,0:T(8,128)(2,1)S(1)}, bf16[6,2,128,128]{3,2,1,0:T(8,128)(2,1)S(1)}, u32[]{:S(2)}, u32[]{:S(2)}) %collective-permute-start.15) | collective-permute-done | bytes 393248 | tf_op jit(solution)/shard_map/ppermute | solution.py:547
  121.3 3.7 %stage_4.1 = (bf16[680,128,128]{2,1,0:T(8,128)(2,1)S(1)}, f32[96,128,128]{2,1,0:T(8,128)S(1)}, f32[96,128,128]{2,1,0:T(8,128)}) custom-call(s32[25]{0:T(128)S(1)} %get-tuple-element.33.refs_1_.count_ref, s32[13312]{0:T(1024)S(1)} %get-tuple-element.34.terms_hbm, ...), custom_call_target="tpu_custom_call", output_to_operand_aliasing={{0}: (3, {}), {1}: (4, {})} | custom-call | flops 4294967296 | bytes 4294967296 | tf_op jit(solution)/shard_map/stage_4/pallas_call | solution.py:447
  125.0 3.7 %stage_5.1 = (bf16[680,128,128]{2,1,0:T(8,128)(2,1)S(1)}, f32[96,128,128]{2,1,0:T(8,128)S(1)}, f32[96,128,128]{2,1,0:T(8,128)}) custom-call(s32[25]{0:T(128)S(1)} %get-tuple-element.33.refs_1_.count_ref, s32[13312]{0:T(1024)S(1)} %get-tuple-element.34.terms_hbm, ...), custom_call_target="tpu_custom_call", output_to_operand_aliasing={{0}: (3, {}), {1}: (4, {}), {2}: (5, {})} | custom-call | flops 1 | bytes 1 | tf_op jit(solution)/shard_map/stage_5/pallas_call | solution.py:447
  (12 shorter events, 0.0 us)
Async XLA Ops:
  0.0 53.8 %copy-start.2 = (s32[24,4]{0,1:T(4,128)S(1)}, s32[24,4]{0,1:T(4,128)}, u32[]{:S(2)}) copy-start(s32[24,4]{0,1:T(4,128)} %param.5) | copy-start | bytes 1156
  0.0 43.5 %collective-permute-start.1 = (bf16[24,2,128,128]{3,2,1,0:T(8,128)(2,1)}, bf16[24,2,128,128]{3,2,1,0:T(8,128)(2,1)S(1)}, u32[]{:S(2)}, u32[]{:S(2)}) collective-permute-start(bf16[24,2,128,128]{3,2,1,0:T(8,128)(2,1)} %refs_0_.3), channel_id=1, source_target_pairs={{1,2},{2,1},{5,6},{6,5},{9,10},{10,9},{13,14},{14,13},{17,18},{18,... | collective-permute-start | bytes 4718600 | tf_op jit(solution)/shard_map/ppermute | solution.py:534
  0.9 42.6 %collective-permute-start = (bf16[24,2,128,128]{3,2,1,0:T(8,128)(2,1)}, bf16[24,2,128,128]{3,2,1,0:T(8,128)(2,1)S(1)}, u32[]{:S(2)}, u32[]{:S(2)}) collective-permute-start(bf16[24,2,128,128]{3,2,1,0:T(8,128)(2,1)} %refs_0_.3), channel_id=1, source_target_pairs={{0,1},{1,0},{2,3},{3,2},{4,5},{5,4},{6,7},{7,6},{8,9},{9,8},{10,11... | collective-permute-start | bytes 4718600 | tf_op jit(solution)/shard_map/ppermute | solution.py:534
  5.6 1.4 %copy-start = (bf16[24,2,128,128]{3,2,1,0:T(8,128)(2,1)S(1)}, bf16[24,2,128,128]{3,2,1,0:T(8,128)(2,1)}, u32[]{:S(2)}) copy-start(bf16[24,2,128,128]{3,2,1,0:T(8,128)(2,1)} %refs_0_.3) | copy-start | bytes 4718596
  8.6 34.9 %collective-permute-start.2 = (bf16[9,2,128,128]{3,2,1,0:T(8,128)(2,1)}, bf16[9,2,128,128]{3,2,1,0:T(8,128)(2,1)}, u32[]{:S(2)}, u32[]{:S(2)}) collective-permute-start(bf16[9,2,128,128]{3,2,1,0:T(8,128)(2,1)} %get-tuple-element.35), channel_id=1, source_target_pairs={{4,0},{8,4},{12,8},{5,1},{9,5},{13,9},{6,2},{10,6},{14,10},{7,3},{... | collective-permute-start | bytes 1769480 | tf_op jit(solution)/shard_map/ppermute | solution.py:82
  11.7 31.8 %collective-permute-start.3 = (bf16[9,2,128,128]{3,2,1,0:T(8,128)(2,1)}, bf16[9,2,128,128]{3,2,1,0:T(8,128)(2,1)}, u32[]{:S(2)}, u32[]{:S(2)}) collective-permute-start(bf16[9,2,128,128]{3,2,1,0:T(8,128)(2,1)} %get-tuple-element.36), channel_id=1, source_target_pairs={{0,4},{4,8},{8,12},{1,5},{5,9},{9,13},{2,6},{6,10},{10,14},{3,7},{... | collective-permute-start | bytes 1769480 | tf_op jit(solution)/shard_map/ppermute | solution.py:82
  43.5 40.0 %collective-permute-start.6 = (bf16[24,2,128,128]{3,2,1,0:T(8,128)(2,1)S(1)}, bf16[24,2,128,128]{3,2,1,0:T(8,128)(2,1)S(1)}, u32[]{:S(2)}, u32[]{:S(2)}) collective-permute-start(bf16[24,2,128,128]{3,2,1,0:T(8,128)(2,1)S(1)} %get-tuple-element.39.refs_4_.refs_1_), channel_id=1, source_target_pairs={{1,0},{2,3},{5,4},{6,7},{9,8},{10,11},{13,12},{14,15},{17,16},{18,... | collective-permute-start | bytes 4718600 | tf_op jit(solution)/shard_map/ppermute | solution.py:539
  46.8 28.1 %collective-permute-start.4 = (bf16[9,2,128,128]{3,2,1,0:T(8,128)(2,1)S(1)}, bf16[9,2,128,128]{3,2,1,0:T(8,128)(2,1)S(1)}, u32[]{:S(2)}, u32[]{:S(2)}) collective-permute-start(bf16[9,2,128,128]{3,2,1,0:T(8,128)(2,1)S(1)} %get-tuple-element.38), channel_id=1, source_target_pairs={{1,2},{2,1},{5,6},{6,5},{9,10},{10,9},{13,14},{14,13},{17,18},{18,... | collective-permute-start | bytes 1769480 | tf_op jit(solution)/shard_map/ppermute | solution.py:543
  47.5 26.1 %collective-permute-start.7 = (bf16[9,2,128,128]{3,2,1,0:T(8,128)(2,1)S(1)}, bf16[9,2,128,128]{3,2,1,0:T(8,128)(2,1)S(1)}, u32[]{:S(2)}, u32[]{:S(2)}) collective-permute-start(bf16[9,2,128,128]{3,2,1,0:T(8,128)(2,1)S(1)} %get-tuple-element.40), channel_id=1, source_target_pairs={{1,2},{2,1},{5,6},{6,5},{9,10},{10,9},{13,14},{14,13},{17,18},{18,... | collective-permute-start | bytes 1769480 | tf_op jit(solution)/shard_map/ppermute | solution.py:543
  48.2 40.0 %collective-permute-start.12 = (bf16[18,2,128,128]{3,2,1,0:T(8,128)(2,1)S(1)}, bf16[18,2,128,128]{3,2,1,0:T(8,128)(2,1)S(1)}, u32[]{:S(2)}, u32[]{:S(2)}) collective-permute-start(bf16[18,2,128,128]{3,2,1,0:T(8,128)(2,1)S(1)} %get-tuple-element.45), channel_id=1, source_target_pairs={{4,0},{8,4},{12,8},{5,1},{9,5},{13,9},{6,2},{10,6},{14,10},{7,3},{... | collective-permute-start | bytes 3538952 | tf_op jit(solution)/shard_map/ppermute | solution.py:82
  50.6 41.3 %collective-permute-start.13 = (bf16[18,2,128,128]{3,2,1,0:T(8,128)(2,1)S(1)}, bf16[18,2,128,128]{3,2,1,0:T(8,128)(2,1)S(1)}, u32[]{:S(2)}, u32[]{:S(2)}) collective-permute-start(bf16[18,2,128,128]{3,2,1,0:T(8,128)(2,1)S(1)} %get-tuple-element.46), channel_id=1, source_target_pairs={{0,4},{4,8},{8,12},{1,5},{5,9},{9,13},{2,6},{6,10},{10,14},{3,7},{... | collective-permute-start | bytes 3538952 | tf_op jit(solution)/shard_map/ppermute | solution.py:82
  53.8 21.8 %copy-start.1 = (bf16[24,2,128,128]{3,2,1,0:T(8,128)(2,1)S(1)}, bf16[24,2,128,128]{3,2,1,0:T(8,128)(2,1)}, u32[]{:S(2)}) copy-start(bf16[24,2,128,128]{3,2,1,0:T(8,128)(2,1)} %refs_0_.3) | copy-start | bytes 4718596
  73.6 25.4 %collective-permute-start.10 = (bf16[9,2,128,128]{3,2,1,0:T(8,128)(2,1)S(1)}, bf16[9,2,128,128]{3,2,1,0:T(8,128)(2,1)S(1)}, u32[]{:S(2)}, u32[]{:S(2)}) collective-permute-start(bf16[9,2,128,128]{3,2,1,0:T(8,128)(2,1)S(1)} %after_all.5.refs_1_), channel_id=1, source_target_pairs={{2,3},{1,0},{6,7},{5,4},{10,11},{9,8},{14,15},{13,12},{18,19},{17,... | collective-permute-start | bytes 1769480 | tf_op jit(solution)/shard_map/ppermute | solution.py:547
  75.0 11.3 %collective-permute-start.11 = (bf16[6,2,128,128]{3,2,1,0:T(8,128)(2,1)S(1)}, bf16[6,2,128,128]{3,2,1,0:T(8,128)(2,1)S(1)}, u32[]{:S(2)}, u32[]{:S(2)}) collective-permute-start(bf16[6,2,128,128]{3,2,1,0:T(8,128)(2,1)S(1)} %get-tuple-element.44), channel_id=1, source_target_pairs={{1,2},{2,1},{5,6},{6,5},{9,10},{10,9},{13,14},{14,13},{17,18},{18,... | collective-permute-start | bytes 1179656 | tf_op jit(solution)/shard_map/ppermute | solution.py:543
  83.5 25.2 %collective-permute-start.5 = (bf16[9,2,128,128]{3,2,1,0:T(8,128)(2,1)S(1)}, bf16[9,2,128,128]{3,2,1,0:T(8,128)(2,1)S(1)}, u32[]{:S(2)}, u32[]{:S(2)}) collective-permute-start(bf16[9,2,128,128]{3,2,1,0:T(8,128)(2,1)S(1)} %collective-permute-done.4.refs_3_.refs_2_), channel_id=1, source_target_pairs={{2,3},{1,0},{6,7},{5,4},{10,11},{9,8},{14,15},{13,12},{18,19},{17,... | collective-permute-start | bytes 1769480 | tf_op jit(solution)/shard_map/ppermute | solution.py:547
  86.3 16.7 %collective-permute-start.8 = (bf16[9,2,128,128]{3,2,1,0:T(8,128)(2,1)S(1)}, bf16[9,2,128,128]{3,2,1,0:T(8,128)(2,1)S(1)}, u32[]{:S(2)}, u32[]{:S(2)}) collective-permute-start(bf16[9,2,128,128]{3,2,1,0:T(8,128)(2,1)S(1)} %get-tuple-element.42), channel_id=1, source_target_pairs={{4,0},{8,4},{12,8},{5,1},{9,5},{13,9},{6,2},{10,6},{14,10},{7,3},{... | collective-permute-start | bytes 1769480 | tf_op jit(solution)/shard_map/ppermute | solution.py:82
  88.2 14.8 %collective-permute-start.9 = (bf16[9,2,128,128]{3,2,1,0:T(8,128)(2,1)S(1)}, bf16[9,2,128,128]{3,2,1,0:T(8,128)(2,1)S(1)}, u32[]{:S(2)}, u32[]{:S(2)}) collective-permute-start(bf16[9,2,128,128]{3,2,1,0:T(8,128)(2,1)S(1)} %get-tuple-element.43), channel_id=1, source_target_pairs={{0,4},{4,8},{8,12},{1,5},{5,9},{9,13},{2,6},{6,10},{10,14},{3,7},{... | collective-permute-start | bytes 1769480 | tf_op jit(solution)/shard_map/ppermute | solution.py:82
  99.8 12.3 %collective-permute-start.16 = (bf16[9,2,128,128]{3,2,1,0:T(8,128)(2,1)S(1)}, bf16[9,2,128,128]{3,2,1,0:T(8,128)(2,1)S(1)}, u32[]{:S(2)}, u32[]{:S(2)}) collective-permute-start(bf16[9,2,128,128]{3,2,1,0:T(8,128)(2,1)S(1)} %after_all.6.refs_2_), channel_id=1, source_target_pairs={{4,0},{7,3},{8,4},{11,7},{12,8},{15,11},{20,16},{23,19},{24,20},{2... | collective-permute-start | bytes 1769480 | tf_op jit(solution)/shard_map/ppermute | solution.py:83
  101.7 19.6 %collective-permute-start.15 = (bf16[6,2,128,128]{3,2,1,0:T(8,128)(2,1)S(1)}, bf16[6,2,128,128]{3,2,1,0:T(8,128)(2,1)S(1)}, u32[]{:S(2)}, u32[]{:S(2)}) collective-permute-start(bf16[6,2,128,128]{3,2,1,0:T(8,128)(2,1)S(1)} %collective-permute-done.11.refs_3_), channel_id=1, source_target_pairs={{2,3},{1,0},{6,7},{5,4},{10,11},{9,8},{14,15},{13,12},{18,19},{17,... | collective-permute-start | bytes 1179656 | tf_op jit(solution)/shard_map/ppermute | solution.py:547
  109.3 15.7 %collective-permute-start.14 = (bf16[9,2,128,128]{3,2,1,0:T(8,128)(2,1)S(1)}, bf16[9,2,128,128]{3,2,1,0:T(8,128)(2,1)S(1)}, u32[]{:S(2)}, u32[]{:S(2)}) collective-permute-start(bf16[9,2,128,128]{3,2,1,0:T(8,128)(2,1)S(1)} %after_all.7.refs_1_), channel_id=1, source_target_pairs={{0,4},{3,7},{4,8},{7,11},{8,12},{11,15},{16,20},{19,23},{20,24},{2... | collective-permute-start | bytes 1769480 | tf_op jit(solution)/shard_map/ppermute | solution.py:83

commit v6 on v5

--- a/solution.py
+++ b/solution.py
@@ -11,7 +11,7 @@
 LEAD = W - 1
 SPAN = 2 * W - 1
 WIDE = 4 * W
-UNROLL = 16
+UNROLL = 32
 FEW = 8
 BITS = 10
 MASK = (1 << BITS) - 1
@@ -84,7 +84,7 @@
 
 
 def segment_size(part_rows, slot_count):
-    most = part_rows * (slot_count * (SPAN + 1) - slot_count * (slot_count - 1) // 2) + 4 * UNROLL
+    most = part_rows * (slot_count * (SPAN + 1) - slot_count * (slot_count - 1) // 2) + 4 * FEW
     return -(-most // 256) * 256
 
 
@@ -229,7 +229,7 @@
         for chunk in lanes:
             at = at_ref[chunk * lines + stage]
             tag = (chunk * part * slot_count) << (2 * BITS)
-            for extra in range(2 * UNROLL):
+            for extra in range(2 * FEW):
                 terms_ref[at + extra] = zero_term + tag
             used = at - (stage * CHUNKS + chunk) * segment
             count_ref[stage * CHUNKS + chunk] = (used + 2 * FEW - 1) // (2 * FEW)

time: 129 us -> 129 us (level); the launches traced: 129 us -> 127 us
  Pallas kernels: 58 us -> 56.7 us
where the time goes in v6:
time: 129 us; the launch traced here: 127 us
  Pallas kernels  56.7 us (44%)
  starting transfers between devices  34.5 us (27%)
  blocking collectives  27.9 us (22%)
  waiting for transfers between devices  5.41 us (4%)
  local copies, waits for them, and re-layouts  2.19 us (2%)
    pallas_call x6, Pallas kernels, run(): pl.pallas_call(functools.partial(stage_kernel, stage, tuple(plans[stage])...  30.8 us
    all_to_all x1, blocking collectives, body(): lax.all_to_all(spread, ('rows', 'cols'), 0, 0, tiled=True).reshape(-1)  27.9 us
    pallas_call x1, Pallas kernels, body(): pl.pallas_call(functools.partial(list_kernel, row_count, own, wanted_slot...  19.6 us
    ppermute x6, starting transfers between devices, row_shift(): return lax.ppermute(array, 'rows', [(i, i + by) for i in steps])  17.3 us
    ppermute x2, starting transfers between devices, along_four(): near = [lax.ppermute(block_values, 'cols', p) for p in swaps]  5.52 us
    ppermute x3, waiting for transfers between devices, along_four(): arrived = [lax.ppermute(array, 'cols', pairs) for array in inner]  5.37 us
    pallas_call x4, Pallas kernels, rows_of(): pl.pallas_call(kernel, out_shape=[jax.ShapeDtypeStruct((sum((folds[g] * (...  5.07 us
    ppermute x2, starting transfers between devices, row_shift(): lax.ppermute(array, ('rows', 'cols'), [(i * size + c, (i + by) * size + c...  4.44 us
  transfers between devices with their start and end apart: 17, of which 2 were waited for; matrix products, arithmetic and copies ran while one was open for 1% of the time, Pallas kernels for 42%

profile of v6, /device:TPU:1, one launch (start us, length us, event | category | flops | bytes accessed | tf_op | source)
XLA Modules:
  0.0 127.4 jit_solution(59392245650018570)
XLA Ops:
  0.0 0.9 collective-permute-start.1
  0.9 4.6 %collective-permute-start = (bf16[24,2,128,128]{3,2,1,0:T(8,128)(2,1)}, bf16[24,2,128,128]{3,2,1,0:T(8,128)(2,1)S(1)}, u32[]{:S(2)}, u32[]{:S(2)}) collective-permute-start(bf16[24,2,128,128]{3,2,1,0:T(8,128)(2,1)} %refs_0_.3), channel_id=1, source_target_pairs={{0,1},{1,0},{2,3},{3,2},{4,5},{5,4},{6,7},{7,6},{8,9},{9,8},{10,11... | collective-permute-start | bytes 4718600 | tf_op jit(solution)/shard_map/ppermute | solution.py:534
  5.5 0.1 pad_add_fusion.place_ref
  5.6 1.4 %copy-done = bf16[24,2,128,128]{3,2,1,0:T(8,128)(2,1)S(1)} copy-done((bf16[24,2,128,128]{3,2,1,0:T(8,128)(2,1)S(1)}, bf16[24,2,128,128]{3,2,1,0:T(8,128)(2,1)}, u32[]{:S(2)}) %copy-start) | copy-done | bytes 1572888
  7.0 1.6 %rows_of.4 = (bf16[9,2,128,128]{3,2,1,0:T(8,128)(2,1)}, bf16[9,2,128,128]{3,2,1,0:T(8,128)(2,1)}) custom-call(s32[2]{0:T(128)S(1)} %pad_add_fusion.place_ref, bf16[24,2,128,128]{3,2,1,0:T(8,128)(2,1)S(1)} %copy-done), custom_call_target="tpu_custom_call" | custom-call | flops 1 | bytes 1 | tf_op jit(solution)/shard_map/rows_of/pallas_call | solution.py:399
  8.6 3.1 %collective-permute-start.2 = (bf16[9,2,128,128]{3,2,1,0:T(8,128)(2,1)}, bf16[9,2,128,128]{3,2,1,0:T(8,128)(2,1)}, u32[]{:S(2)}, u32[]{:S(2)}) collective-permute-start(bf16[9,2,128,128]{3,2,1,0:T(8,128)(2,1)} %get-tuple-element.35), channel_id=1, source_target_pairs={{4,0},{8,4},{12,8},{5,1},{9,5},{13,9},{6,2},{10,6},{14,10},{7,3},{... | collective-permute-start | bytes 1769480 | tf_op jit(solution)/shard_map/ppermute | solution.py:82
  11.7 3.0 %collective-permute-start.3 = (bf16[9,2,128,128]{3,2,1,0:T(8,128)(2,1)}, bf16[9,2,128,128]{3,2,1,0:T(8,128)(2,1)}, u32[]{:S(2)}, u32[]{:S(2)}) collective-permute-start(bf16[9,2,128,128]{3,2,1,0:T(8,128)(2,1)} %get-tuple-element.36), channel_id=1, source_target_pairs={{0,4},{4,8},{8,12},{1,5},{5,9},{9,13},{2,6},{6,10},{10,14},{3,7},{... | collective-permute-start | bytes 1769480 | tf_op jit(solution)/shard_map/ppermute | solution.py:82
  14.8 0.8 reshape.11
  15.5 27.9 %all_to_all.5 = s32[16,8,128]{2,1,0:T(8,128)S(1)} all-to-all(s32[16,8,128]{2,1,0:T(8,128)S(1)} %broadcast_in_dim.8), channel_id=1, replica_groups=mesh['groups'=2,'rows'=4,'cols'=4] {'rows','cols'}, dimensions={0} | all-to-all | bytes 131072 | tf_op jit(solution)/shard_map/all_to_all | solution.py:480
  43.5 0.0 collective-permute-done.2.refs_3_.refs_1_
  43.5 0.0 collective-permute-done.3.refs_4_.refs_2_
  43.5 0.0 collective-permute-done.1.refs_1_
  43.5 0.0 collective-permute-done.refs_0_
  43.5 1.3 %collective-permute-start.6 = (bf16[24,2,128,128]{3,2,1,0:T(8,128)(2,1)S(1)}, bf16[24,2,128,128]{3,2,1,0:T(8,128)(2,1)S(1)}, u32[]{:S(2)}, u32[]{:S(2)}) collective-permute-start(bf16[24,2,128,128]{3,2,1,0:T(8,128)(2,1)S(1)} %get-tuple-element.39.refs_4_.refs_1_), channel_id=1, source_target_pairs={{1,0},{2,3},{5,4},{6,7},{9,8},{10,11},{13,12},{14,15},{17,16},{18,... | collective-permute-start | bytes 4718600 | tf_op jit(solution)/shard_map/ppermute | solution.py:539
  44.8 1.0 rows_of.5
  45.8 1.0 rows_of.7
  46.8 0.7 collective-permute-start.4
  47.5 0.7 collective-permute-start.7
  48.2 2.3 %collective-permute-start.12 = (bf16[18,2,128,128]{3,2,1,0:T(8,128)(2,1)S(1)}, bf16[18,2,128,128]{3,2,1,0:T(8,128)(2,1)S(1)}, u32[]{:S(2)}, u32[]{:S(2)}) collective-permute-start(bf16[18,2,128,128]{3,2,1,0:T(8,128)(2,1)S(1)} %get-tuple-element.45), channel_id=1, source_target_pairs={{4,0},{8,4},{12,8},{5,1},{9,5},{13,9},{6,2},{10,6},{14,10},{7,3},{... | collective-permute-start | bytes 3538952 | tf_op jit(solution)/shard_map/ppermute | solution.py:82
  50.6 3.3 %collective-permute-start.13 = (bf16[18,2,128,128]{3,2,1,0:T(8,128)(2,1)S(1)}, bf16[18,2,128,128]{3,2,1,0:T(8,128)(2,1)S(1)}, u32[]{:S(2)}, u32[]{:S(2)}) collective-permute-start(bf16[18,2,128,128]{3,2,1,0:T(8,128)(2,1)S(1)} %get-tuple-element.46), channel_id=1, source_target_pairs={{0,4},{4,8},{8,12},{1,5},{5,9},{9,13},{2,6},{6,10},{10,14},{3,7},{... | collective-permute-start | bytes 3538952 | tf_op jit(solution)/shard_map/ppermute | solution.py:82
  53.8 0.0 copy-start.1
  53.8 19.6 %lists.1 = (s32[25]{0:T(128)S(1)}, s32[13312]{0:T(1024)S(1)}) custom-call(s32[2]{0:T(128)S(1)} %pad_add_fusion.place_ref, s32[4,24]{1,0:T(4,128)S(1)} %bitcast.10, s32[16384]{0:T(1024)S(1)} %bitcast.9), custom_call_target="tpu_custom_call" | custom-call | flops 8589934592 | bytes 8589934592 | tf_op jit(solution)/shard_map/lists/pallas_call | solution.py:481
  73.4 1.3 %collective-permute-start.10 = (bf16[9,2,128,128]{3,2,1,0:T(8,128)(2,1)S(1)}, bf16[9,2,128,128]{3,2,1,0:T(8,128)(2,1)S(1)}, u32[]{:S(2)}, u32[]{:S(2)}) collective-permute-start(bf16[9,2,128,128]{3,2,1,0:T(8,128)(2,1)S(1)} %after_all.5.refs_1_), channel_id=1, source_target_pairs={{2,3},{1,0},{6,7},{5,4},{10,11},{9,8},{14,15},{13,12},{18,19},{17,... | collective-permute-start | bytes 1769480 | tf_op jit(solution)/shard_map/ppermute | solution.py:547
  74.7 0.0 collective-permute-done.4.refs_3_.refs_2_
  74.8 0.7 collective-permute-start.11
  75.5 7.3 %stage_0.1 = (bf16[680,128,128]{2,1,0:T(8,128)(2,1)S(1)}, f32[96,128,128]{2,1,0:T(8,128)S(1)}, s32[1]{0:T(128)}) custom-call(s32[25]{0:T(128)S(1)} %get-tuple-element.33.refs_1_.count_ref, s32[13312]{0:T(1024)S(1)} %get-tuple-element.34.terms_hbm, bf16[24,2,128,128]{3,2,1,0:T(8,128)(2,1)S(1)} %copy-done.1, ...), custom_call_target="tpu_custom_call" | custom-call | flops 1 | bytes 1 | tf_op jit(solution)/shard_map/stage_0/pallas_call | solution.py:447
  82.8 0.0 collective-permute-done.6.refs_0_.refs_2_
  82.8 1.3 %collective-permute-start.5 = (bf16[9,2,128,128]{3,2,1,0:T(8,128)(2,1)S(1)}, bf16[9,2,128,128]{3,2,1,0:T(8,128)(2,1)S(1)}, u32[]{:S(2)}, u32[]{:S(2)}) collective-permute-start(bf16[9,2,128,128]{3,2,1,0:T(8,128)(2,1)S(1)} %collective-permute-done.4.refs_3_.refs_2_), channel_id=1, source_target_pairs={{2,3},{1,0},{6,7},{5,4},{10,11},{9,8},{14,15},{13,12},{18,19},{17,... | collective-permute-start | bytes 1769480 | tf_op jit(solution)/shard_map/ppermute | solution.py:547
  84.1 1.5 %rows_of.6 = (bf16[9,2,128,128]{3,2,1,0:T(8,128)(2,1)S(1)}, bf16[9,2,128,128]{3,2,1,0:T(8,128)(2,1)S(1)}) custom-call(s32[2]{0:T(128)S(1)} %pad_add_fusion.place_ref, bf16[24,2,128,128]{3,2,1,0:T(8,128)(2,1)S(1)} %collective-permute-done.6.refs_0_.refs_2_, bf16[9,2,128,128]{3,2,1,0:T(8,128)(2,1)S(1)} %after_all.5.refs_1_, ...), custom_call_target="tpu_custom_call" | custom-call | flops 1 | bytes 1 | tf_op jit(solution)/shard_map/rows_of/pallas_call | solution.py:399
  85.6 0.0 collective-permute-done.11.refs_3_
  85.6 1.9 %collective-permute-start.8 = (bf16[9,2,128,128]{3,2,1,0:T(8,128)(2,1)S(1)}, bf16[9,2,128,128]{3,2,1,0:T(8,128)(2,1)S(1)}, u32[]{:S(2)}, u32[]{:S(2)}) collective-permute-start(bf16[9,2,128,128]{3,2,1,0:T(8,128)(2,1)S(1)} %get-tuple-element.42), channel_id=1, source_target_pairs={{4,0},{8,4},{12,8},{5,1},{9,5},{13,9},{6,2},{10,6},{14,10},{7,3},{... | collective-permute-start | bytes 1769480 | tf_op jit(solution)/shard_map/ppermute | solution.py:82
  87.6 3.6 %collective-permute-start.9 = (bf16[9,2,128,128]{3,2,1,0:T(8,128)(2,1)S(1)}, bf16[9,2,128,128]{3,2,1,0:T(8,128)(2,1)S(1)}, u32[]{:S(2)}, u32[]{:S(2)}) collective-permute-start(bf16[9,2,128,128]{3,2,1,0:T(8,128)(2,1)S(1)} %get-tuple-element.43), channel_id=1, source_target_pairs={{0,4},{4,8},{8,12},{1,5},{5,9},{9,13},{2,6},{6,10},{10,14},{3,7},{... | collective-permute-start | bytes 1769480 | tf_op jit(solution)/shard_map/ppermute | solution.py:82
  91.2 6.2 %stage_1.1 = (bf16[680,128,128]{2,1,0:T(8,128)(2,1)S(1)}, f32[96,128,128]{2,1,0:T(8,128)S(1)}, s32[1]{0:T(128)}) custom-call(s32[25]{0:T(128)S(1)} %get-tuple-element.33.refs_1_.count_ref, s32[13312]{0:T(1024)S(1)} %get-tuple-element.34.terms_hbm, ...), custom_call_target="tpu_custom_call", output_to_operand_aliasing={{0}: (10, {}), {1}: (11, {})} | custom-call | flops 1 | bytes 1 | tf_op jit(solution)/shard_map/stage_1/pallas_call | solution.py:447
  97.4 0.0 collective-permute-done.10.refs_0_
  97.4 0.6 after_all.6.refs_2_
  98.1 1.9 %collective-permute-start.16 = (bf16[9,2,128,128]{3,2,1,0:T(8,128)(2,1)S(1)}, bf16[9,2,128,128]{3,2,1,0:T(8,128)(2,1)S(1)}, u32[]{:S(2)}, u32[]{:S(2)}) collective-permute-start(bf16[9,2,128,128]{3,2,1,0:T(8,128)(2,1)S(1)} %after_all.6.refs_2_), channel_id=1, source_target_pairs={{4,0},{7,3},{8,4},{11,7},{12,8},{15,11},{20,16},{23,19},{24,20},{2... | collective-permute-start | bytes 1769480 | tf_op jit(solution)/shard_map/ppermute | solution.py:83
  100.0 1.3 %collective-permute-start.15 = (bf16[6,2,128,128]{3,2,1,0:T(8,128)(2,1)S(1)}, bf16[6,2,128,128]{3,2,1,0:T(8,128)(2,1)S(1)}, u32[]{:S(2)}, u32[]{:S(2)}) collective-permute-start(bf16[6,2,128,128]{3,2,1,0:T(8,128)(2,1)S(1)} %collective-permute-done.11.refs_3_), channel_id=1, source_target_pairs={{2,3},{1,0},{6,7},{5,4},{10,11},{9,8},{14,15},{13,12},{18,19},{17,... | collective-permute-start | bytes 1179656 | tf_op jit(solution)/shard_map/ppermute | solution.py:547
  101.3 0.0 collective-permute-done.8.refs_0_
  101.3 0.0 collective-permute-done.9.refs_1_
  101.3 4.6 %stage_2.1 = (bf16[680,128,128]{2,1,0:T(8,128)(2,1)S(1)}, f32[96,128,128]{2,1,0:T(8,128)S(1)}, s32[1]{0:T(128)}) custom-call(s32[25]{0:T(128)S(1)} %get-tuple-element.33.refs_1_.count_ref, s32[13312]{0:T(1024)S(1)} %get-tuple-element.34.terms_hbm, ...), custom_call_target="tpu_custom_call", output_to_operand_aliasing={{0}: (5, {}), {1}: (6, {})} | custom-call | flops 1 | bytes 1 | tf_op jit(solution)/shard_map/stage_2/pallas_call | solution.py:447
  105.9 1.3 %collective-permute-done.5.refs_0_ = bf16[9,2,128,128]{3,2,1,0:T(8,128)(2,1)S(1)} collective-permute-done((bf16[9,2,128,128]{3,2,1,0:T(8,128)(2,1)S(1)}, bf16[9,2,128,128]{3,2,1,0:T(8,128)(2,1)S(1)}, u32[]{:S(2)}, u32[]{:S(2)}) %collective-permute-start.5) | collective-permute-done | bytes 589856 | tf_op jit(solution)/shard_map/ppermute | solution.py:547
  107.2 0.6 after_all.7.refs_1_
  107.8 2.5 %collective-permute-start.14 = (bf16[9,2,128,128]{3,2,1,0:T(8,128)(2,1)S(1)}, bf16[9,2,128,128]{3,2,1,0:T(8,128)(2,1)S(1)}, u32[]{:S(2)}, u32[]{:S(2)}) collective-permute-start(bf16[9,2,128,128]{3,2,1,0:T(8,128)(2,1)S(1)} %after_all.7.refs_1_), channel_id=1, source_target_pairs={{0,4},{3,7},{4,8},{7,11},{8,12},{11,15},{16,20},{19,23},{20,24},{2... | collective-permute-start | bytes 1769480 | tf_op jit(solution)/shard_map/ppermute | solution.py:83
  110.4 5.0 %stage_3.1 = (bf16[680,128,128]{2,1,0:T(8,128)(2,1)S(1)}, f32[96,128,128]{2,1,0:T(8,128)S(1)}, s32[1]{0:T(128)}) custom-call(s32[25]{0:T(128)S(1)} %get-tuple-element.33.refs_1_.count_ref, s32[13312]{0:T(1024)S(1)} %get-tuple-element.34.terms_hbm, ...), custom_call_target="tpu_custom_call", output_to_operand_aliasing={{0}: (4, {}), {1}: (5, {})} | custom-call | flops 1 | bytes 1 | tf_op jit(solution)/shard_map/stage_3/pallas_call | solution.py:447
  115.4 4.1 %collective-permute-done.15.refs_0_ = bf16[6,2,128,128]{3,2,1,0:T(8,128)(2,1)S(1)} collective-permute-done((bf16[6,2,128,128]{3,2,1,0:T(8,128)(2,1)S(1)}, bf16[6,2,128,128]{3,2,1,0:T(8,128)(2,1)S(1)}, u32[]{:S(2)}, u32[]{:S(2)}) %collective-permute-start.15) | collective-permute-done | bytes 393248 | tf_op jit(solution)/shard_map/ppermute | solution.py:547
  119.5 3.8 %stage_4.1 = (bf16[680,128,128]{2,1,0:T(8,128)(2,1)S(1)}, f32[96,128,128]{2,1,0:T(8,128)S(1)}, f32[96,128,128]{2,1,0:T(8,128)}) custom-call(s32[25]{0:T(128)S(1)} %get-tuple-element.33.refs_1_.count_ref, s32[13312]{0:T(1024)S(1)} %get-tuple-element.34.terms_hbm, ...), custom_call_target="tpu_custom_call", output_to_operand_aliasing={{0}: (3, {}), {1}: (4, {})} | custom-call | flops 4294967296 | bytes 4294967296 | tf_op jit(solution)/shard_map/stage_4/pallas_call | solution.py:447
  123.3 0.0 collective-permute-done.14.refs_0_
  123.4 3.9 %stage_5.1 = (bf16[680,128,128]{2,1,0:T(8,128)(2,1)S(1)}, f32[96,128,128]{2,1,0:T(8,128)S(1)}, f32[96,128,128]{2,1,0:T(8,128)}) custom-call(s32[25]{0:T(128)S(1)} %get-tuple-element.33.refs_1_.count_ref, s32[13312]{0:T(1024)S(1)} %get-tuple-element.34.terms_hbm, ...), custom_call_target="tpu_custom_call", output_to_operand_aliasing={{0}: (3, {}), {1}: (4, {}), {2}: (5, {})} | custom-call | flops 1 | bytes 1 | tf_op jit(solution)/shard_map/stage_5/pallas_call | solution.py:447
  (12 shorter events, 0.0 us)
Async XLA Ops:
  0.0 53.8 %copy-start.2 = (s32[24,4]{0,1:T(4,128)S(1)}, s32[24,4]{0,1:T(4,128)}, u32[]{:S(2)}) copy-start(s32[24,4]{0,1:T(4,128)} %param.5) | copy-start | bytes 1156
  0.0 43.5 %collective-permute-start.1 = (bf16[24,2,128,128]{3,2,1,0:T(8,128)(2,1)}, bf16[24,2,128,128]{3,2,1,0:T(8,128)(2,1)S(1)}, u32[]{:S(2)}, u32[]{:S(2)}) collective-permute-start(bf16[24,2,128,128]{3,2,1,0:T(8,128)(2,1)} %refs_0_.3), channel_id=1, source_target_pairs={{1,2},{2,1},{5,6},{6,5},{9,10},{10,9},{13,14},{14,13},{17,18},{18,... | collective-permute-start | bytes 4718600 | tf_op jit(solution)/shard_map/ppermute | solution.py:534
  0.9 42.6 %collective-permute-start = (bf16[24,2,128,128]{3,2,1,0:T(8,128)(2,1)}, bf16[24,2,128,128]{3,2,1,0:T(8,128)(2,1)S(1)}, u32[]{:S(2)}, u32[]{:S(2)}) collective-permute-start(bf16[24,2,128,128]{3,2,1,0:T(8,128)(2,1)} %refs_0_.3), channel_id=1, source_target_pairs={{0,1},{1,0},{2,3},{3,2},{4,5},{5,4},{6,7},{7,6},{8,9},{9,8},{10,11... | collective-permute-start | bytes 4718600 | tf_op jit(solution)/shard_map/ppermute | solution.py:534
  5.6 1.4 %copy-start = (bf16[24,2,128,128]{3,2,1,0:T(8,128)(2,1)S(1)}, bf16[24,2,128,128]{3,2,1,0:T(8,128)(2,1)}, u32[]{:S(2)}) copy-start(bf16[24,2,128,128]{3,2,1,0:T(8,128)(2,1)} %refs_0_.3) | copy-start | bytes 4718596
  8.6 34.9 %collective-permute-start.2 = (bf16[9,2,128,128]{3,2,1,0:T(8,128)(2,1)}, bf16[9,2,128,128]{3,2,1,0:T(8,128)(2,1)}, u32[]{:S(2)}, u32[]{:S(2)}) collective-permute-start(bf16[9,2,128,128]{3,2,1,0:T(8,128)(2,1)} %get-tuple-element.35), channel_id=1, source_target_pairs={{4,0},{8,4},{12,8},{5,1},{9,5},{13,9},{6,2},{10,6},{14,10},{7,3},{... | collective-permute-start | bytes 1769480 | tf_op jit(solution)/shard_map/ppermute | solution.py:82
  11.7 31.8 %collective-permute-start.3 = (bf16[9,2,128,128]{3,2,1,0:T(8,128)(2,1)}, bf16[9,2,128,128]{3,2,1,0:T(8,128)(2,1)}, u32[]{:S(2)}, u32[]{:S(2)}) collective-permute-start(bf16[9,2,128,128]{3,2,1,0:T(8,128)(2,1)} %get-tuple-element.36), channel_id=1, source_target_pairs={{0,4},{4,8},{8,12},{1,5},{5,9},{9,13},{2,6},{6,10},{10,14},{3,7},{... | collective-permute-start | bytes 1769480 | tf_op jit(solution)/shard_map/ppermute | solution.py:82
  43.5 39.3 %collective-permute-start.6 = (bf16[24,2,128,128]{3,2,1,0:T(8,128)(2,1)S(1)}, bf16[24,2,128,128]{3,2,1,0:T(8,128)(2,1)S(1)}, u32[]{:S(2)}, u32[]{:S(2)}) collective-permute-start(bf16[24,2,128,128]{3,2,1,0:T(8,128)(2,1)S(1)} %get-tuple-element.39.refs_4_.refs_1_), channel_id=1, source_target_pairs={{1,0},{2,3},{5,4},{6,7},{9,8},{10,11},{13,12},{14,15},{17,16},{18,... | collective-permute-start | bytes 4718600 | tf_op jit(solution)/shard_map/ppermute | solution.py:539
  46.8 27.9 %collective-permute-start.4 = (bf16[9,2,128,128]{3,2,1,0:T(8,128)(2,1)S(1)}, bf16[9,2,128,128]{3,2,1,0:T(8,128)(2,1)S(1)}, u32[]{:S(2)}, u32[]{:S(2)}) collective-permute-start(bf16[9,2,128,128]{3,2,1,0:T(8,128)(2,1)S(1)} %get-tuple-element.38), channel_id=1, source_target_pairs={{1,2},{2,1},{5,6},{6,5},{9,10},{10,9},{13,14},{14,13},{17,18},{18,... | collective-permute-start | bytes 1769480 | tf_op jit(solution)/shard_map/ppermute | solution.py:543
  47.5 25.9 %collective-permute-start.7 = (bf16[9,2,128,128]{3,2,1,0:T(8,128)(2,1)S(1)}, bf16[9,2,128,128]{3,2,1,0:T(8,128)(2,1)S(1)}, u32[]{:S(2)}, u32[]{:S(2)}) collective-permute-start(bf16[9,2,128,128]{3,2,1,0:T(8,128)(2,1)S(1)} %get-tuple-element.40), channel_id=1, source_target_pairs={{1,2},{2,1},{5,6},{6,5},{9,10},{10,9},{13,14},{14,13},{17,18},{18,... | collective-permute-start | bytes 1769480 | tf_op jit(solution)/shard_map/ppermute | solution.py:543
  48.2 39.3 %collective-permute-start.12 = (bf16[18,2,128,128]{3,2,1,0:T(8,128)(2,1)S(1)}, bf16[18,2,128,128]{3,2,1,0:T(8,128)(2,1)S(1)}, u32[]{:S(2)}, u32[]{:S(2)}) collective-permute-start(bf16[18,2,128,128]{3,2,1,0:T(8,128)(2,1)S(1)} %get-tuple-element.45), channel_id=1, source_target_pairs={{4,0},{8,4},{12,8},{5,1},{9,5},{13,9},{6,2},{10,6},{14,10},{7,3},{... | collective-permute-start | bytes 3538952 | tf_op jit(solution)/shard_map/ppermute | solution.py:82
  50.6 40.7 %collective-permute-start.13 = (bf16[18,2,128,128]{3,2,1,0:T(8,128)(2,1)S(1)}, bf16[18,2,128,128]{3,2,1,0:T(8,128)(2,1)S(1)}, u32[]{:S(2)}, u32[]{:S(2)}) collective-permute-start(bf16[18,2,128,128]{3,2,1,0:T(8,128)(2,1)S(1)} %get-tuple-element.46), channel_id=1, source_target_pairs={{0,4},{4,8},{8,12},{1,5},{5,9},{9,13},{2,6},{6,10},{10,14},{3,7},{... | collective-permute-start | bytes 3538952 | tf_op jit(solution)/shard_map/ppermute | solution.py:82
  53.8 21.6 %copy-start.1 = (bf16[24,2,128,128]{3,2,1,0:T(8,128)(2,1)S(1)}, bf16[24,2,128,128]{3,2,1,0:T(8,128)(2,1)}, u32[]{:S(2)}) copy-start(bf16[24,2,128,128]{3,2,1,0:T(8,128)(2,1)} %refs_0_.3) | copy-start | bytes 4718596
  73.4 24.0 %collective-permute-start.10 = (bf16[9,2,128,128]{3,2,1,0:T(8,128)(2,1)S(1)}, bf16[9,2,128,128]{3,2,1,0:T(8,128)(2,1)S(1)}, u32[]{:S(2)}, u32[]{:S(2)}) collective-permute-start(bf16[9,2,128,128]{3,2,1,0:T(8,128)(2,1)S(1)} %after_all.5.refs_1_), channel_id=1, source_target_pairs={{2,3},{1,0},{6,7},{5,4},{10,11},{9,8},{14,15},{13,12},{18,19},{17,... | collective-permute-start | bytes 1769480 | tf_op jit(solution)/shard_map/ppermute | solution.py:547
  74.8 10.9 %collective-permute-start.11 = (bf16[6,2,128,128]{3,2,1,0:T(8,128)(2,1)S(1)}, bf16[6,2,128,128]{3,2,1,0:T(8,128)(2,1)S(1)}, u32[]{:S(2)}, u32[]{:S(2)}) collective-permute-start(bf16[6,2,128,128]{3,2,1,0:T(8,128)(2,1)S(1)} %get-tuple-element.44), channel_id=1, source_target_pairs={{1,2},{2,1},{5,6},{6,5},{9,10},{10,9},{13,14},{14,13},{17,18},{18,... | collective-permute-start | bytes 1179656 | tf_op jit(solution)/shard_map/ppermute | solution.py:543
  82.8 24.4 %collective-permute-start.5 = (bf16[9,2,128,128]{3,2,1,0:T(8,128)(2,1)S(1)}, bf16[9,2,128,128]{3,2,1,0:T(8,128)(2,1)S(1)}, u32[]{:S(2)}, u32[]{:S(2)}) collective-permute-start(bf16[9,2,128,128]{3,2,1,0:T(8,128)(2,1)S(1)} %collective-permute-done.4.refs_3_.refs_2_), channel_id=1, source_target_pairs={{2,3},{1,0},{6,7},{5,4},{10,11},{9,8},{14,15},{13,12},{18,19},{17,... | collective-permute-start | bytes 1769480 | tf_op jit(solution)/shard_map/ppermute | solution.py:547
  85.6 15.7 %collective-permute-start.8 = (bf16[9,2,128,128]{3,2,1,0:T(8,128)(2,1)S(1)}, bf16[9,2,128,128]{3,2,1,0:T(8,128)(2,1)S(1)}, u32[]{:S(2)}, u32[]{:S(2)}) collective-permute-start(bf16[9,2,128,128]{3,2,1,0:T(8,128)(2,1)S(1)} %get-tuple-element.42), channel_id=1, source_target_pairs={{4,0},{8,4},{12,8},{5,1},{9,5},{13,9},{6,2},{10,6},{14,10},{7,3},{... | collective-permute-start | bytes 1769480 | tf_op jit(solution)/shard_map/ppermute | solution.py:82
  87.6 13.7 %collective-permute-start.9 = (bf16[9,2,128,128]{3,2,1,0:T(8,128)(2,1)S(1)}, bf16[9,2,128,128]{3,2,1,0:T(8,128)(2,1)S(1)}, u32[]{:S(2)}, u32[]{:S(2)}) collective-permute-start(bf16[9,2,128,128]{3,2,1,0:T(8,128)(2,1)S(1)} %get-tuple-element.43), channel_id=1, source_target_pairs={{0,4},{4,8},{8,12},{1,5},{5,9},{9,13},{2,6},{6,10},{10,14},{3,7},{... | collective-permute-start | bytes 1769480 | tf_op jit(solution)/shard_map/ppermute | solution.py:82
  98.1 12.3 %collective-permute-start.16 = (bf16[9,2,128,128]{3,2,1,0:T(8,128)(2,1)S(1)}, bf16[9,2,128,128]{3,2,1,0:T(8,128)(2,1)S(1)}, u32[]{:S(2)}, u32[]{:S(2)}) collective-permute-start(bf16[9,2,128,128]{3,2,1,0:T(8,128)(2,1)S(1)} %after_all.6.refs_2_), channel_id=1, source_target_pairs={{4,0},{7,3},{8,4},{11,7},{12,8},{15,11},{20,16},{23,19},{24,20},{2... | collective-permute-start | bytes 1769480 | tf_op jit(solution)/shard_map/ppermute | solution.py:83
  100.0 19.5 %collective-permute-start.15 = (bf16[6,2,128,128]{3,2,1,0:T(8,128)(2,1)S(1)}, bf16[6,2,128,128]{3,2,1,0:T(8,128)(2,1)S(1)}, u32[]{:S(2)}, u32[]{:S(2)}) collective-permute-start(bf16[6,2,128,128]{3,2,1,0:T(8,128)(2,1)S(1)} %collective-permute-done.11.refs_3_), channel_id=1, source_target_pairs={{2,3},{1,0},{6,7},{5,4},{10,11},{9,8},{14,15},{13,12},{18,19},{17,... | collective-permute-start | bytes 1179656 | tf_op jit(solution)/shard_map/ppermute | solution.py:547
  107.8 15.5 %collective-permute-start.14 = (bf16[9,2,128,128]{3,2,1,0:T(8,128)(2,1)S(1)}, bf16[9,2,128,128]{3,2,1,0:T(8,128)(2,1)S(1)}, u32[]{:S(2)}, u32[]{:S(2)}) collective-permute-start(bf16[9,2,128,128]{3,2,1,0:T(8,128)(2,1)S(1)} %after_all.7.refs_1_), channel_id=1, source_target_pairs={{0,4},{3,7},{4,8},{7,11},{8,12},{11,15},{16,20},{19,23},{20,24},{2... | collective-permute-start | bytes 1769480 | tf_op jit(solution)/shard_map/ppermute | solution.py:83
